TPU v7x, 32 devices: a whole 2x2x4 slice. The times are simulated.
32 devices in a mesh: img: 8 (over z, y), blk: 4 (over x, core).
Axes of the slice: x: 2, y: 2, z: 4, core: 2. Of those that a mesh axis runs over, the one named last changes fastest.
Arguments:
- x_small: bfloat16 [32, 196, 768], P('img', 'blk'), may hold values from -6 to 6
- x_large: bfloat16 [48, 576, 768], P('img', 'blk'), may hold values from -6 to 6
- live_counts: int32 [8, 2], P('img'), may hold values from 1 to 6, as said below
- ln1_gain: float32 [768], replicated, may hold values from 0.1 to 1.9
- ln1_bias: float32 [768], replicated, may hold values from -1.5 to 1.5
- tok_w1_small: bfloat16 [196, 384], P('blk'), may hold values from -0.4375 to 0.4375
- tok_b1_small: float32 [384], replicated, may hold values from -2.5 to 2.5
- tok_w2_small: bfloat16 [384, 196], P(None, 'blk'), may hold values from -0.3125 to 0.3125
- tok_b2_small: float32 [196], P('blk'), may hold values from -2.5 to 2.5
- tok_w1_large: bfloat16 [576, 384], P('blk'), may hold values from -0.25 to 0.25
- tok_b1_large: float32 [384], replicated, may hold values from -2.5 to 2.5
- tok_w2_large: bfloat16 [384, 576], P(None, 'blk'), may hold values from -0.3125 to 0.3125
- tok_b2_large: float32 [576], P('blk'), may hold values from -2.5 to 2.5
- ln2_gain: float32 [768], replicated, may hold values from 0.1 to 1.9
- ln2_bias: float32 [768], replicated, may hold values from -1.5 to 1.5
- ch_w1: bfloat16 [768, 3072], replicated, may hold values from -0.21875 to 0.21875
- ch_b1: float32 [3072], replicated, may hold values from -2.5 to 2.5
- ch_w2: bfloat16 [3072, 768], replicated, may hold values from -0.109375 to 0.109375
- ch_b2: float32 [768], replicated, may hold values from -2.5 to 2.5
- cot_small: bfloat16 [32, 196, 768], P('img', 'blk'), may hold values from -6 to 6
- cot_large: bfloat16 [48, 576, 768], P('img', 'blk'), may hold values from -6 to 6
Outputs:
- out_small: bfloat16 [32, 196, 768], P('img', 'blk')
- out_large: bfloat16 [48, 576, 768], P('img', 'blk')
- grad_x_small: float32 [32, 196, 768], P('img', 'blk')
- grad_x_large: float32 [48, 576, 768], P('img', 'blk')
- grad_ln1_gain: float32 [768], replicated
- grad_ln1_bias: float32 [768], replicated
- grad_tok_w1_small: float32 [196, 384], P('blk')
- grad_tok_b1_small: float32 [384], replicated
- grad_tok_w2_small: float32 [384, 196], P(None, 'blk')
- grad_tok_b2_small: float32 [196], P('blk')
- grad_tok_w1_large: float32 [576, 384], P('blk')
- grad_tok_b1_large: float32 [384], replicated
- grad_tok_w2_large: float32 [384, 576], P(None, 'blk')
- grad_tok_b2_large: float32 [576], P('blk')
- grad_ln2_gain: float32 [768], replicated
- grad_ln2_bias: float32 [768], replicated
- grad_ch_w1: float32 [768, 3072], replicated
- grad_ch_b1: float32 [3072], replicated
- grad_ch_w2: float32 [3072, 768], replicated
- grad_ch_b2: float32 [768], replicated
Inputs may be any that keep to these rules, and one draw needn't show every extreme that they name: `live_counts`: row i gives how many of the 4 224 px slots and of the 6 384 px slots of img index i hold live images; live slots come first, the others are empty. In every draw some index has all slots of both groups live and another has one of each.
All inputs are finite; a program needn't handle non-finite values.
Results may differ from a plain program's by a relative error of at most 0.007.
Values may be sent and summed in bfloat16 or wider, within the bound.
A program may use at most 192 MiB of HBM per device.

v0:
```python
import jax
import jax.numpy as jnp
from jax import lax
from jax.sharding import PartitionSpec as P

EPSILON = 1e-06


def norm_rows(values, scales, shifts):
    row_mean = jnp.mean(values, axis=-1, keepdims=True)
    centered = values - row_mean
    row_var = jnp.mean(centered * centered, axis=-1, keepdims=True)
    return centered * lax.rsqrt(row_var + EPSILON) * scales + shifts


def gelu_back(preact, upstream):
    unused, pullback = jax.vjp(jax.nn.gelu, preact)
    return pullback(upstream)[0]


def local(
    x_small,
    x_large,
    live_counts,
    ln1_gain,
    ln1_bias,
    tok_w1_small,
    tok_b1_small,
    tok_w2_small,
    tok_b2_small,
    tok_w1_large,
    tok_b1_large,
    tok_w2_large,
    tok_b2_large,
    ln2_gain,
    ln2_bias,
    ch_w1,
    ch_b1,
    ch_w2,
    ch_b2,
    cot_small,
    cot_large,
):
    model_width = x_small.shape[2]
    mask_small = (jnp.arange(x_small.shape[0]) < live_counts[0, 0]).astype(jnp.float32)
    mask_large = (jnp.arange(x_large.shape[0]) < live_counts[0, 1]).astype(jnp.float32)
    input_small = x_small.astype(jnp.float32)
    input_large = x_large.astype(jnp.float32)
    normed_small, back_small = jax.vjp(norm_rows, input_small, ln1_gain, ln1_bias)
    normed_large, back_large = jax.vjp(norm_rows, input_large, ln1_gain, ln1_bias)
    low_small = normed_small.astype(jnp.bfloat16)
    low_large = normed_large.astype(jnp.bfloat16)
    part_small = jnp.einsum(
        "nsd,sj->ndj", low_small, tok_w1_small, preferred_element_type=jnp.float32
    )
    part_large = jnp.einsum(
        "nsd,sj->ndj", low_large, tok_w1_large, preferred_element_type=jnp.float32
    )
    sum_small, sum_large = (
        lax.psum_scatter(part_small, "blk", scatter_dimension=1, tiled=True),
        lax.psum_scatter(part_large, "blk", scatter_dimension=1, tiled=True),
    )
    preact_small = sum_small + tok_b1_small
    preact_large = sum_large + tok_b1_large
    hidden_small, hidden_large = (
        lax.all_gather(jax.nn.gelu(preact_small).astype(jnp.bfloat16), "blk", axis=1, tiled=True),
        lax.all_gather(jax.nn.gelu(preact_large).astype(jnp.bfloat16), "blk", axis=1, tiled=True),
    )
    mid_small = (
        input_small
        + jnp.einsum("ndj,js->nsd", hidden_small, tok_w2_small, preferred_element_type=jnp.float32)
        + tok_b2_small[:, None]
    )
    mid_large = (
        input_large
        + jnp.einsum("ndj,js->nsd", hidden_large, tok_w2_large, preferred_element_type=jnp.float32)
        + tok_b2_large[:, None]
    )
    split_at = x_small.shape[0] * x_small.shape[1]
    rows_mid = jnp.concatenate(
        [mid_small.reshape(-1, model_width), mid_large.reshape(-1, model_width)], axis=0
    )
    row_mask = jnp.concatenate(
        [jnp.repeat(mask_small, x_small.shape[1]), jnp.repeat(mask_large, x_large.shape[1])]
    )
    normed_two, back_two = jax.vjp(norm_rows, rows_mid, ln2_gain, ln2_bias)
    normed_two_low = normed_two.astype(jnp.bfloat16)
    activation = jnp.dot(normed_two_low, ch_w1, preferred_element_type=jnp.float32) + ch_b1
    hidden_two = jax.nn.gelu(activation).astype(jnp.bfloat16)
    result = (
        rows_mid + jnp.dot(hidden_two, ch_w2, preferred_element_type=jnp.float32) + ch_b2
    ) * row_mask[:, None]
    out_small = result[:split_at].reshape(x_small.shape).astype(jnp.bfloat16)
    out_large = result[split_at:].reshape(x_large.shape).astype(jnp.bfloat16)
    cotangent = (
        jnp.concatenate(
            [
                cot_small.astype(jnp.float32).reshape(-1, model_width),
                cot_large.astype(jnp.float32).reshape(-1, model_width),
            ],
            axis=0,
        )
        * row_mask[:, None]
    )
    cot_low = cotangent.astype(jnp.bfloat16)
    grad_chan_w2 = jnp.einsum("rk,rd->kd", hidden_two, cot_low, preferred_element_type=jnp.float32)
    grad_chan_b2 = jnp.sum(cot_low.astype(jnp.float32), axis=0)
    grad_hidden_two = jnp.einsum("rd,kd->rk", cot_low, ch_w2, preferred_element_type=jnp.float32)
    grad_act_low = gelu_back(activation, grad_hidden_two).astype(jnp.bfloat16)
    grad_chan_w1 = jnp.einsum(
        "rd,rk->dk", normed_two_low, grad_act_low, preferred_element_type=jnp.float32
    )
    grad_chan_b1 = jnp.sum(grad_act_low.astype(jnp.float32), axis=0)
    grad_normed_two = jnp.einsum(
        "rk,dk->rd", grad_act_low, ch_w1, preferred_element_type=jnp.float32
    )
    grad_rows_norm, grad_gain_two, grad_shift_two = back_two(grad_normed_two)
    grad_mid = cotangent + grad_rows_norm
    grad_mid_small = grad_mid[:split_at].reshape(x_small.shape)
    grad_mid_large = grad_mid[split_at:].reshape(x_large.shape)
    mixed_low_small = grad_mid_small.astype(jnp.bfloat16)
    mixed_low_large = grad_mid_large.astype(jnp.bfloat16)
    grad_b2_small = jnp.sum(mixed_low_small.astype(jnp.float32), axis=(0, 2))
    grad_b2_large = jnp.sum(mixed_low_large.astype(jnp.float32), axis=(0, 2))
    grad_w2_small = jnp.einsum(
        "ndj,nsd->js", hidden_small, mixed_low_small, preferred_element_type=jnp.float32
    )
    grad_w2_large = jnp.einsum(
        "ndj,nsd->js", hidden_large, mixed_low_large, preferred_element_type=jnp.float32
    )
    upper_small = jnp.einsum(
        "nsd,js->ndj", mixed_low_small, tok_w2_small, preferred_element_type=jnp.float32
    )
    upper_large = jnp.einsum(
        "nsd,js->ndj", mixed_low_large, tok_w2_large, preferred_element_type=jnp.float32
    )
    summed_small, summed_large = (
        lax.psum_scatter(upper_small, "blk", scatter_dimension=1, tiled=True),
        lax.psum_scatter(upper_large, "blk", scatter_dimension=1, tiled=True),
    )
    pre_low_small = gelu_back(preact_small, summed_small).astype(jnp.bfloat16)
    pre_low_large = gelu_back(preact_large, summed_large).astype(jnp.bfloat16)
    grad_b1_small = jnp.sum(pre_low_small.astype(jnp.float32), axis=(0, 1))
    grad_b1_large = jnp.sum(pre_low_large.astype(jnp.float32), axis=(0, 1))
    whole_pre_small, whole_pre_large = (
        lax.all_gather(pre_low_small, "blk", axis=1, tiled=True),
        lax.all_gather(pre_low_large, "blk", axis=1, tiled=True),
    )
    grad_w1_small = jnp.einsum(
        "nsd,ndj->sj", low_small, whole_pre_small, preferred_element_type=jnp.float32
    )
    grad_w1_large = jnp.einsum(
        "nsd,ndj->sj", low_large, whole_pre_large, preferred_element_type=jnp.float32
    )
    grad_normed_small = jnp.einsum(
        "ndj,sj->nsd", whole_pre_small, tok_w1_small, preferred_element_type=jnp.float32
    )
    grad_normed_large = jnp.einsum(
        "ndj,sj->nsd", whole_pre_large, tok_w1_large, preferred_element_type=jnp.float32
    )
    input_grad_small, gain_part_small, shift_part_small = back_small(grad_normed_small)
    input_grad_large, gain_part_large, shift_part_large = back_large(grad_normed_large)
    grad_x_small = grad_mid_small + input_grad_small
    grad_x_large = grad_mid_large + input_grad_large
    grad_gain_one = gain_part_small + gain_part_large
    grad_shift_one = shift_part_small + shift_part_large
    (
        total_w1_small,
        total_w2_small,
        total_b2_small,
        total_w1_large,
        total_w2_large,
        total_b2_large,
    ) = lax.psum(
        (grad_w1_small, grad_w2_small, grad_b2_small, grad_w1_large, grad_w2_large, grad_b2_large),
        "img",
    )
    (
        total_gain_one,
        total_shift_one,
        total_b1_small,
        total_b1_large,
        total_gain_two,
        total_shift_two,
        total_chan_w1,
        total_chan_b1,
        total_chan_w2,
        total_chan_b2,
    ) = lax.psum(
        (
            grad_gain_one,
            grad_shift_one,
            grad_b1_small,
            grad_b1_large,
            grad_gain_two,
            grad_shift_two,
            grad_chan_w1,
            grad_chan_b1,
            grad_chan_w2,
            grad_chan_b2,
        ),
        ("img", "blk"),
    )
    return (
        out_small,
        out_large,
        grad_x_small,
        grad_x_large,
        total_gain_one,
        total_shift_one,
        total_w1_small,
        total_b1_small,
        total_w2_small,
        total_b2_small,
        total_w1_large,
        total_b1_large,
        total_w2_large,
        total_b2_large,
        total_gain_two,
        total_shift_two,
        total_chan_w1,
        total_chan_b1,
        total_chan_w2,
        total_chan_b2,
    )


def solution(mesh):
    in_specs = (
        P("img", "blk", None),
        P("img", "blk", None),
        P("img", None),
        P(),
        P(),
        P("blk", None),
        P(),
        P(None, "blk"),
        P("blk"),
        P("blk", None),
        P(),
        P(None, "blk"),
        P("blk"),
        P(),
        P(),
        P(),
        P(),
        P(),
        P(),
        P("img", "blk", None),
        P("img", "blk", None),
    )
    out_specs = (
        P("img", "blk", None),
        P("img", "blk", None),
        P("img", "blk", None),
        P("img", "blk", None),
        P(),
        P(),
        P("blk", None),
        P(),
        P(None, "blk"),
        P("blk"),
        P("blk", None),
        P(),
        P(None, "blk"),
        P("blk"),
        P(),
        P(),
        P(),
        P(),
        P(),
        P(),
    )
    return jax.shard_map(local, mesh=mesh, in_specs=in_specs, out_specs=out_specs, check_vma=False)
```

profile of v0, /device:TPU:0, one launch (start us, length us, event | category | flops | bytes accessed | tf_op | source)
XLA Modules:
  0.0 849.4 jit_solution(15147690231007265798)
XLA Ops:
  9.6 4.2 fusion.62
  16.0 4.8 fusion.52
  20.9 43.6 %reduce-scatter.5.cloned.1.call-done = f32[4,192,384]{2,1,0:T(8,128)} async-done(((f32[4,768,384]{2,1,0:T(8,128)}), f32[4,192,384]{2,1,0:T(8,128)}) %reduce-scatter.5.cloned.1.call-update) | async-done | bytes 1179664 | tf_op jit(solution)/shard_map/reduce_scatter | solution.py:60
  67.0 64.4 %reduce-scatter.7.cloned.1.call-done = f32[6,192,384]{2,1,0:T(8,128)} async-done(((f32[6,768,384]{2,1,0:T(8,128)}), f32[6,192,384]{2,1,0:T(8,128)}) %reduce-scatter.7.cloned.1.call-update) | async-done | bytes 1769488 | tf_op jit(solution)/shard_map/reduce_scatter | solution.py:61
  137.6 20.1 %all-gather.5.cloned.1.call-done = bf16[4,768,384]{2,1,0:T(8,128)(2,1)} async-done(((bf16[4,192,384]{2,1,0:T(8,128)(2,1)}), bf16[4,768,384]{2,1,0:T(8,128)(2,1)}) %all-gather.5.cloned.1.call-update) | async-done | bytes 2359312 | tf_op jit(solution)/shard_map/all_gather | solution.py:66
  160.5 30.0 %all-gather.7.cloned.1.call-done = bf16[6,768,384]{2,1,0:T(8,128)(2,1)} async-done(((bf16[6,192,384]{2,1,0:T(8,128)(2,1)}), bf16[6,768,384]{2,1,0:T(8,128)(2,1)}) %all-gather.7.cloned.1.call-update) | async-done | bytes 3538960 | tf_op jit(solution)/shard_map/all_gather | solution.py:67
  195.1 12.6 %convolution_add_fusion = f32[1060,3072]{1,0:T(8,128)} fusion(bf16[768,3072]{1,0:T(8,128)(2,1)} %param.36, f32[3072]{0:T(1024)S(1)} %copy-done.37, f32[768]{0:T(1024)S(1)} %copy-done.38, f32[768]{0:T(1024)S(1)} %copy-done.29, f32[1060]{0:T(1024)S(1)} %fusion.75, f32[1060]{0:T(1024)S(1)} %broadcast_multiply_fusion, f32[864,768]{1,0:T(8,128)S(1)} %bitcast.84, ...), kind=kOutput, calls=%fused_computation.2 | convolution fusion | flops 5009848320 | bytes 21027104 | tf_op jit(solution)/shard_map/dot_general | solution.py:88
  207.8 18.1 %convert_reduce_fusion = (f32[3072]{0:T(1024)}, bf16[1060,3072]{1,0:T(8,128)(2,1)}) fusion(f32[1060,3072]{1,0:T(8,128)} %convolution_add_fusion, bf16[3072,768]{1,0:T(8,128)(2,1)S(1)} %bitcast.101, f32[1060]{0:T(1024)S(1)} %copy-done.17, bf16[864,768]{1,0:T(8,128)(2,1)S(1)} %bitcast.94, bf16[196,768]{1,0:T(8,128)(2,1)S(1)} %reshape.177), kind=kOutput, calls=%fused_computation.10 | convolution fusion | flops 5078227968 | bytes 25901200 | tf_op jit(solution)/shard_map/rd,kd->rk/dot_general | solution.py:108
  225.8 9.4 %multiply_reduce_fusion = (f32[768]{0:T(1024)}, f32[1060]{0:T(1024)S(1)}, f32[768]{0:T(1024)}, f32[1060,768]{1,0:T(8,128)S(1)}) fusion(f32[1060]{0:T(1024)S(1)} %fusion.75, f32[1060]{0:T(1024)S(1)} %broadcast_multiply_fusion, f32[864,768]{1,0:T(8,128)S(1)} %bitcast.85, f32[196,768]{1,0:T(8,128)S(1)} %reshape.173, f32[768]{0:T(1024)S(1)} %copy-done.29, ...), kind=kOutput, calls=%fused_computation.27 | convolution fusion | flops 5009031168 | bytes 17765808 | tf_op jit(solution)/shard_map/rk,dk->rd/dot_general | solution.py:114
  236.6 15.1 %convert_reduce_fusion.2 = (f32[768]{0:T(1024)}, f32[1060,768]{1,0:T(8,128)S(1)}) fusion(f32[1060]{0:T(1024)S(1)} %copy-done.17, bf16[864,768]{1,0:T(8,128)(2,1)S(1)} %bitcast.95, bf16[196,768]{1,0:T(8,128)(2,1)S(1)} %reshape.177, f32[1060,768]{1,0:T(8,128)S(1)} %get-tuple-element.108, f32[1060]{0:T(1024)S(1)} %negate_multiply_fusion.1), kind=kLoop, calls=%fused_computation.26 | loop fusion | flops 8140032 | bytes 8152352 | tf_op jit(solution)/shard_map/reduce_sum | solution.py:107
  263.5 5.0 fusion.55
  268.6 38.4 %reduce-scatter.9.cloned.1.call-done = f32[4,192,384]{2,1,0:T(8,128)} async-done(((f32[4,768,384]{2,1,0:T(8,128)}), f32[4,192,384]{2,1,0:T(8,128)}) %reduce-scatter.9.cloned.1.call-update) | async-done | bytes 1179664 | tf_op jit(solution)/shard_map/reduce_scatter | solution.py:138
  310.4 63.3 %reduce-scatter.11.cloned.1.call-done = f32[6,192,384]{2,1,0:T(8,128)} async-done(((f32[6,768,384]{2,1,0:T(8,128)}), f32[6,192,384]{2,1,0:T(8,128)}) %reduce-scatter.11.cloned.1.call-update) | async-done | bytes 1769488 | tf_op jit(solution)/shard_map/reduce_scatter | solution.py:139
  373.8 4.2 convert_reduce_fusion.4
  378.1 12.5 %fusion.81 = f32[768,3072]{1,0:T(8,128)} fusion(bf16[1060,3072]{1,0:T(8,128)(2,1)} %get-tuple-element.123, f32[768]{0:T(1024)S(1)} %copy-done.39, f32[768]{0:T(1024)S(1)} %copy-done.30, f32[1060]{0:T(1024)S(1)} %copy-done.20, f32[1060]{0:T(1024)S(1)} %broadcast_multiply_fusion, f32[864,768]{1,0:T(8,128)} %bitcast.87, f32[196,768]{1,0:T(8,128)S(1)} %reshape.173), kind=kOutput, calls=%fused_computation.132 | convolution fusion | flops 5006592000 | bytes 19220768 | tf_op jit(solution)/shard_map/rd,rk->dk/dot_general | solution.py:110
  390.6 14.2 %fusion.78 = f32[3072,768]{1,0:T(8,128)} fusion(f32[1060]{0:T(1024)S(1)} %copy-done.18, bf16[864,768]{1,0:T(8,128)(2,1)S(1)} %bitcast.96, bf16[196,768]{1,0:T(8,128)(2,1)S(1)} %reshape.177, f32[1060,3072]{1,0:T(8,128)} %convolution_add_fusion), kind=kOutput, calls=%fused_computation.131 | convolution fusion | flops 5035898880 | bytes 24094864 | tf_op jit(solution)/shard_map/rk,rd->kd/dot_general | solution.py:106
  405.5 13.7 %fusion.13 = bf16[1060,768]{1,0:T(8,128)(2,1)S(1)} fusion(bf16[3072,768]{1,0:T(8,128)(2,1)} %param.38, f32[1060]{0:T(1024)S(1)} %copy-done.18, f32[768]{0:T(1024)S(1)} %copy-done.40, f32[864,768]{1,0:T(8,128)} %bitcast.88, f32[196,768]{1,0:T(8,128)S(1)} %reshape.173, f32[1060,3072]{1,0:T(8,128)} %convolution_add_fusion), kind=kOutput, calls=%fused_computation.24 | convolution fusion | flops 5035084800 | bytes 22635664 | tf_op jit(solution)/shard_map/dot_general | solution.py:91
  421.8 21.9 %all-reduce.2 = (f32[49]{0:T(128)}, f32[144]{0:T(256)}) all-reduce(f32[49]{0:T(128)S(1)} %reduce_sum.297, f32[144]{0:T(256)S(1)} %reduce_sum.301), channel_id=1, replica_groups=mesh['img'=8,'blk'=4] {'img'}, use_global_device_ids=true, to_apply=%region_28.0 | all-reduce | flops 193 | bytes 1544 | tf_op jit(solution)/shard_map/psum | solution.py:174
  456.8 4.9 fusion.21
  468.4 39.4 %all-reduce = (f32[768]{0:T(1024)}, f32[768]{0:T(1024)}, f32[384]{0:T(512)}, f32[384]{0:T(512)}, f32[768]{0:T(1024)}, /*index=5*/f32[768]{0:T(1024)}, f32[3072]{0:T(1024)}, f32[768]{0:T(1024)}) all-reduce(f32[768]{0:T(1024)S(1)} %add.238, f32[768]{0:T(1024)S(1)} %add.239, ...), channel_id=1, replica_groups=mesh['img'=8,'blk'=4] {'img','blk'}, use_global_device_ids=true, to_apply=%region_18.0 | all-reduce | flops 7680 | bytes 61440 | tf_op jit(solution)/shard_map/psum | solution.py:189
  507.8 4.3 add_add_fusion.3
  512.1 232.6 %all-reduce.7.cloned.1.call-done = (f32[768,3072]{1,0:T(8,128)}, f32[3072,768]{1,0:T(8,128)}) async-done(((f32[768,3072]{1,0:T(8,128)}, f32[3072,768]{1,0:T(8,128)}), (f32[768,3072]{1,0:T(8,128)}, f32[3072,768]{1,0:T(8,128)})) %all-reduce.7.cloned.1.call-update) | async-done | bytes 18874384 | tf_op jit(solution)/shard_map/psum | solution.py:189
  744.7 78.7 %all-reduce.9.cloned.1.call-done = (f32[49,384]{1,0:T(8,128)}, f32[384,49]{0,1:T(8,128)}, f32[144,384]{1,0:T(8,128)}, f32[384,144]{0,1:T(8,128)}) async-done(((f32[49,384]{1,0:T(8,128)}, f32[384,49]{0,1:T(8,128)}, f32[144,384]{1,0:T(8,128)}, f32[384,144]{0,1:T(8,128)}), (f32[49,384]{1,0:T(8,128)}, f32[384,49]{0,1:T(8,128)}, f32[144,384]{1,0:T(8,128)}, f32[384,144]{0,1:T(8,128)})) %all-reduce.9.cloned.1.call-update) | async-done | bytes 592912 | tf_op jit(solution)/shard_map/psum | solution.py:174
  829.8 8.8 %copy.73 = f32[768,3072]{1,0:T(8,128)} copy(f32[768,3072]{1,0:T(8,128)} %get-tuple-element.140) | data formatting | bytes 18874368
  (186 shorter events, 70.4 us)
Async XLA Ops:
  7.2 57.3 %reduce-scatter.5.cloned.1.call-start = ((), (), s32[]{:S(2)}) async-start(), calls=%async_computation.4 | async-start | bytes 5898240 | tf_op jit(solution)/shard_map/reduce_scatter | solution.py:60
  13.8 117.7 %reduce-scatter.7.cloned.1.call-start = ((), (), s32[]{:S(2)}) async-start(), calls=%async_computation.6 | async-start | bytes 8847360 | tf_op jit(solution)/shard_map/reduce_scatter | solution.py:61
  20.8 43.7 %copy-start.27 = (f32[384]{0:T(512)S(1)}, f32[384]{0:T(512)}, u32[]{:S(2)}) copy-start(f32[384]{0:T(512)} %param.27) | copy-start | bytes 4612
  20.8 110.7 %copy-start.25 = (f32[384]{0:T(512)S(1)}, f32[384]{0:T(512)}, u32[]{:S(2)}) copy-start(f32[384]{0:T(512)} %param.31) | copy-start | bytes 4612
  20.8 113.7 %copy-start.34 = (s32[1,2]{1,0:T(1,128)S(1)}, s32[1,2]{1,0:T(1,128)}, u32[]{:S(2)}) copy-start(s32[1,2]{1,0:T(1,128)} %param.23) | copy-start | bytes 28
  20.8 115.9 %copy-start.13 = (bf16[4,49,768]{2,0,1:T(4,128)(2,1)S(1)}, bf16[4,49,768]{2,0,1:T(4,128)(2,1)}, u32[]{:S(2)}) copy-start(bf16[4,49,768]{2,0,1:T(4,128)(2,1)} %param.40) | copy-start | bytes 903172
  20.8 136.9 %all-gather.5.cloned.1.call-start = ((), (), s32[]{:S(2)}) async-start(), calls=%async_computation.5 | async-start | bytes 2949120 | tf_op jit(solution)/shard_map/all_gather | solution.py:66
  67.0 90.7 %copy-start.5 = (bf16[4,49,768]{2,0,1:T(4,128)(2,1)S(1)}, bf16[4,49,768]{2,0,1:T(4,128)(2,1)}, u32[]{:S(2)}) copy-start(bf16[4,49,768]{2,0,1:T(4,128)(2,1)} %param.21) | copy-start | bytes 903172
  67.0 90.7 %copy-start.14 = (bf16[384,49]{0,1:T(8,128)(2,1)S(1)}, bf16[384,49]{0,1:T(8,128)(2,1)}, u32[]{:S(2)}) copy-start(bf16[384,49]{0,1:T(8,128)(2,1)} %param.28) | copy-start | bytes 112900
  67.0 90.7 %copy-start.36 = (f32[49]{0:T(128)S(1)}, f32[49]{0:T(128)}, u32[]{:S(2)}) copy-start(f32[49]{0:T(128)} %param.29) | copy-start | bytes 592
  67.0 123.5 %all-gather.7.cloned.1.call-start = ((), (), s32[]{:S(2)}) async-start(), calls=%async_computation.7 | async-start | bytes 4423680 | tf_op jit(solution)/shard_map/all_gather | solution.py:67
  134.5 172.5 %reduce-scatter.9.cloned.1.call-start = ((), (), s32[]{:S(2)}) async-start(), calls=%async_computation.8 | async-start | bytes 5898240 | tf_op jit(solution)/shard_map/reduce_scatter | solution.py:138
  136.8 53.7 %copy-start.11 = (bf16[384,144]{0,1:T(8,128)(2,1)S(1)}, bf16[384,144]{0,1:T(8,128)(2,1)}, u32[]{:S(2)}) copy-start(bf16[384,144]{0,1:T(8,128)(2,1)} %param.32) | copy-start | bytes 331780
  136.8 53.7 %copy-start.35 = (f32[144]{0:T(256)S(1)}, f32[144]{0:T(256)}, u32[]{:S(2)}) copy-start(f32[144]{0:T(256)} %param.33) | copy-start | bytes 1732
  193.8 41.5 %copy-start.2 = (f32[6,144,768]{2,1,0:T(8,128)}, f32[6,144,768]{2,1,0:T(8,128)S(1)}, u32[]{:S(2)}) copy-start(f32[6,144,768]{2,1,0:T(8,128)S(1)} %fusion.22) | copy-start | bytes 7962628
  259.0 114.8 %reduce-scatter.11.cloned.1.call-start = ((), (), s32[]{:S(2)}) async-start(), calls=%async_computation.10 | async-start | bytes 8847360 | tf_op jit(solution)/shard_map/reduce_scatter | solution.py:139
  268.6 105.2 %copy-start.26 = (f32[384]{0:T(512)S(1)}, f32[384]{0:T(512)}, u32[]{:S(2)}) copy-start(f32[384]{0:T(512)} %param.31) | copy-start | bytes 4612
  268.6 182.3 %all-gather.9.cloned.1.call-start = ((), (), s32[]{:S(2)}) async-start(), calls=%async_computation.9 | async-start | bytes 2949120 | tf_op jit(solution)/shard_map/all_gather | solution.py:146
  310.3 67.8 %copy-start.20 = (f32[1060]{0:T(1024)S(1)}, f32[1060]{0:T(1024)}, u32[]{:S(2)}) copy-start(f32[1060]{0:T(1024)} %copy-done.19) | copy-start | bytes 12724
  310.3 67.7 %copy-start.30 = (f32[768]{0:T(1024)S(1)}, f32[768]{0:T(1024)}, u32[]{:S(2)}) copy-start(f32[768]{0:T(1024)} %param.34) | copy-start | bytes 9220
  310.3 67.7 %copy-start.39 = (f32[768]{0:T(1024)S(1)}, f32[768]{0:T(1024)}, u32[]{:S(2)}) copy-start(f32[768]{0:T(1024)} %param.35) | copy-start | bytes 9220
  310.4 146.4 %all-gather.11.cloned.1.call-start = ((), (), s32[]{:S(2)}) async-start(), calls=%async_computation.11 | async-start | bytes 4423680 | tf_op jit(solution)/shard_map/all_gather | solution.py:147
  378.0 366.6 %all-reduce.7.cloned.1.call-start = ((), (), s32[]{:S(2)}) async-start(), calls=%async_computation.12 | async-start | bytes 37748736 | tf_op jit(solution)/shard_map/psum | solution.py:189
  404.9 418.5 %all-reduce.9.cloned.1.call-start = ((), (), s32[]{:S(2)}) async-start(), calls=%async_computation.13 | async-start | bytes 1228800 | tf_op jit(solution)/shard_map/psum | solution.py:174
  (34 other events, 282.6 us)
Sparse Core Ops, SparseCore 0:
  13.9 50.5 reduce-scatter.4
  67.7 63.6 reduce-scatter.6
  133.6 24.0 all-gather.4
  159.7 30.7 all-gather.6
  259.1 47.8 reduce-scatter.8
  310.1 63.6 reduce-scatter.10
  375.9 24.0 all-gather.8
  401.6 30.7 all-gather.10
  439.4 305.2 all-reduce.6
  749.5 73.8 all-reduce.8
where the time goes:
time: 850 us; the launch traced here: 849 us
  waiting for transfers between devices  571 us (67%)
  matrix products  121 us (14%)
  blocking collectives  61.2 us (7%)
  other arithmetic  50.2 us (6%)
  local copies, waits for them, and re-layouts  30.2 us (4%)
  between operations  15 us (2%)
    psum x1, waiting for transfers between devices, local(): lax.psum((grad_gain_one, grad_shift_one, grad_b1_small, grad_b1_large, gr...  233 us
    psum x1, waiting for transfers between devices, local(): lax.psum((grad_w1_small, grad_w2_small, grad_b2_small, grad_w1_large, gra...  78.7 us
    reduce_scatter x1, waiting for transfers between devices, local(): lax.psum_scatter(part_large, 'blk', scatter_dimension=1, tiled=True)  64.4 us
    reduce_scatter x1, waiting for transfers between devices, local(): lax.psum_scatter(upper_large, 'blk', scatter_dimension=1, tiled=True)  63.3 us
    reduce_scatter x1, waiting for transfers between devices, local(): lax.psum_scatter(part_small, 'blk', scatter_dimension=1, tiled=True)  43.6 us
    psum x1, blocking collectives, local(): lax.psum((grad_gain_one, grad_shift_one, grad_b1_small, grad_b1_large, gr...  39.4 us
    reduce_scatter x1, waiting for transfers between devices, local(): lax.psum_scatter(upper_small, 'blk', scatter_dimension=1, tiled=True)  38.4 us
    all_gather x1, waiting for transfers between devices, local(): lax.all_gather(jax.nn.gelu(preact_large).astype(jnp.bfloat16), 'blk', axi...  30 us
  transfers between devices with their start and end apart: 10, of which 8 were waited for; matrix products, arithmetic and copies ran while one was open for 12% of the time, Pallas kernels for 0%

commit v1 on v0

v1 whole, which is shorter than its diff:
```python
import jax
import jax.numpy as jnp
from jax import lax
from jax.sharding import PartitionSpec as P

EPSILON = 1e-06
LANES = 128
BF = jnp.bfloat16
F32 = jnp.float32


def norm_rows(values, scales, shifts):
    row_mean = jnp.mean(values, axis=-1, keepdims=True)
    centered = values - row_mean
    row_var = jnp.mean(centered * centered, axis=-1, keepdims=True)
    return centered * lax.rsqrt(row_var + EPSILON) * scales + shifts


def gelu_back(preact, upstream):
    unused, pullback = jax.vjp(jax.nn.gelu, preact)
    return pullback(upstream)[0]


def to_columns(rows):
    count, patches, width = rows.shape
    blocks = rows.reshape(count, patches, width // LANES, LANES).transpose(0, 2, 1, 3)
    blocks = blocks.reshape(count * (width // LANES), patches, LANES)
    size = lax.axis_size("blk")
    moved = lax.all_to_all(blocks, "blk", 0, 0, tiled=True)
    share = moved.shape[0] // size
    moved = moved.reshape(size, share, patches, LANES).transpose(0, 2, 1, 3)
    return moved.reshape(size * patches, share * LANES)


def to_rows(columns, shape):
    count, patches, width = shape
    size = lax.axis_size("blk")
    share = columns.shape[1] // LANES
    blocks = columns.reshape(size, patches, share, LANES).transpose(0, 2, 1, 3)
    blocks = blocks.reshape(size * share, patches, LANES)
    moved = lax.all_to_all(blocks, "blk", 0, 0, tiled=True)
    moved = moved.reshape(count, width // LANES, patches, LANES).transpose(0, 2, 1, 3)
    return moved.reshape(shape)


def mm(spec, left, right):
    return jnp.einsum(spec, left, right, preferred_element_type=F32)


def sum_low(values, axes):
    return lax.psum(values.astype(BF), axes).astype(F32)


def local(
    x_small, x_large, live_counts, ln1_gain, ln1_bias,
    tok_w1_small, tok_b1_small, tok_w2_small, tok_b2_small,
    tok_w1_large, tok_b1_large, tok_w2_large, tok_b2_large,
    ln2_gain, ln2_bias, ch_w1, ch_b1, ch_w2, ch_b2, cot_small, cot_large,
):
    width = x_small.shape[2]
    mask_small = (jnp.arange(x_small.shape[0]) < live_counts[0, 0]).astype(F32)
    mask_large = (jnp.arange(x_large.shape[0]) < live_counts[0, 1]).astype(F32)
    groups = []
    for x, w1, b1, w2, b2 in (
        (x_small, tok_w1_small, tok_b1_small, tok_w2_small, tok_b2_small),
        (x_large, tok_w1_large, tok_b1_large, tok_w2_large, tok_b2_large),
    ):
        wide = x.astype(F32)
        normed, back = jax.vjp(norm_rows, wide, ln1_gain, ln1_bias)
        w1_all = lax.all_gather(w1, "blk", axis=0, tiled=True)
        w2_all = lax.all_gather(w2, "blk", axis=1, tiled=True)
        u_cols = to_columns(normed.astype(BF))
        preact = mm("sj,sd->jd", w1_all, u_cols) + b1[:, None]
        hidden = jax.nn.gelu(preact).astype(BF)
        mixed = to_rows(mm("js,jd->sd", w2_all, hidden).astype(BF), x.shape)
        mid = wide + mixed.astype(F32) + b2[:, None]
        groups.append((x, mid, back, w1_all, w2_all, u_cols, preact, hidden))
    rows_mid = jnp.concatenate([g[1].reshape(-1, width) for g in groups], axis=0)
    row_mask = jnp.concatenate(
        [jnp.repeat(mask_small, x_small.shape[1]), jnp.repeat(mask_large, x_large.shape[1])]
    )
    split_at = x_small.shape[0] * x_small.shape[1]
    normed_two, back_two = jax.vjp(norm_rows, rows_mid, ln2_gain, ln2_bias)
    v = normed_two.astype(BF)
    activation = mm("rd,dk->rk", v, ch_w1) + ch_b1
    g = jax.nn.gelu(activation).astype(BF)
    result = (rows_mid + mm("rk,kd->rd", g, ch_w2) + ch_b2) * row_mask[:, None]
    out_small = result[:split_at].reshape(x_small.shape).astype(BF)
    out_large = result[split_at:].reshape(x_large.shape).astype(BF)
    e = (
        jnp.concatenate([cot_small.reshape(-1, width), cot_large.reshape(-1, width)]).astype(F32)
        * row_mask[:, None]
    )
    ec = e.astype(BF)
    grad_ch_w2 = mm("rk,rd->kd", g, ec)
    grad_ch_b2 = jnp.sum(ec.astype(F32), axis=0)
    ea = gelu_back(activation, mm("rd,kd->rk", ec, ch_w2)).astype(BF)
    grad_ch_w1 = mm("rd,rk->dk", v, ea)
    grad_ch_b1 = jnp.sum(ea.astype(F32), axis=0)
    rows_norm, grad_gain2, grad_bias2 = back_two(mm("rk,dk->rd", ea, ch_w1))
    ey = e + rows_norm
    grads = []
    gain1 = 0.0
    bias1 = 0.0
    for (x, mid, back, w1_all, w2_all, u_cols, preact, hidden), part in zip(
        groups, (ey[:split_at], ey[split_at:])
    ):
        part = part.reshape(x.shape)
        et = part.astype(BF)
        grad_b2 = jnp.sum(et.astype(F32), axis=(0, 2))
        et_cols = to_columns(et)
        grad_w2 = mm("jd,sd->js", hidden, et_cols)
        ep = gelu_back(preact, mm("js,sd->jd", w2_all, et_cols)).astype(BF)
        grad_b1 = jnp.sum(ep.astype(F32), axis=1)
        grad_w1 = mm("sd,jd->sj", u_cols, ep)
        eu = to_rows(mm("sj,jd->sd", w1_all, ep).astype(BF), x.shape)
        norm_grad, gain_part, bias_part = back(eu.astype(F32))
        gain1 = gain1 + gain_part
        bias1 = bias1 + bias_part
        grads.append((part + norm_grad, grad_w1, grad_b1, grad_w2, grad_b2))
    scattered = [
        (
            lax.psum_scatter(grad_w1, "blk", scatter_dimension=0, tiled=True),
            lax.psum_scatter(grad_w2, "blk", scatter_dimension=1, tiled=True),
        )
        for _, grad_w1, _, grad_w2, _ in grads
    ]
    (w1_s, w2_s), (w1_l, w2_l) = lax.psum(scattered, "img")
    b2_s, b2_l = lax.psum((grads[0][4], grads[1][4]), "img")
    both = ("img", "blk")
    grad_ch_w1 = sum_low(grad_ch_w1, both)
    grad_ch_w2 = sum_low(grad_ch_w2, both)
    gain1, bias1, b1_s, b1_l, grad_gain2, grad_bias2, grad_ch_b1, grad_ch_b2 = lax.psum(
        (gain1, bias1, grads[0][2], grads[1][2], grad_gain2, grad_bias2, grad_ch_b1, grad_ch_b2), both
    )
    return (
        out_small, out_large, grads[0][0], grads[1][0], gain1, bias1,
        w1_s, b1_s, w2_s, b2_s, w1_l, b1_l, w2_l, b2_l,
        grad_gain2, grad_bias2, grad_ch_w1, grad_ch_b1, grad_ch_w2, grad_ch_b2,
    )


def solution(mesh):
    image = P("img", "blk", None)
    whole = P()
    rows = P("blk", None)
    columns = P(None, "blk")
    vector = P("blk")
    in_specs = (
        image, image, P("img", None), whole, whole,
        rows, whole, columns, vector, rows, whole, columns, vector,
        whole, whole, whole, whole, whole, whole, image, image,
    )
    out_specs = (
        image, image, image, image, whole, whole,
        rows, whole, columns, vector, rows, whole, columns, vector,
        whole, whole, whole, whole, whole, whole,
    )
    return jax.shard_map(local, mesh=mesh, in_specs=in_specs, out_specs=out_specs, check_vma=False)
```

time: 850 us -> 532 us (0.63)
  waiting for transfers between devices: 571 us -> 154 us
  blocking collectives: 61.2 us -> 115 us
  starting transfers between devices: 0.42 us -> 37.8 us
  local copies, waits for them, and re-layouts: 30.2 us -> 59.4 us
  matrix products: 121 us -> 95.8 us
    reduce_scatter x4 -> x2, waiting for transfers between devices: 210 us -> 0.01 us  [the longest x1 0.01 us: local(): lax.psum_scatter(grad_w1, 'blk', scatter_dimension=0, tiled=True)]
    psum x2, waiting for transfers between devices: 311 us -> 111 us  [the longest x1 67 us: local(): (w1_s, w2_s), (w1_l, w2_l) = lax.psum(scattered, 'img')]
    all_gather x4 -> x0, waiting for transfers between devices: 50.1 us -> none  [the longest x1 30 us: local(): lax.all_gather(jax.nn.gelu(preact_large).astype(jnp.bfloat16), 'blk', axi...]
    all_to_all x0 -> x8, waiting for transfers between devices: none -> 43 us  [the longest x4 30.9 us: to_rows(): moved = lax.all_to_all(blocks, 'blk', 0, 0, tiled=True)]
    all_gather x0 -> x4, blocking collectives: none -> 39.3 us  [the longest x2 26 us: local(): w1_all = lax.all_gather(w1, 'blk', axis=0, tiled=True)]
    all_to_all x0 -> x8, starting transfers between devices: none -> 31.5 us  [the longest x4 15.9 us: to_rows(): moved = lax.all_to_all(blocks, 'blk', 0, 0, tiled=True)]
    dot_general x18, matrix products: 121 us -> 95.8 us  [mm(): return jnp.einsum(spec, left, right, preferred_element_type=F32)]
    reduce_sum x7 -> x5, other arithmetic: 27.1 us -> 6.96 us  [the longest x4 5.13 us: local(): grad_b2 = jnp.sum(et.astype(F32), axis=(0, 2))]
  transfers between devices with their start and end apart: 10 -> 14, of which waited for: 8 -> 7; matrix products, arithmetic and copies ran while one was open for 12% -> 26% of each run, Pallas kernels for 0% -> 0%
where the time goes in v1:
time: 532 us; the launch traced here: 523 us
  waiting for transfers between devices  154 us (29%)
  blocking collectives  115 us (22%)
  matrix products  95.8 us (18%)
  local copies, waits for them, and re-layouts  59.4 us (11%)
  other arithmetic  43.9 us (8%)
  starting transfers between devices  37.8 us (7%)
  between operations  17.8 us (3%)
    dot_general x18, matrix products, mm(): return jnp.einsum(spec, left, right, preferred_element_type=F32)  95.8 us
    psum x1, waiting for transfers between devices, local(): (w1_s, w2_s), (w1_l, w2_l) = lax.psum(scattered, 'img')  67 us
    psum x1, waiting for transfers between devices, sum_low(): return lax.psum(values.astype(BF), axes).astype(F32)  43.7 us
    psum x1, blocking collectives, local(): lax.psum((gain1, bias1, grads[0][2], grads[1][2], grad_gain2, grad_bias2,...  39.7 us
    all_to_all x4, waiting for transfers between devices, to_rows(): moved = lax.all_to_all(blocks, 'blk', 0, 0, tiled=True)  30.9 us
    all_gather x2, blocking collectives, local(): w1_all = lax.all_gather(w1, 'blk', axis=0, tiled=True)  26 us
    psum x1, blocking collectives, local(): b2_s, b2_l = lax.psum((grads[0][4], grads[1][4]), 'img')  24 us
    unnamed x153, local copies, waits for them, and re-layouts  17.9 us
  transfers between devices with their start and end apart: 14, of which 7 were waited for; matrix products, arithmetic and copies ran while one was open for 26% of the time, Pallas kernels for 0%

profile of v1, /device:TPU:0, one launch (start us, length us, event | category | flops | bytes accessed | tf_op | source)
XLA Modules:
  0.0 522.9 jit_solution(3761951671542207293)
XLA Ops:
  29.5 19.2 %all-gather = bf16[4,49,384]{2,1,0:T(8,128)(2,1)S(1)} all-gather(bf16[1,49,384]{2,1,0:T(8,128)(2,1)S(1)} %bitcast.191), channel_id=1, replica_groups=mesh['img'=8,'blk'=4] {'blk'}, dimensions={0}, use_global_device_ids=true | all-gather | bytes 188160 | tf_op jit(solution)/shard_map/all_gather | solution.py:70
  48.8 5.5 %all-gather.1 = bf16[4,49,384]{2,1,0:T(8,128)(2,1)S(1)} all-gather(bf16[1,49,384]{2,1,0:T(8,128)(2,1)S(1)} %bitcast.192), channel_id=1, replica_groups=mesh['img'=8,'blk'=4] {'blk'}, dimensions={0}, use_global_device_ids=true | all-gather | bytes 188160 | tf_op jit(solution)/shard_map/all_gather | solution.py:71
  55.1 6.8 %all_gather.14 = bf16[576,384]{1,0:T(8,128)(2,1)S(1)} all-gather(bf16[144,384]{1,0:T(8,128)(2,1)S(1)} %copy-done.38), channel_id=1, replica_groups=mesh['img'=8,'blk'=4] {'blk'}, dimensions={0}, use_global_device_ids=true | all-gather | bytes 552960 | tf_op jit(solution)/shard_map/all_gather | solution.py:70
  61.9 7.7 %all_gather.15 = bf16[384,576]{0,1:T(8,128)(2,1)} all-gather(bf16[384,144]{0,1:T(8,128)(2,1)} %param.32), channel_id=1, replica_groups=mesh['img'=8,'blk'=4] {'blk'}, dimensions={1}, use_global_device_ids=true | all-gather | bytes 552960 | tf_op jit(solution)/shard_map/all_gather | solution.py:71
  92.7 4.5 all-to-all-start.3
  101.7 13.1 %all-to-all-done.3 = bf16[36,144,128]{2,1,0:T(8,128)(2,1)} async-done(((bf16[36,144,128]{2,1,0:T(8,128)(2,1)}), bf16[36,144,128]{2,1,0:T(8,128)(2,1)}, u32[]{:S(2)}, u32[]{:S(2)}) %all-to-all-start.3) | async-done | bytes 1327136 | tf_op jit(solution)/shard_map/all_to_all | solution.py:41
  117.8 12.3 %convolution_add_fusion = f32[1060,3072]{1,0:T(8,128)} fusion(bf16[768,3072]{1,0:T(8,128)(2,1)} %param.36, f32[3072]{0:T(1024)S(1)} %copy-done.54, f32[768]{0:T(1024)S(1)} %copy-done.55, f32[768]{0:T(1024)S(1)} %copy-done.45, f32[1060]{0:T(1024)S(1)} %fusion.70, f32[1060]{0:T(1024)S(1)} %broadcast_multiply_fusion.1, f32[864,768]{1,0:T(8,128)S(1)} %bitcast.150, ...), kind=kOutput, calls=%fused_computation.2 | convolution fusion | flops 5009848320 | bytes 21027104 | tf_op jit(solution)/shard_map/rd,dk->rk/dot_general | solution.py:47
  130.1 18.6 %convert_reduce_fusion = (f32[3072]{0:T(1024)}, bf16[1060,3072]{1,0:T(8,128)(2,1)}) fusion(f32[1060,3072]{1,0:T(8,128)} %convolution_add_fusion, bf16[3072,768]{1,0:T(8,128)(2,1)S(1)} %bitcast.196, f32[1060]{0:T(1024)S(1)} %pad_maximum_fusion.2, bf16[864,768]{1,0:T(8,128)(2,1)S(1)} %bitcast.184, bf16[196,768]{1,0:T(8,128)(2,1)S(1)} %reshape.292), kind=kOutput, calls=%fused_computation.10 | convolution fusion | flops 5078227968 | bytes 25901200 | tf_op jit(solution)/shard_map/rd,kd->rk/dot_general | solution.py:47
  148.7 9.6 %multiply_reduce_fusion = (f32[768]{0:T(1024)}, f32[1060]{0:T(1024)S(1)}, f32[768]{0:T(1024)}, f32[1060,768]{1,0:T(8,128)S(1)}) fusion(f32[1060]{0:T(1024)S(1)} %fusion.70, f32[1060]{0:T(1024)S(1)} %broadcast_multiply_fusion.1, f32[864,768]{1,0:T(8,128)S(1)} %bitcast.151, f32[196,768]{1,0:T(8,128)S(1)} %reshape.282, f32[768]{0:T(1024)S(1)} %copy-done.45, ...), kind=kOutput, calls=%fused_computation.29 | convolution fusion | flops 5009031168 | bytes 17765808 | tf_op jit(solution)/shard_map/rk,dk->rd/dot_general | solution.py:47
  171.3 4.3 all-to-all-start.6
  181.7 11.5 %all-to-all-done.6 = bf16[36,144,128]{2,1,0:T(8,128)(2,1)} async-done(((bf16[36,144,128]{2,1,0:T(8,128)(2,1)}), bf16[36,144,128]{2,1,0:T(8,128)(2,1)}, u32[]{:S(2)}, u32[]{:S(2)}) %all-to-all-start.6) | async-done | bytes 1327136 | tf_op jit(solution)/shard_map/all_to_all | solution.py:29
  204.5 13.9 %convolution_convert_fusion = bf16[3072,768]{1,0:T(8,128)(2,1)} fusion(f32[1060]{0:T(1024)S(1)} %pad_maximum_fusion.2, bf16[864,768]{1,0:T(8,128)(2,1)} %bitcast.183, bf16[196,768]{1,0:T(8,128)(2,1)S(1)} %copy-done.17, f32[1060,3072]{1,0:T(8,128)} %convolution_add_fusion), kind=kOutput, calls=%fused_computation.12 | convolution fusion | flops 5038258176 | bytes 19376272 | tf_op jit(solution)/shard_map/rk,rd->kd/dot_general | solution.py:47
  220.6 11.9 %convolution_convert_fusion.1 = bf16[768,3072]{1,0:T(8,128)(2,1)} fusion(bf16[1060,3072]{1,0:T(8,128)(2,1)} %get-tuple-element.147, f32[768]{0:T(1024)S(1)} %copy-done.55, f32[768]{0:T(1024)S(1)} %copy-done.45, f32[1060]{0:T(1024)S(1)} %fusion.70, f32[1060]{0:T(1024)S(1)} %broadcast_multiply_fusion.1, f32[864,768]{1,0:T(8,128)} %bitcast.153, ...), kind=kOutput, calls=%fused_computation.13 | convolution fusion | flops 5008951296 | bytes 14502176 | tf_op jit(solution)/shard_map/rd,rk->dk/dot_general | solution.py:47
  233.2 12.8 %fusion.15 = bf16[1060,768]{1,0:T(8,128)(2,1)S(1)} fusion(bf16[3072,768]{1,0:T(8,128)(2,1)} %param.38, f32[1060]{0:T(1024)S(1)} %pad_maximum_fusion.2, f32[768]{0:T(1024)S(1)} %copy-done.56, f32[864,768]{1,0:T(8,128)} %bitcast.154, f32[196,768]{1,0:T(8,128)S(1)} %reshape.282, f32[1060,3072]{1,0:T(8,128)} %convolution_add_fusion), kind=kOutput, calls=%fused_computation.26 | convolution fusion | flops 5035084800 | bytes 22635664 | tf_op jit(solution)/shard_map/rk,kd->rd/dot_general | solution.py:47
  251.2 24.0 %all-reduce.5 = (f32[49]{0:T(128)}, f32[144]{0:T(256)}) all-reduce(f32[49]{0:T(128)S(1)} %reduce_sum.315, f32[144]{0:T(256)S(1)} %reduce_sum.319), channel_id=1, replica_groups=mesh['img'=8,'blk'=4] {'img'}, use_global_device_ids=true, to_apply=%region_28.0 | all-reduce | flops 193 | bytes 1544 | tf_op jit(solution)/shard_map/psum | solution.py:129
  277.9 11.5 %fusion.75 = (f32[64,384]{1,0:T(8,128)S(1)}, f32[384,64]{0,1:T(8,128)S(1)}) fusion(f32[196,384]{1,0:T(8,128)S(1)} %fusion.78, f32[384,196]{0,1:T(8,128)S(1)} %fusion.79), kind=kCustom, calls=%all-reduce-scatter.2 | all-reduce-scatter fusion | flops 196609 | bytes 799232
  291.0 4.3 collective-permute-start
  302.4 5.0 all-to-all-done.5
  326.7 12.8 %all-to-all-done.7 = bf16[36,144,128]{2,1,0:T(8,128)(2,1)S(1)} async-done(((bf16[36,144,128]{2,1,0:T(8,128)(2,1)}), bf16[36,144,128]{2,1,0:T(8,128)(2,1)S(1)}, u32[]{:S(2)}, u32[]{:S(2)}) %all-to-all-start.7) | async-done | bytes 1327136 | tf_op jit(solution)/shard_map/all_to_all | solution.py:41
  342.4 39.7 %all-reduce.4 = (f32[768]{0:T(1024)}, f32[768]{0:T(1024)}, f32[384]{0:T(512)}, f32[384]{0:T(512)}, f32[768]{0:T(1024)}, /*index=5*/f32[768]{0:T(1024)}, f32[3072]{0:T(1024)}, f32[768]{0:T(1024)}) all-reduce(f32[768]{0:T(1024)S(1)} %add.249, f32[768]{0:T(1024)S(1)} %add_bitcast_fusion, ...), channel_id=1, replica_groups=mesh['img'=8,'blk'=4] {'img','blk'}, use_global_device_ids=true, to_apply=%region_14.0 | all-reduce | flops 7680 | bytes 61440 | tf_op jit(solution)/shard_map/psum | solution.py:133
  386.0 43.7 %all-reduce.14.cloned.1.call-done = (bf16[768,3072]{1,0:T(8,128)(2,1)}, bf16[3072,768]{1,0:T(8,128)(2,1)}) async-done(((bf16[768,3072]{1,0:T(8,128)(2,1)}, bf16[3072,768]{1,0:T(8,128)(2,1)}), (bf16[768,3072]{1,0:T(8,128)(2,1)}, bf16[3072,768]{1,0:T(8,128)(2,1)})) %all-reduce.14.cloned.1.call-update) | async-done | bytes 9437200 | tf_op jit(solution)/shard_map/psum | solution.py:51
  429.7 7.5 %convert_element_type.235 = f32[768,3072]{1,0:T(8,128)} convert(bf16[768,3072]{1,0:T(8,128)(2,1)} %get-tuple-element.121) | non-fusion elementwise | flops 2359296 | bytes 14155776 | tf_op jit(solution)/shard_map/convert_element_type | solution.py:51
  437.2 4.5 convert_element_type.238
  441.7 67.0 %all-reduce.12.cloned.1.call-done = (f32[49,384]{1,0:T(8,128)}, f32[384,49]{0,1:T(8,128)}, f32[144,384]{1,0:T(8,128)}, f32[384,144]{0,1:T(8,128)}) async-done(((f32[49,384]{1,0:T(8,128)}, f32[384,49]{0,1:T(8,128)}, f32[144,384]{1,0:T(8,128)}, f32[384,144]{0,1:T(8,128)}), (f32[49,384]{1,0:T(8,128)}, f32[384,49]{0,1:T(8,128)}, f32[144,384]{1,0:T(8,128)}, f32[384,144]{0,1:T(8,128)})) %all-reduce.12.cloned.1.call-update) | async-done | bytes 592912 | tf_op jit(solution)/shard_map/psum | solution.py:128
  (275 shorter events, 133.3 us)
Async XLA Ops:
  14.2 11.7 %all-to-all-start = ((bf16[24,49,128]{2,1,0:T(8,128)(2,1)}), bf16[24,49,128]{2,1,0:T(8,128)(2,1)}, u32[]{:S(2)}, u32[]{:S(2)}) async-start(bf16[24,49,128]{2,1,0:T(8,128)(2,1)} %bitcast.1), calls=%async_computation | async-start | bytes 688128 | tf_op jit(solution)/shard_map/all_to_all | solution.py:29
  24.0 31.0 %copy-start.38 = (bf16[144,384]{1,0:T(8,128)(2,1)S(1)}, bf16[144,384]{1,0:T(8,128)(2,1)}, u32[]{:S(2)}) copy-start(bf16[144,384]{1,0:T(8,128)(2,1)} %param.30) | copy-start | bytes 331780
  25.3 23.5 %copy-start.42 = (bf16[384,49]{0,1:T(8,128)(2,1)S(1)}, bf16[384,49]{0,1:T(8,128)(2,1)}, u32[]{:S(2)}) copy-start(bf16[384,49]{0,1:T(8,128)(2,1)} %param.28) | copy-start | bytes 112900
  25.9 53.1 %all-to-all-start.2 = ((bf16[36,144,128]{2,1,0:T(8,128)(2,1)}), bf16[36,144,128]{2,1,0:T(8,128)(2,1)S(1)}, u32[]{:S(2)}, u32[]{:S(2)}) async-start(bf16[36,144,128]{2,1,0:T(8,128)(2,1)} %bitcast.165), calls=%async_computation.2 | async-start | bytes 2654208 | tf_op jit(solution)/shard_map/all_to_all | solution.py:29
  29.5 42.0 %copy-start.57 = (f32[384]{0:T(512)S(1)}, f32[384]{0:T(512)}, u32[]{:S(2)}) copy-start(f32[384]{0:T(512)} %param.27) | copy-start | bytes 4612
  48.8 24.4 %copy-start.21 = (bf16[196,384]{1,0:T(8,128)(2,1)}, bf16[196,384]{1,0:T(8,128)(2,1)S(1)}, u32[]{:S(2)}) copy-start(bf16[196,384]{1,0:T(8,128)(2,1)S(1)} %reshape.315) | copy-start | bytes 451588
  61.9 21.8 %copy-start.12 = (bf16[576,384]{1,0:T(8,128)(2,1)}, bf16[576,384]{1,0:T(8,128)(2,1)S(1)}, u32[]{:S(2)}) copy-start(bf16[576,384]{1,0:T(8,128)(2,1)S(1)} %all_gather.14) | copy-start | bytes 1327108
  79.0 13.7 %all-to-all-start.1 = ((bf16[24,49,128]{2,1,0:T(8,128)(2,1)}), bf16[24,49,128]{2,1,0:T(8,128)(2,1)}, u32[]{:S(2)}, u32[]{:S(2)}) async-start(bf16[24,49,128]{2,1,0:T(8,128)(2,1)} %bitcast.182), calls=%async_computation.1 | async-start | bytes 688128 | tf_op jit(solution)/shard_map/all_to_all | solution.py:41
  92.7 22.0 %all-to-all-start.3 = ((bf16[36,144,128]{2,1,0:T(8,128)(2,1)}), bf16[36,144,128]{2,1,0:T(8,128)(2,1)}, u32[]{:S(2)}, u32[]{:S(2)}) async-start(bf16[36,144,128]{2,1,0:T(8,128)(2,1)} %bitcast.20), calls=%async_computation.3 | async-start | bytes 2654208 | tf_op jit(solution)/shard_map/all_to_all | solution.py:41
  99.6 60.1 %copy-start.16 = (bf16[196,768]{1,0:T(8,128)(2,1)}, bf16[196,768]{1,0:T(8,128)(2,1)S(1)}, u32[]{:S(2)}) copy-start(bf16[196,768]{1,0:T(8,128)(2,1)S(1)} %reshape.292) | copy-start | bytes 903172
  116.5 41.8 %copy-start.1 = (f32[6,144,768]{2,1,0:T(8,128)}, f32[6,144,768]{2,1,0:T(8,128)S(1)}, u32[]{:S(2)}) copy-start(f32[6,144,768]{2,1,0:T(8,128)S(1)} %fusion.27) | copy-start | bytes 7962628
  117.7 31.0 %slice-start = ((s8[4718592]{0:T(1024)(128)(4,1)}), s8[4194304]{0:T(1024)(128)(4,1)S(1)}, s32[]{:S(2)}) async-start(s8[4718592]{0:T(1024)(128)(4,1)} %bitcast.193), calls=%async_computation.14 | async-start | bytes 8388608
  171.3 21.8 %all-to-all-start.6 = ((bf16[36,144,128]{2,1,0:T(8,128)(2,1)}), bf16[36,144,128]{2,1,0:T(8,128)(2,1)}, u32[]{:S(2)}, u32[]{:S(2)}) async-start(bf16[36,144,128]{2,1,0:T(8,128)(2,1)} %bitcast.166), calls=%async_computation.6 | async-start | bytes 2654208 | tf_op jit(solution)/shard_map/all_to_all | solution.py:29
  193.2 82.1 %all-to-all-start.4 = ((bf16[24,49,128]{2,1,0:T(8,128)(2,1)}), bf16[24,49,128]{2,1,0:T(8,128)(2,1)S(1)}, u32[]{:S(2)}, u32[]{:S(2)}) async-start(bf16[24,49,128]{2,1,0:T(8,128)(2,1)} %bitcast.180), calls=%async_computation.4 | async-start | bytes 688128 | tf_op jit(solution)/shard_map/all_to_all | solution.py:29
  196.6 185.5 %reduce-scatter.7.cloned.1.call-start = ((), (), s32[]{:S(2)}) async-start(), calls=%async_computation.10 | async-start | bytes 1105920 | tf_op jit(solution)/shard_map/reduce_scatter | solution.py:123
  204.4 177.7 %reduce-scatter.9.cloned.1.call-start = ((), (), s32[]{:S(2)}) async-start(), calls=%async_computation.11 | async-start | bytes 1105920 | tf_op jit(solution)/shard_map/reduce_scatter | solution.py:124
  220.4 209.3 %all-reduce.14.cloned.1.call-start = ((), (), s32[]{:S(2)}) async-start(), calls=%async_computation.13 | async-start | bytes 18874368 | tf_op jit(solution)/shard_map/psum | solution.py:51
  248.1 27.4 %copy-start.11 = (bf16[384,768]{0,1:T(8,128)(2,1)S(1)}, bf16[384,768]{0,1:T(8,128)(2,1)}, u32[]{:S(2)}) copy-start(bf16[384,768]{0,1:T(8,128)(2,1)} %copy-done.10) | copy-start | bytes 1769476
  250.1 25.7 %copy-start.24 = (bf16[196,384]{1,0:T(8,128)(2,1)S(1)}, bf16[196,384]{1,0:T(8,128)(2,1)}, u32[]{:S(2)}) copy-start(bf16[196,384]{1,0:T(8,128)(2,1)} %reshape.317) | copy-start | bytes 451588
  289.4 11.1 %collective-permute-start.1 = (f32[384,45]{0,1:T(8,128)S(1)}, f32[384,45]{0,1:T(8,128)S(1)}, u32[]{:S(2)}, u32[]{:S(2)}) collective-permute-start(f32[384,45]{0,1:T(8,128)S(1)} %slice.31), channel_id=1, source_target_pairs={{0,1},{1,2},{2,3},{4,5},{5,6},{6,7},{8,9},{9,10},{10,11},{12,13},{... | collective-permute-start | bytes 207368
  291.0 9.8 %collective-permute-start = (f32[45,384]{1,0:T(8,128)S(1)}, f32[45,384]{1,0:T(8,128)S(1)}, u32[]{:S(2)}, u32[]{:S(2)}) collective-permute-start(f32[45,384]{1,0:T(8,128)S(1)} %slice.30), channel_id=1, source_target_pairs={{0,1},{1,2},{2,3},{4,5},{5,6},{6,7},{8,9},{9,10},{10,11},{12,13},{... | collective-permute-start | bytes 207368
  296.8 10.6 %all-to-all-start.5 = ((bf16[24,49,128]{2,1,0:T(8,128)(2,1)}), bf16[24,49,128]{2,1,0:T(8,128)(2,1)S(1)}, u32[]{:S(2)}, u32[]{:S(2)}) async-start(bf16[24,49,128]{2,1,0:T(8,128)(2,1)} %bitcast.35), calls=%async_computation.5 | async-start | bytes 688128 | tf_op jit(solution)/shard_map/all_to_all | solution.py:41
  318.5 21.0 %all-to-all-start.7 = ((bf16[36,144,128]{2,1,0:T(8,128)(2,1)}), bf16[36,144,128]{2,1,0:T(8,128)(2,1)S(1)}, u32[]{:S(2)}, u32[]{:S(2)}) async-start(bf16[36,144,128]{2,1,0:T(8,128)(2,1)} %bitcast.164), calls=%async_computation.7 | async-start | bytes 2654208 | tf_op jit(solution)/shard_map/all_to_all | solution.py:41
  322.1 186.7 %all-reduce.12.cloned.1.call-start = ((), (), s32[]{:S(2)}) async-start(), calls=%async_computation.12 | async-start | bytes 1228800 | tf_op jit(solution)/shard_map/psum | solution.py:128
  (57 other events, 347.0 us)
Sparse Core Ops, SparseCore 0:
  204.5 26.2 reduce-scatter.6
  233.4 26.2 reduce-scatter.8
Sparse Core Ops, SparseCore 1:
  232.6 197.0 all-reduce.13
  435.0 73.6 all-reduce.11

commit v2 on v1

--- a/solution.py
+++ b/solution.py
@@ -1,6 +1,10 @@
+import functools
+
 import jax
 import jax.numpy as jnp
 from jax import lax
+from jax.experimental import pallas as pl
+from jax.experimental.pallas import tpu as pltpu
 from jax.sharding import PartitionSpec as P
 
 EPSILON = 1e-06
@@ -47,8 +51,469 @@
     return jnp.einsum(spec, left, right, preferred_element_type=F32)
 
 
-def sum_low(values, axes):
-    return lax.psum(values.astype(BF), axes).astype(F32)
+MESH = pl.DeviceIdType.MESH
+ANY = pl.BlockSpec(memory_space=pl.ANY)
+TILE = 256
+TOP = 62 * 1024 * 1024
+
+
+def img_split(size):
+    near = 2 if size <= 8 else 8
+    return near, size // near
+
+
+def gelu_pair(a):
+    square = a * a
+    slope = 0.7978845608028654
+    t = jnp.tanh(a * (slope + (slope * 0.044715) * square))
+    half = 0.5 + 0.5 * t
+    inner = slope + (3.0 * slope * 0.044715) * square
+    return a * half, half + (0.5 * a) * (1.0 - t * t) * inner
+
+
+class Peers:
+    def __init__(self, near_count):
+        self.img = lax.axis_index("img")
+        self.blk = lax.axis_index("blk")
+        self.core = lax.rem(self.blk, 2)
+        self.x = self.blk // 2
+        self.near_count = near_count
+        self.near = lax.rem(self.img, near_count)
+        self.far = self.img // near_count
+
+    def at(self, axis, place):
+        if axis == "core":
+            return (self.img, self.x * 2 + place)
+        if axis == "x":
+            return (self.img, place * 2 + self.core)
+        if axis == "near":
+            return (self.far * self.near_count + place, self.blk)
+        return (place * self.near_count + self.near, self.blk)
+
+    def mine(self, axis):
+        return {"core": self.core, "x": self.x, "near": self.near, "far": self.far}[axis]
+
+
+def greet(peers, axes):
+    barrier = pltpu.get_barrier_semaphore()
+    total = 0
+    for axis, count in axes:
+        for j in range(1, count):
+            there = lax.rem(peers.mine(axis) + j, count)
+            pl.semaphore_signal(barrier, inc=1, device_id=peers.at(axis, there), device_id_type=MESH)
+            total += 1
+    pl.semaphore_wait(barrier, total)
+
+
+def channel_kernel(
+    near, far, far_inside,
+    y_hbm, ec_hbm, w1_hbm, w2_hbm, b1_ref, gain_ref, bias_ref, b2_ref,
+    out_hbm, ey_hbm, chunk_ref, small_ref,
+    y, ec, v, lt, rt, w1, w2, acc_out, acc_ev, out_low,
+    keep, core_tx, core_rx, keep_n, near_tx, near_rx, keep_f, far_tx, far_rx, keep_x, x_tx, x_rx,
+    in_sem, w_sem, out_sem, core_ss, core_rs, near_ss, near_rs, far_ss, far_rs, x_ss, x_rs,
+):
+    rows, width = y.shape
+    tiles = w1.shape[0]
+    peers = Peers(near)
+    core = peers.core
+    part = 128
+    parts = rows // part
+
+    def w_copies(t):
+        return (
+            pltpu.make_async_copy(w1_hbm.at[:, pl.ds(t * TILE, TILE)], w1.at[t], w_sem.at[0, t]),
+            pltpu.make_async_copy(w2_hbm.at[pl.ds(t * TILE, TILE)], w2.at[t], w_sem.at[1, t]),
+        )
+
+    y_in = pltpu.make_async_copy(y_hbm, y, in_sem.at[0])
+    ec_in = pltpu.make_async_copy(ec_hbm, ec, in_sem.at[1])
+    y_in.start()
+    ec_in.start()
+
+    def start_w(t, carry):
+        for copy in w_copies(t):
+            copy.start()
+        return carry
+
+    lax.fori_loop(0, tiles, start_w, 0)
+    axes = [("core", 2), ("near", near)] + ([("far", far)] if far_inside else []) + [("x", 2)]
+    greet(peers, axes)
+    y_in.wait()
+    ec_in.wait()
+    small_ref[...] = jnp.zeros_like(small_ref)
+
+    def prepare(p, carry):
+        at = pl.ds(pl.multiple_of(p * part, part), part)
+        row = y[at, :]
+        mean = jnp.mean(row, axis=-1, keepdims=True)
+        centered = row - mean
+        var = jnp.mean(centered * centered, axis=-1, keepdims=True)
+        normed = centered * lax.rsqrt(var + EPSILON) * gain_ref[...] + bias_ref[...]
+        low = normed.astype(BF)
+        v[at, :] = low
+        lt[0, :, at] = low.T
+        own = ec[at, :]
+        lt[1, :, at] = own.T
+        small_ref[4:5, :] += jnp.sum(own.astype(F32), axis=0, keepdims=True)
+        acc_out[at, :] = jnp.zeros((part, width), F32)
+        acc_ev[at, :] = jnp.zeros((part, width), F32)
+        return carry
+
+    lax.fori_loop(0, parts, prepare, 0)
+
+    def send(src, dst, ss, rs, device):
+        return pltpu.make_async_remote_copy(
+            src_ref=src, dst_ref=dst, send_sem=ss, recv_sem=rs, device_id=device, device_id_type=MESH
+        )
+
+    def core_copy(t):
+        slot = lax.rem(t, 2)
+        return send(core_tx.at[slot], core_rx.at[t], core_ss.at[slot], core_rs.at[t], peers.at("core", 1 - core))
+
+    def near_copy(t, j):
+        slot = lax.rem(t, 2)
+        there = lax.rem(peers.near + j, near)
+        return send(
+            near_tx.at[slot, j - 1], near_rx.at[t, j - 1], near_ss.at[slot, j - 1], near_rs.at[t, j - 1],
+            peers.at("near", there),
+        )
+
+    def far_copy(t, j):
+        slot = lax.rem(t, 2)
+        there = lax.rem(peers.far + j, far)
+        return send(
+            far_tx.at[slot, j - 1], far_rx.at[t, j - 1], far_ss.at[slot, j - 1], far_rs.at[t, j - 1],
+            peers.at("far", there),
+        )
+
+    def x_copy(t):
+        slot = lax.rem(t, 2)
+        return send(x_tx.at[slot], x_rx.at[t], x_ss.at[slot], x_rs.at[t], peers.at("x", 1 - peers.x))
+
+    step_rows = rows // 3
+
+    def tile_step(t):
+        for copy in w_copies(t):
+            copy.wait()
+        columns = pl.ds(pl.multiple_of(t * TILE, TILE), TILE)
+        bias = b1_ref[:, columns]
+
+        def act(p, total):
+            at = pl.ds(pl.multiple_of(p * step_rows, step_rows), step_rows)
+            a = jnp.dot(v[at, :], w1[t], preferred_element_type=F32) + bias
+            gh = lax.dot_general(ec[at, :], w2[t], (((1,), (1,)), ((), ())), preferred_element_type=F32)
+            g, slope = gelu_pair(a)
+            ea = (slope * gh).astype(BF)
+            rt[1, at, :] = g.astype(BF)
+            rt[0, at, :] = ea
+            return total + jnp.sum(ea.astype(F32), axis=0, keepdims=True)
+
+        total = lax.fori_loop(0, rows // step_rows, act, jnp.zeros((1, TILE), F32))
+        small_ref[lax.div(t, 3), pl.ds(pl.multiple_of(lax.rem(t, 3) * TILE, TILE), TILE)] = total[0]
+
+        slot = lax.rem(t, 2)
+
+        @pl.when(t >= 2)
+        def _():
+            core_copy(t - 2).wait_send()
+
+        core_tx[slot] = jnp.dot(lt[1 - core], rt[1 - core], preferred_element_type=F32).astype(BF)
+        core_copy(t).start()
+        keep[slot] = jnp.dot(lt[core], rt[core], preferred_element_type=F32)
+        def add(p, carry):
+            at = pl.ds(pl.multiple_of(p * step_rows, step_rows), step_rows)
+            acc_out[at, :] += jnp.dot(rt[1, at, :], w2[t], preferred_element_type=F32)
+            acc_ev[at, :] += lax.dot_general(
+                rt[0, at, :], w1[t], (((1,), (1,)), ((), ())), preferred_element_type=F32
+            )
+            return carry
+
+        lax.fori_loop(0, rows // step_rows, add, 0)
+
+    share = rows // 4
+    piece = share // 3
+
+    def out_copies(p):
+        at = pl.ds(pl.multiple_of(p * share, share), share)
+        return (
+            pltpu.make_async_copy(out_low.at[at], out_hbm.at[at], out_sem.at[0, p]),
+            pltpu.make_async_copy(acc_ev.at[at], ey_hbm.at[at], out_sem.at[1, p]),
+        )
+
+    def finish(p):
+        def one(q, carry):
+            at = pl.ds(pl.multiple_of(p * share + q * piece, piece), piece)
+            row = y[at, :]
+            out_low[at, :] = (row + acc_out[at, :] + b2_ref[...]).astype(BF)
+            mean = jnp.mean(row, axis=-1, keepdims=True)
+            centered = row - mean
+            var = jnp.mean(centered * centered, axis=-1, keepdims=True)
+            scale = lax.rsqrt(var + EPSILON)
+            unit = centered * scale
+            ev = acc_ev[at, :]
+            small_ref[5:6, :] += jnp.sum(ev * unit, axis=0, keepdims=True)
+            small_ref[6:7, :] += jnp.sum(ev, axis=0, keepdims=True)
+            d = ev * gain_ref[...]
+            m1 = jnp.mean(d, axis=-1, keepdims=True)
+            m2 = jnp.mean(d * unit, axis=-1, keepdims=True)
+            acc_ev[at, :] = ec[at, :].astype(F32) + scale * (d - m1 - unit * m2)
+            return carry
+
+        lax.fori_loop(0, 3, one, 0)
+        for copy in out_copies(p):
+            copy.start()
+
+    def core_sum(t):
+        slot = lax.rem(t, 2)
+        core_copy(t).wait_recv()
+
+        @pl.when(t >= 2)
+        def _():
+            for j in range(1, near):
+                near_copy(t - 2, j).wait_send()
+
+        each = width // near
+        for j in range(near):
+            there = lax.rem(peers.near + j, near)
+            at = pl.ds(pl.multiple_of(there * each, each), each)
+            value = keep[slot, at, :] + core_rx[t, at, :].astype(F32)
+            if j == 0:
+                keep_n[slot] = value
+            else:
+                near_tx[slot, j - 1] = value.astype(BF)
+                near_copy(t, j).start()
+
+    def near_sum(t):
+        slot = lax.rem(t, 2)
+        for j in range(1, near):
+            near_copy(t, j).wait_recv()
+
+        if far_inside:
+            @pl.when(t >= 2)
+            def _():
+                for j in range(1, far):
+                    far_copy(t - 2, j).wait_send()
+
+            each = width // near // far
+            for j in range(1, far + 1):
+                there = lax.rem(peers.far + j, far)
+                at = pl.ds(pl.multiple_of(there * each, each), each)
+                value = keep_n[slot, at, :]
+                for k in range(near - 1):
+                    value += near_rx[t, k, at, :].astype(F32)
+                if j == far:
+                    keep_f[slot] = value
+                else:
+                    far_tx[slot, j - 1] = value.astype(BF)
+                    far_copy(t, j).start()
+        else:
+            value = keep_n[slot]
+            for k in range(near - 1):
+                value += near_rx[t, k].astype(F32)
+            keep_f[slot] = value
+
+    def far_sum(t):
+        slot = lax.rem(t, 2)
+        if far_inside:
+            for j in range(1, far):
+                far_copy(t, j).wait_recv()
+
+        @pl.when(t >= 2)
+        def _():
+            x_copy(t - 2).wait_send()
+
+        each = chunk_ref.shape[0]
+        for there, own in ((peers.x, True), (1 - peers.x, False)):
+            at = pl.ds(pl.multiple_of(there * each, each), each)
+            value = keep_f[slot, at, :]
+            if far_inside:
+                for k in range(far - 1):
+                    value += far_rx[t, k, at, :].astype(F32)
+            if own:
+                keep_x[slot] = value
+            else:
+                x_tx[slot] = value.astype(BF)
+                x_copy(t).start()
+
+    def x_sum(t):
+        slot = lax.rem(t, 2)
+        x_copy(t).wait_recv()
+        columns = pl.ds(pl.multiple_of(t * TILE, TILE), TILE)
+        chunk_ref[:, columns] = (keep_x[slot] + x_rx[t].astype(F32)).astype(BF)
+
+    stages = (core_sum, near_sum, far_sum, x_sum)
+
+    def step(s, carry):
+        @pl.when(s < tiles)
+        def _():
+            tile_step(s)
+
+        for lag, stage in enumerate(stages):
+            t = s - lag
+            @pl.when((t >= 0) & (t < tiles))
+            def _(t=t, stage=stage):
+                stage(t)
+
+        @pl.when(s >= tiles)
+        def _():
+            finish(s - tiles)
+
+        return carry
+
+    lax.fori_loop(0, tiles + 4, step, 0)
+    for t in (tiles - 2, tiles - 1):
+        core_copy(t).wait_send()
+        for j in range(1, near):
+            near_copy(t, j).wait_send()
+        if far_inside:
+            for j in range(1, far):
+                far_copy(t, j).wait_send()
+        x_copy(t).wait_send()
+    for p in range(4):
+        for copy in out_copies(p):
+            copy.wait()
+
+
+def channel(y, ec, w1, w2, b1, gain, bias, b2):
+    rows, width = y.shape
+    hidden = w1.shape[1]
+    tiles = hidden // TILE
+    near, far = img_split(lax.axis_size("img"))
+    far_inside = width % (near * far * 2 * 16) == 0
+    f = far if far_inside else 1
+    chunk = width // near // f // 2
+    vmem = pl.BlockSpec(memory_space=pltpu.VMEM)
+    V = pltpu.VMEM
+    DMA = pltpu.SemaphoreType.DMA
+    fm = max(f - 1, 1)
+    return pl.pallas_call(
+        functools.partial(channel_kernel, near, far, far_inside),
+        out_shape=(
+            jax.ShapeDtypeStruct((rows, width), BF),
+            jax.ShapeDtypeStruct((rows, width), F32),
+            jax.ShapeDtypeStruct((chunk, hidden), BF),
+            jax.ShapeDtypeStruct((8, width), F32),
+        ),
+        in_specs=[ANY] * 4 + [vmem] * 4,
+        out_specs=(ANY, ANY, vmem, vmem),
+        scratch_shapes=[
+            V((rows, width), F32), V((rows, width), BF), V((rows, width), BF),
+            V((2, width, rows), BF), V((2, rows, TILE), BF),
+            V((tiles, width, TILE), BF), V((tiles, TILE, width), BF),
+            V((rows, width), F32), V((rows, width), F32), V((rows, width), BF),
+            V((2, width, TILE), F32), V((2, width, TILE), BF), V((tiles, width, TILE), BF),
+            V((2, width // near, TILE), F32), V((2, near - 1, width // near, TILE), BF),
+            V((tiles, near - 1, width // near, TILE), BF),
+            V((2, chunk * 2, TILE), F32), V((2, fm, chunk * 2, TILE), BF), V((tiles, fm, chunk * 2, TILE), BF),
+            V((2, chunk, TILE), F32), V((2, chunk, TILE), BF), V((tiles, chunk, TILE), BF),
+            DMA((2,)), DMA((2, tiles)), DMA((2, 4)),
+            DMA((2,)), DMA((tiles,)),
+            DMA((2, near - 1)), DMA((tiles, near - 1)),
+            DMA((2, fm)), DMA((tiles, fm)),
+            DMA((2,)), DMA((tiles,)),
+        ],
+        compiler_params=pltpu.CompilerParams(
+            collective_id=0, has_side_effects=True, vmem_limit_bytes=TOP
+        ),
+    )(y, ec, w1, w2, b1.reshape(1, -1), gain.reshape(1, -1), bias.reshape(1, -1), b2.reshape(1, -1))
+
+
+GROUPS = 6
+
+
+def gather_kernel(near, far, far_inside, chunk_hbm, full_hbm, own_sem, x_ss, x_rs, far_ss, far_rs, near_ss, near_rs, core_ss, core_rs):
+    each, hidden = chunk_hbm.shape
+    peers = Peers(near)
+    f = far if far_inside else 1
+    f_place = peers.far if far_inside else 0
+    cols = hidden // GROUPS
+    axes = [("core", 2), ("near", near)] + ([("far", far)] if far_inside else []) + [("x", 2)]
+    base_n = peers.near * (each * 2 * f)
+    base_f = base_n + f_place * (each * 2)
+    base_x = base_f + peers.x * each
+
+    def block(start, size, k):
+        return full_hbm.at[peers.core, pl.ds(pl.multiple_of(start, each), size), pl.ds(k * cols, cols)]
+
+    def send(src, dst, ss, rs, device):
+        return pltpu.make_async_remote_copy(
+            src_ref=src, dst_ref=dst, send_sem=ss, recv_sem=rs, device_id=device, device_id_type=MESH
+        )
+
+    def own(k):
+        return pltpu.make_async_copy(chunk_hbm.at[:, pl.ds(k * cols, cols)], block(base_x, each, k), own_sem.at[k])
+
+    def x_copy(k):
+        return send(chunk_hbm.at[:, pl.ds(k * cols, cols)], block(base_x, each, k), x_ss.at[k], x_rs.at[k], peers.at("x", 1 - peers.x))
+
+    def far_copy(k, j):
+        there = lax.rem(peers.far + j, far)
+        span = block(base_f, each * 2, k)
+        return send(span, span, far_ss.at[k, j - 1], far_rs.at[k, j - 1], peers.at("far", there))
+
+    def near_copy(k, j):
+        there = lax.rem(peers.near + j, near)
+        span = block(base_n, each * 2 * f, k)
+        return send(span, span, near_ss.at[k, j - 1], near_rs.at[k, j - 1], peers.at("near", there))
+
+    def core_copy(k):
+        span = block(0, each * 2 * f * near, k)
+        return send(span, span, core_ss.at[k], core_rs.at[k], peers.at("core", 1 - peers.core))
+
+    greet(peers, axes)
+    for k in range(GROUPS):
+        x_copy(k).start()
+        own(k).start()
+    for s in range(GROUPS + 2):
+        k = s
+        if 0 <= k < GROUPS:
+            own(k).wait()
+            x_copy(k).wait_recv()
+            if far_inside:
+                for j in range(1, far):
+                    far_copy(k, j).start()
+        k = s - 1
+        if 0 <= k < GROUPS:
+            if far_inside:
+                for j in range(1, far):
+                    far_copy(k, j).wait_recv()
+            for j in range(1, near):
+                near_copy(k, j).start()
+        k = s - 2
+        if 0 <= k < GROUPS:
+            for j in range(1, near):
+                near_copy(k, j).wait_recv()
+            core_copy(k).start()
+    for k in range(GROUPS):
+        core_copy(k).wait_recv()
+    for k in range(GROUPS):
+        x_copy(k).wait_send()
+        if far_inside:
+            for j in range(1, far):
+                far_copy(k, j).wait_send()
+        for j in range(1, near):
+            near_copy(k, j).wait_send()
+        core_copy(k).wait_send()
+
+
+def gather(chunk, width):
+    each, hidden = chunk.shape
+    near, far = img_split(lax.axis_size("img"))
+    far_inside = width % (near * far * 2 * 16) == 0
+    fm = far - 1
+    DMA = pltpu.SemaphoreType.DMA
+    return pl.pallas_call(
+        functools.partial(gather_kernel, near, far, far_inside),
+        out_shape=jax.ShapeDtypeStruct((2, width, hidden), BF),
+        in_specs=[ANY],
+        out_specs=ANY,
+        scratch_shapes=[
+            DMA((GROUPS,)), DMA((GROUPS,)), DMA((GROUPS,)), DMA((GROUPS, fm)), DMA((GROUPS, fm)),
+            DMA((GROUPS, near - 1)), DMA((GROUPS, near - 1)), DMA((GROUPS,)), DMA((GROUPS,)),
+        ],
+        compiler_params=pltpu.CompilerParams(collective_id=1, has_side_effects=True),
+    )(chunk)
 
 
 def local(
@@ -75,38 +540,44 @@
         mixed = to_rows(mm("js,jd->sd", w2_all, hidden).astype(BF), x.shape)
         mid = wide + mixed.astype(F32) + b2[:, None]
         groups.append((x, mid, back, w1_all, w2_all, u_cols, preact, hidden))
-    rows_mid = jnp.concatenate([g[1].reshape(-1, width) for g in groups], axis=0)
-    row_mask = jnp.concatenate(
-        [jnp.repeat(mask_small, x_small.shape[1]), jnp.repeat(mask_large, x_large.shape[1])]
+    pad_small = -x_small.shape[1] % 64
+    small_rows = x_small.shape[0] * (x_small.shape[1] + pad_small)
+    large_rows = x_large.shape[0] * x_large.shape[1]
+    spare = -(small_rows + large_rows) % (3 * LANES)
+
+    def join(small, large):
+        small = jnp.pad(small, ((0, 0), (0, pad_small), (0, 0))).reshape(-1, width)
+        return jnp.concatenate([small, large.reshape(-1, width), jnp.zeros((spare, width), small.dtype)])
+
+    def part(joined):
+        small = joined[:small_rows].reshape(x_small.shape[0], -1, width)[:, : x_small.shape[1]]
+        return small, joined[small_rows : small_rows + large_rows].reshape(x_large.shape)
+
+    mask_small = mask_small[:, None, None]
+    mask_large = mask_large[:, None, None]
+    ec = join(cot_small * mask_small.astype(BF), cot_large * mask_large.astype(BF))
+    out, ey, chunk, small_grads = channel(
+        join(groups[0][1], groups[1][1]), ec, ch_w1, ch_w2, ch_b1, ln2_gain, ln2_bias, ch_b2
     )
-    split_at = x_small.shape[0] * x_small.shape[1]
-    normed_two, back_two = jax.vjp(norm_rows, rows_mid, ln2_gain, ln2_bias)
-    v = normed_two.astype(BF)
-    activation = mm("rd,dk->rk", v, ch_w1) + ch_b1
-    g = jax.nn.gelu(activation).astype(BF)
-    result = (rows_mid + mm("rk,kd->rd", g, ch_w2) + ch_b2) * row_mask[:, None]
-    out_small = result[:split_at].reshape(x_small.shape).astype(BF)
-    out_large = result[split_at:].reshape(x_large.shape).astype(BF)
-    e = (
-        jnp.concatenate([cot_small.reshape(-1, width), cot_large.reshape(-1, width)]).astype(F32)
-        * row_mask[:, None]
-    )
-    ec = e.astype(BF)
-    grad_ch_w2 = mm("rk,rd->kd", g, ec)
-    grad_ch_b2 = jnp.sum(ec.astype(F32), axis=0)
-    ea = gelu_back(activation, mm("rd,kd->rk", ec, ch_w2)).astype(BF)
-    grad_ch_w1 = mm("rd,rk->dk", v, ea)
-    grad_ch_b1 = jnp.sum(ea.astype(F32), axis=0)
-    rows_norm, grad_gain2, grad_bias2 = back_two(mm("rk,dk->rd", ea, ch_w1))
-    ey = e + rows_norm
+    out_small, out_large = part(out)
+    out_small = out_small * mask_small.astype(BF)
+    out_large = out_large * mask_large.astype(BF)
+    grad_ch_b1 = small_grads[:4].reshape(-1)
+    grad_ch_b2, grad_gain2, grad_bias2 = small_grads[4], small_grads[5], small_grads[6]
+    near, far = img_split(lax.axis_size("img"))
+    if width % (near * far * 2 * 16):
+        same = [[a * near + b for a in range(far)] for b in range(near)]
+        chunk = lax.psum(chunk.astype(F32), "img", axis_index_groups=same).astype(BF)
+    full = gather(chunk, width)
+    grad_ch_w1 = full[0].astype(F32)
+    grad_ch_w2 = full[1].T.astype(F32)
     grads = []
     gain1 = 0.0
     bias1 = 0.0
-    for (x, mid, back, w1_all, w2_all, u_cols, preact, hidden), part in zip(
-        groups, (ey[:split_at], ey[split_at:])
+    for (x, mid, back, w1_all, w2_all, u_cols, preact, hidden), part_ey in zip(
+        groups, part(ey)
     ):
-        part = part.reshape(x.shape)
-        et = part.astype(BF)
+        et = part_ey.astype(BF)
         grad_b2 = jnp.sum(et.astype(F32), axis=(0, 2))
         et_cols = to_columns(et)
         grad_w2 = mm("jd,sd->js", hidden, et_cols)
@@ -117,7 +588,7 @@
         norm_grad, gain_part, bias_part = back(eu.astype(F32))
         gain1 = gain1 + gain_part
         bias1 = bias1 + bias_part
-        grads.append((part + norm_grad, grad_w1, grad_b1, grad_w2, grad_b2))
+        grads.append((part_ey + norm_grad, grad_w1, grad_b1, grad_w2, grad_b2))
     scattered = [
         (
             lax.psum_scatter(grad_w1, "blk", scatter_dimension=0, tiled=True),
@@ -128,8 +599,6 @@
     (w1_s, w2_s), (w1_l, w2_l) = lax.psum(scattered, "img")
     b2_s, b2_l = lax.psum((grads[0][4], grads[1][4]), "img")
     both = ("img", "blk")
-    grad_ch_w1 = sum_low(grad_ch_w1, both)
-    grad_ch_w2 = sum_low(grad_ch_w2, both)
     gain1, bias1, b1_s, b1_l, grad_gain2, grad_bias2, grad_ch_b1, grad_ch_b2 = lax.psum(
         (gain1, bias1, grads[0][2], grads[1][2], grad_gain2, grad_bias2, grad_ch_b1, grad_ch_b2), both
     )

time: 532 us -> 598 us (1.12)
  Pallas kernels: 0 us -> 169 us
  matrix products: 95.8 us -> 19.2 us
  waiting for transfers between devices: 154 us -> 97.5 us
  local copies, waits for them, and re-layouts: 59.4 us -> 74 us
  blocking collectives: 115 us -> 126 us
    pallas_call x0 -> x2, Pallas kernels: none -> 169 us  [the longest x1 98.9 us: channel(): pl.pallas_call(functools.partial(channel_kernel, near, far, far_inside),...]
    dot_general x18 -> x12, matrix products: 95.8 us -> 19.2 us  [mm(): return jnp.einsum(spec, left, right, preferred_element_type=F32)]
    psum x1 -> x0, waiting for transfers between devices: 43.7 us -> none  [sum_low(): return lax.psum(values.astype(BF), axes).astype(F32)]
    all_gather x2, blocking collectives: 13.2 us -> 26.8 us  [local(): w2_all = lax.all_gather(w2, 'blk', axis=1, tiled=True)]
    unnamed x153 -> x156, local copies, waits for them, and re-layouts: 17.9 us -> 30.3 us
    all_to_all x4, waiting for transfers between devices: 12.1 us -> 0.01 us  [to_columns(): moved = lax.all_to_all(blocks, 'blk', 0, 0, tiled=True)]
    all_gather x2, blocking collectives: 26 us -> 14 us  [local(): w1_all = lax.all_gather(w1, 'blk', axis=0, tiled=True)]
    unnamed x1, blocking collectives: 11.5 us -> 19.2 us
  transfers between devices with their start and end apart: 14 -> 13, of which waited for: 7 -> 4; matrix products, arithmetic and copies ran while one was open for 26% -> 20% of each run, Pallas kernels for 0% -> 12%
where the time goes in v2:
time: 598 us; the launch traced here: 587 us
  Pallas kernels  169 us (28%)
  blocking collectives  126 us (21%)
  waiting for transfers between devices  97.5 us (16%)
  local copies, waits for them, and re-layouts  74 us (12%)
  other arithmetic  48 us (8%)
  starting transfers between devices  37.5 us (6%)
  matrix products  19.2 us (3%)
  between operations  16 us (3%)
    pallas_call x1, Pallas kernels, channel(): pl.pallas_call(functools.partial(channel_kernel, near, far, far_inside),...  98.9 us
    psum x1, waiting for transfers between devices, local(): (w1_s, w2_s), (w1_l, w2_l) = lax.psum(scattered, 'img')  70.7 us
    pallas_call x1, Pallas kernels, gather(): pl.pallas_call(functools.partial(gather_kernel, near, far, far_inside), o...  70 us
    psum x1, blocking collectives, local(): lax.psum((gain1, bias1, grads[0][2], grads[1][2], grad_gain2, grad_bias2,...  38.2 us
    unnamed x156, local copies, waits for them, and re-layouts  30.3 us
    psum x1, blocking collectives, local(): b2_s, b2_l = lax.psum((grads[0][4], grads[1][4]), 'img')  27.9 us
    all_gather x2, blocking collectives, local(): w2_all = lax.all_gather(w2, 'blk', axis=1, tiled=True)  26.8 us
    all_to_all x4, waiting for transfers between devices, to_rows(): moved = lax.all_to_all(blocks, 'blk', 0, 0, tiled=True)  26.7 us
  transfers between devices with their start and end apart: 13, of which 4 were waited for; matrix products, arithmetic and copies ran while one was open for 20% of the time, Pallas kernels for 12%

profile of v2, /device:TPU:0, one launch (start us, length us, event | category | flops | bytes accessed | tf_op | source)
XLA Modules:
  0.0 587.3 jit_solution(336900214166063575)
XLA Ops:
  13.3 4.3 all-to-all-start
  21.0 7.1 %all-gather = bf16[4,49,384]{2,1,0:T(8,128)(2,1)} all-gather(bf16[1,49,384]{2,1,0:T(8,128)(2,1)S(1)} %bitcast.198), channel_id=1, replica_groups=mesh['img'=8,'blk'=4] {'blk'}, dimensions={0}, use_global_device_ids=true | all-gather | bytes 188160 | tf_op jit(solution)/shard_map/all_gather | solution.py:535
  28.1 7.0 %all_gather.14 = bf16[576,384]{1,0:T(8,128)(2,1)S(1)} all-gather(bf16[144,384]{1,0:T(8,128)(2,1)S(1)} %copy-done.44), channel_id=1, replica_groups=mesh['img'=8,'blk'=4] {'blk'}, dimensions={0}, use_global_device_ids=true | all-gather | bytes 552960 | tf_op jit(solution)/shard_map/all_gather | solution.py:535
  42.0 3.7 all-to-all-start.2
  45.7 19.2 %all-gather.1 = bf16[4,49,384]{2,1,0:T(8,128)(2,1)S(1)} all-gather(bf16[1,49,384]{2,1,0:T(8,128)(2,1)S(1)} %bitcast.199), channel_id=1, replica_groups=mesh['img'=8,'blk'=4] {'blk'}, dimensions={0}, use_global_device_ids=true | all-gather | bytes 188160 | tf_op jit(solution)/shard_map/all_gather | solution.py:536
  71.2 7.6 %all_gather.15 = bf16[384,576]{0,1:T(8,128)(2,1)} all-gather(bf16[384,144]{0,1:T(8,128)(2,1)} %param.32), channel_id=1, replica_groups=mesh['img'=8,'blk'=4] {'blk'}, dimensions={1}, use_global_device_ids=true | all-gather | bytes 552960 | tf_op jit(solution)/shard_map/all_gather | solution.py:536
  88.4 4.1 all-to-all-start.1
  102.2 4.6 all-to-all-start.3
  110.3 14.0 %all-to-all-done.3 = bf16[36,144,128]{2,1,0:T(8,128)(2,1)} async-done(((bf16[36,144,128]{2,1,0:T(8,128)(2,1)}), bf16[36,144,128]{2,1,0:T(8,128)(2,1)}, u32[]{:S(2)}, u32[]{:S(2)}) %all-to-all-start.3) | async-done | bytes 1327136 | tf_op jit(solution)/shard_map/all_to_all | solution.py:45
  128.1 98.9 %shard_map.356 = (bf16[1152,768]{1,0:T(8,128)(2,1)}, f32[1152,768]{1,0:T(8,128)}, bf16[48,3072]{1,0:T(8,128)(2,1)}, f32[8,768]{1,0:T(8,128)}) custom-call(f32[1152,768]{1,0:T(8,128)} %maximum_maximum_fusion.y_hbm, bf16[1152,768]{1,0:T(8,128)(2,1)} %maximum_maximum_fusion.1.ec_hbm, bf16[768,3072]{1,0:T(8,128)(2,1)} %w1_hbm.1, bf16[3072,768]{1,0:T(8,128)(2,1)} %w2_hbm.1, ...), custom_call_target="tpu_custom_call" | custom-call | tf_op jit(solution)/shard_map/pallas_call | solution.py:390
  253.4 70.0 %shard_map.357 = bf16[2,768,3072]{2,1,0:T(8,128)(2,1)} custom-call(bf16[48,3072]{1,0:T(8,128)(2,1)} %get-tuple-element.27.chunk_hbm), custom_call_target="tpu_custom_call" | custom-call | tf_op jit(solution)/shard_map/pallas_call | solution.py:506
  323.5 12.8 %convert_bitcast_fusion = (f32[3072,768]{0,1:T(8,128)}, f32[768,3072]{1,0:T(8,128)}) fusion(bf16[2,768,3072]{2,1,0:T(8,128)(2,1)} %shard_map.357), kind=kLoop, calls=%fused_computation | loop fusion | flops 4718592 | bytes 28311552 | tf_op jit(solution)/shard_map/convert_element_type | solution.py:573
  336.3 9.6 %copy.108 = f32[3072,768]{1,0:T(8,128)} copy(f32[3072,768]{0,1:T(8,128)} %get-tuple-element.137) | data formatting | bytes 18874368
  345.9 27.9 %all-reduce.7 = (f32[49]{0:T(128)}, f32[144]{0:T(256)}) all-reduce(f32[49]{0:T(128)S(1)} %get-tuple-element.135, f32[144]{0:T(256)S(1)} %reduce_sum.218), channel_id=1, replica_groups=mesh['img'=8,'blk'=4] {'img'}, use_global_device_ids=true, to_apply=%region_23.24 | all-reduce | flops 193 | bytes 1544 | tf_op jit(solution)/shard_map/psum | solution.py:600
  374.8 3.5 all-to-all-start.6
  383.0 19.2 %fusion.62 = (f32[64,384]{1,0:T(8,128)S(1)}, f32[384,64]{0,1:T(8,128)S(1)}) fusion(f32[196,384]{1,0:T(8,128)} %fusion.64, f32[384,196]{0,1:T(8,128)S(1)} %fusion.65), kind=kCustom, calls=%all-reduce-scatter.2 | all-reduce-scatter fusion | flops 196609 | bytes 799232
  404.6 3.6 collective-permute-start
  421.9 4.2 all-to-all-done.5
  430.7 3.8 reshape.302
  437.6 3.7 all-to-all-start.7
  443.1 4.1 fusion.25
  450.2 8.5 %all-to-all-done.7 = bf16[36,144,128]{2,1,0:T(8,128)(2,1)S(1)} async-done(((bf16[36,144,128]{2,1,0:T(8,128)(2,1)}), bf16[36,144,128]{2,1,0:T(8,128)(2,1)S(1)}, u32[]{:S(2)}, u32[]{:S(2)}) %all-to-all-start.7) | async-done | bytes 1327136 | tf_op jit(solution)/shard_map/all_to_all | solution.py:45
  461.6 38.2 %all-reduce.6 = (f32[768]{0:T(1024)}, f32[768]{0:T(1024)}, f32[384]{0:T(512)}, f32[384]{0:T(512)}, f32[768]{0:T(1024)}, /*index=5*/f32[768]{0:T(1024)}, f32[3072]{0:T(1024)}, f32[768]{0:T(1024)}) all-reduce(f32[768]{0:T(1024)S(1)} %add.185, f32[768]{0:T(1024)S(1)} %add_bitcast_fusion, ...), channel_id=1, replica_groups=mesh['img'=8,'blk'=4] {'img','blk'}, use_global_device_ids=true, to_apply=%region_10.11 | all-reduce | flops 7680 | bytes 61440 | tf_op jit(solution)/shard_map/psum | solution.py:602
  503.3 70.7 %all-reduce.12.cloned.1.call-done = (f32[49,384]{1,0:T(8,128)}, f32[384,49]{0,1:T(8,128)}, f32[144,384]{1,0:T(8,128)}, f32[384,144]{0,1:T(8,128)}) async-done(((f32[49,384]{1,0:T(8,128)}, f32[384,49]{0,1:T(8,128)}, f32[144,384]{1,0:T(8,128)}, f32[384,144]{0,1:T(8,128)}), (f32[49,384]{1,0:T(8,128)}, f32[384,49]{0,1:T(8,128)}, f32[144,384]{1,0:T(8,128)}, f32[384,144]{0,1:T(8,128)})) %all-reduce.12.cloned.1.call-update) | async-done | bytes 592912 | tf_op jit(solution)/shard_map/psum | solution.py:599
  (269 shorter events, 120.7 us)
Async XLA Ops:
  13.3 28.7 %all-to-all-start = ((bf16[24,49,128]{2,1,0:T(8,128)(2,1)}), bf16[24,49,128]{2,1,0:T(8,128)(2,1)}, u32[]{:S(2)}, u32[]{:S(2)}) async-start(bf16[24,49,128]{2,1,0:T(8,128)(2,1)} %bitcast.1), calls=%async_computation | async-start | bytes 688128 | tf_op jit(solution)/shard_map/all_to_all | solution.py:33
  17.6 17.5 %copy-start.38 = (f32[768]{0:T(1024)S(1)}, f32[768]{0:T(1024)}, u32[]{:S(2)}) copy-start(f32[768]{0:T(1024)} %param.24) | copy-start | bytes 9220
  17.6 17.5 %copy-start.50 = (f32[768]{0:T(1024)S(1)}, f32[768]{0:T(1024)}, u32[]{:S(2)}) copy-start(f32[768]{0:T(1024)} %param.25) | copy-start | bytes 9220
  18.9 22.1 %copy-start.58 = (bf16[4]{0:T(256)(128)(2,1)}, bf16[4]{0:T(256)(128)(2,1)S(1)}, u32[]{:S(2)}) copy-start(bf16[4]{0:T(256)(128)(2,1)S(1)} %fusion.59) | copy-start | bytes 28
  35.1 58.0 %copy-start.14 = (bf16[576,384]{1,0:T(8,128)(2,1)}, bf16[576,384]{1,0:T(8,128)(2,1)S(1)}, u32[]{:S(2)}) copy-start(bf16[576,384]{1,0:T(8,128)(2,1)S(1)} %all_gather.14) | copy-start | bytes 1327108
  41.0 23.8 %copy-start.54 = (f32[768]{0:T(1024)S(1)}, f32[768]{0:T(1024)}, u32[]{:S(2)}) copy-start(f32[768]{0:T(1024)} %param.34) | copy-start | bytes 9220
  41.0 24.4 %copy-start.55 = (f32[768]{0:T(1024)S(1)}, f32[768]{0:T(1024)}, u32[]{:S(2)}) copy-start(f32[768]{0:T(1024)} %param.35) | copy-start | bytes 9220
  41.0 25.0 %copy-start.56 = (f32[768]{0:T(1024)S(1)}, f32[768]{0:T(1024)}, u32[]{:S(2)}) copy-start(f32[768]{0:T(1024)} %param.39) | copy-start | bytes 9220
  41.1 25.5 %copy-start.26 = (bf16[4,49,384]{2,1,0:T(8,128)(2,1)S(1)}, bf16[4,49,384]{2,1,0:T(8,128)(2,1)}, u32[]{:S(2)}) copy-start(bf16[4,49,384]{2,1,0:T(8,128)(2,1)} %all-gather) | copy-start | bytes 451588
  42.0 27.0 %copy-start.62 = (u32[32]{0:T(128)S(1)}, u32[32]{0:T(128)}, u32[]{:S(2)}) copy-start(u32[32]{0:T(128)} %constant.57) | copy-start | bytes 388
  42.0 46.5 %all-to-all-start.2 = ((bf16[36,144,128]{2,1,0:T(8,128)(2,1)}), bf16[36,144,128]{2,1,0:T(8,128)(2,1)S(1)}, u32[]{:S(2)}, u32[]{:S(2)}) async-start(bf16[36,144,128]{2,1,0:T(8,128)(2,1)} %bitcast.172), calls=%async_computation.2 | async-start | bytes 2654208 | tf_op jit(solution)/shard_map/all_to_all | solution.py:33
  88.4 13.7 %all-to-all-start.1 = ((bf16[24,49,128]{2,1,0:T(8,128)(2,1)}), bf16[24,49,128]{2,1,0:T(8,128)(2,1)}, u32[]{:S(2)}, u32[]{:S(2)}) async-start(bf16[24,49,128]{2,1,0:T(8,128)(2,1)} %bitcast.193), calls=%async_computation.1 | async-start | bytes 688128 | tf_op jit(solution)/shard_map/all_to_all | solution.py:45
  102.2 22.1 %all-to-all-start.3 = ((bf16[36,144,128]{2,1,0:T(8,128)(2,1)}), bf16[36,144,128]{2,1,0:T(8,128)(2,1)}, u32[]{:S(2)}, u32[]{:S(2)}) async-start(bf16[36,144,128]{2,1,0:T(8,128)(2,1)} %bitcast.21), calls=%async_computation.3 | async-start | bytes 2654208 | tf_op jit(solution)/shard_map/all_to_all | solution.py:45
  244.7 130.1 %all-to-all-start.4 = ((bf16[24,49,128]{2,1,0:T(8,128)(2,1)}), bf16[24,49,128]{2,1,0:T(8,128)(2,1)S(1)}, u32[]{:S(2)}, u32[]{:S(2)}) async-start(bf16[24,49,128]{2,1,0:T(8,128)(2,1)} %bitcast.192), calls=%async_computation.4 | async-start | bytes 688128 | tf_op jit(solution)/shard_map/all_to_all | solution.py:33
  336.3 37.6 %copy-start.16 = (bf16[4,49,768]{2,1,0:T(8,128)(2,1)S(1)}, bf16[4,49,768]{2,1,0:T(8,128)(2,1)}, u32[]{:S(2)}) copy-start(bf16[4,49,768]{2,1,0:T(8,128)(2,1)} %slice.56) | copy-start | bytes 903172
  336.3 37.6 %copy-start.59 = (bf16[4]{0:T(256)(128)(2,1)S(1)}, bf16[4]{0:T(256)(128)(2,1)}, u32[]{:S(2)}) copy-start(bf16[4]{0:T(256)(128)(2,1)} %copy-done.58) | copy-start | bytes 28
  374.8 33.5 %all-to-all-start.6 = ((bf16[36,144,128]{2,1,0:T(8,128)(2,1)}), bf16[36,144,128]{2,1,0:T(8,128)(2,1)S(1)}, u32[]{:S(2)}, u32[]{:S(2)}) async-start(bf16[36,144,128]{2,1,0:T(8,128)(2,1)} %bitcast.171), calls=%async_computation.6 | async-start | bytes 2654208 | tf_op jit(solution)/shard_map/all_to_all | solution.py:33
  378.4 121.5 %reduce-scatter.7.cloned.1.call-start = ((), (), s32[]{:S(2)}) async-start(), calls=%async_computation.10 | async-start | bytes 1105920 | tf_op jit(solution)/shard_map/reduce_scatter | solution.py:594
  402.3 16.9 %collective-permute-start.1 = (f32[384,45]{0,1:T(8,128)S(1)}, f32[384,45]{0,1:T(8,128)}, u32[]{:S(2)}, u32[]{:S(2)}) collective-permute-start(f32[384,45]{0,1:T(8,128)S(1)} %slice.59), channel_id=1, source_target_pairs={{0,1},{1,2},{2,3},{4,5},{5,6},{6,7},{8,9},{9,10},{10,11},{12,13},{... | collective-permute-start | bytes 207368
  404.6 15.7 %collective-permute-start = (f32[45,384]{1,0:T(8,128)S(1)}, f32[45,384]{1,0:T(8,128)S(1)}, u32[]{:S(2)}, u32[]{:S(2)}) collective-permute-start(f32[45,384]{1,0:T(8,128)S(1)} %slice.58), channel_id=1, source_target_pairs={{0,1},{1,2},{2,3},{4,5},{5,6},{6,7},{8,9},{9,10},{10,11},{12,13},{... | collective-permute-start | bytes 207368
  415.7 10.3 %all-to-all-start.5 = ((bf16[24,49,128]{2,1,0:T(8,128)(2,1)}), bf16[24,49,128]{2,1,0:T(8,128)(2,1)S(1)}, u32[]{:S(2)}, u32[]{:S(2)}) async-start(bf16[24,49,128]{2,1,0:T(8,128)(2,1)} %bitcast.40), calls=%async_computation.5 | async-start | bytes 688128 | tf_op jit(solution)/shard_map/all_to_all | solution.py:45
  437.6 21.1 %all-to-all-start.7 = ((bf16[36,144,128]{2,1,0:T(8,128)(2,1)}), bf16[36,144,128]{2,1,0:T(8,128)(2,1)S(1)}, u32[]{:S(2)}, u32[]{:S(2)}) async-start(bf16[36,144,128]{2,1,0:T(8,128)(2,1)} %bitcast.169), calls=%async_computation.7 | async-start | bytes 2654208 | tf_op jit(solution)/shard_map/all_to_all | solution.py:45
  441.3 58.5 %reduce-scatter.9.cloned.1.call-start = ((), (), s32[]{:S(2)}) async-start(), calls=%async_computation.11 | async-start | bytes 1105920 | tf_op jit(solution)/shard_map/reduce_scatter | solution.py:595
  447.3 126.7 %all-reduce.12.cloned.1.call-start = ((), (), s32[]{:S(2)}) async-start(), calls=%async_computation.12 | async-start | bytes 1228800 | tf_op jit(solution)/shard_map/psum | solution.py:599
  (57 other events, 226.5 us)
Sparse Core Ops, SparseCore 0:
  414.2 19.7 reduce-scatter.6
  447.4 22.0 reduce-scatter.8
  500.0 74.0 all-reduce.11

commit v3 on v2

--- a/solution.py
+++ b/solution.py
@@ -11,44 +11,6 @@
 LANES = 128
 BF = jnp.bfloat16
 F32 = jnp.float32
-
-
-def norm_rows(values, scales, shifts):
-    row_mean = jnp.mean(values, axis=-1, keepdims=True)
-    centered = values - row_mean
-    row_var = jnp.mean(centered * centered, axis=-1, keepdims=True)
-    return centered * lax.rsqrt(row_var + EPSILON) * scales + shifts
-
-
-def gelu_back(preact, upstream):
-    unused, pullback = jax.vjp(jax.nn.gelu, preact)
-    return pullback(upstream)[0]
-
-
-def to_columns(rows):
-    count, patches, width = rows.shape
-    blocks = rows.reshape(count, patches, width // LANES, LANES).transpose(0, 2, 1, 3)
-    blocks = blocks.reshape(count * (width // LANES), patches, LANES)
-    size = lax.axis_size("blk")
-    moved = lax.all_to_all(blocks, "blk", 0, 0, tiled=True)
-    share = moved.shape[0] // size
-    moved = moved.reshape(size, share, patches, LANES).transpose(0, 2, 1, 3)
-    return moved.reshape(size * patches, share * LANES)
-
-
-def to_rows(columns, shape):
-    count, patches, width = shape
-    size = lax.axis_size("blk")
-    share = columns.shape[1] // LANES
-    blocks = columns.reshape(size, patches, share, LANES).transpose(0, 2, 1, 3)
-    blocks = blocks.reshape(size * share, patches, LANES)
-    moved = lax.all_to_all(blocks, "blk", 0, 0, tiled=True)
-    moved = moved.reshape(count, width // LANES, patches, LANES).transpose(0, 2, 1, 3)
-    return moved.reshape(shape)
-
-
-def mm(spec, left, right):
-    return jnp.einsum(spec, left, right, preferred_element_type=F32)
 
 
 MESH = pl.DeviceIdType.MESH
@@ -191,7 +153,7 @@
         slot = lax.rem(t, 2)
         return send(x_tx.at[slot], x_rx.at[t], x_ss.at[slot], x_rs.at[t], peers.at("x", 1 - peers.x))
 
-    step_rows = rows // 3
+    step_rows = rows
 
     def tile_step(t):
         for copy in w_copies(t):
@@ -419,101 +381,655 @@
     )(y, ec, w1, w2, b1.reshape(1, -1), gain.reshape(1, -1), bias.reshape(1, -1), b2.reshape(1, -1))
 
 
+NT = (((1,), (1,)), ((), ()))
+
+
+def matmul(left, right):
+    return jnp.dot(left, right, preferred_element_type=F32)
+
+
+def matmul_nt(left, right):
+    return lax.dot_general(left, right, NT, preferred_element_type=F32)
+
+
+class Swap:
+    def __init__(self, peers, size, per_l, per_s, patches_l, patches_s):
+        self.peers, self.size = peers, size
+        self.per_l, self.per_s = per_l, per_s
+        self.pl, self.ps = patches_l, patches_s
+
+    def other(self, step):
+        return lax.rem(self.peers.blk + step, self.size)
+
+    def copy(self, src, dst, ss, rs, place):
+        return pltpu.make_async_remote_copy(
+            src_ref=src, dst_ref=dst, send_sem=ss, recv_sem=rs,
+            device_id=(self.peers.img, place), device_id_type=MESH,
+        )
+
+    def rows(self, place, patches):
+        return pl.ds(pl.multiple_of(place * patches, patches), patches)
+
+    def out(self, kind, j, place, source, tx, cols, ss, rs):
+        per, patches = (self.per_l, self.pl) if kind == "l" else (self.per_s, self.ps)
+        unit = place * per + j
+        return self.copy(
+            tx.at[unit], cols.at[j, self.rows(source, patches)], ss.at[unit], rs.at[j, source], place
+        )
+
+    def back(self, kind, j, owner, place, cols, rx, ss, rs):
+        per, patches = (self.per_l, self.pl) if kind == "l" else (self.per_s, self.ps)
+        unit = owner * per + j
+        return self.copy(
+            cols.at[j, self.rows(place, patches)], rx.at[unit], ss.at[j, place], rs.at[unit], place
+        )
+
+
+def greet_all(peers, size, near, far):
+    barrier = pltpu.get_barrier_semaphore()
+    total = 0
+    for j in range(1, size):
+        there = lax.rem(peers.blk + j, size)
+        pl.semaphore_signal(barrier, inc=1, device_id=(peers.img, there), device_id_type=MESH)
+        total += 1
+    for axis, count in (("near", near), ("far", far)):
+        for j in range(1, count):
+            there = lax.rem(peers.mine(axis) + j, count)
+            pl.semaphore_signal(barrier, inc=1, device_id=peers.at(axis, there), device_id_type=MESH)
+            total += 1
+    pl.semaphore_wait(barrier, total)
+
+
+def unit_rows(row):
+    mean = jnp.mean(row, axis=-1, keepdims=True)
+    centered = row - mean
+    var = jnp.mean(centered * centered, axis=-1, keepdims=True)
+    scale = lax.rsqrt(var + EPSILON)
+    return centered * scale, scale
+
+
+def token_kernel(
+    near, size,
+    xl, xs, wq_l, wq_s, b1_l, b1_s, b2_l, b2_s, gain_ref, bias_ref,
+    y_hbm, u_l, u_s, h_l, h_s, sl_l, sl_s, w_l, w_s,
+    tx_l, tx_s, w1t_l, w1t_s, m_l, m_s, rx_l, rx_s, y,
+    y_sem, own_sem, wown, w_ss, w_rs, out_ss_l, out_ss_s, out_rs_l, out_rs_s, bk_ss_l, bk_ss_s, bk_rs_l, bk_rs_s,
+):
+    peers = Peers(near)
+    me = peers.blk
+    count_l, patches_l, width = xl.shape
+    count_s, patches_s, _ = xs.shape
+    half = width // 2
+    per_l, per_s = count_l * 2 // size, count_s // size
+    swap = Swap(peers, size, per_l, per_s, patches_l, patches_s)
+
+    barrier = pltpu.get_barrier_semaphore()
+    for j in range(1, size):
+        pl.semaphore_signal(barrier, inc=1, device_id=(peers.img, swap.other(j)), device_id_type=MESH)
+    pl.semaphore_wait(barrier, size - 1)
+
+    def weights(src_l, src_s, quarter, n, place):
+        return (
+            swap.copy(src_l, w_l.at[:, swap.rows(quarter, patches_l)], w_ss.at[n, 0], w_rs.at[n, 0], place),
+            swap.copy(src_s, w_s.at[:, swap.rows(quarter, patches_s)], w_ss.at[n, 1], w_rs.at[n, 1], place),
+        )
+
+    x_peer = (1 - peers.x) * 2 + peers.core
+    core_peer = peers.x * 2 + 1 - peers.core
+    to_x = weights(wq_l, wq_s, me, 0, x_peer)
+    to_core = weights(wq_l, wq_s, me, 1, core_peer)
+    relay = weights(
+        w_l.at[:, swap.rows(x_peer, patches_l)], w_s.at[:, swap.rows(x_peer, patches_s)], x_peer, 2, core_peer
+    )
+    for copy in to_x + to_core:
+        copy.start()
+    own_w = (
+        pltpu.make_async_copy(wq_l, w_l.at[:, swap.rows(me, patches_l)], wown.at[0]),
+        pltpu.make_async_copy(wq_s, w_s.at[:, swap.rows(me, patches_s)], wown.at[1]),
+    )
+    for copy in own_w:
+        copy.start()
+
+    def norm(row):
+        unit, _ = unit_rows(row.astype(F32))
+        return (unit * gain_ref[...] + bias_ref[...]).astype(BF)
+
+    def norm_l(n, carry):
+        u = norm(xl[n])
+        tx_l[2 * n] = u[:, :half]
+        tx_l[2 * n + 1] = u[:, half:]
+        return carry
+
+    def norm_s(n, carry):
+        tx_s[n] = norm(xs[n])
+        return carry
+
+    lax.fori_loop(0, count_l, norm_l, 0)
+    for j in range(per_l):
+        for k in range(1, size):
+            swap.out("l", j, swap.other(k), me, tx_l, u_l, out_ss_l, out_rs_l).start()
+    lax.fori_loop(0, count_s, norm_s, 0)
+    for j in range(per_s):
+        for k in range(1, size):
+            swap.out("s", j, swap.other(k), me, tx_s, u_s, out_ss_s, out_rs_s).start()
+    for j in range(per_l):
+        u_l[j, swap.rows(me, patches_l)] = tx_l[me * per_l + j]
+    for j in range(per_s):
+        u_s[j, swap.rows(me, patches_s)] = tx_s[me * per_s + j]
+
+    for copy in to_x:
+        copy.wait_recv()
+    for copy in relay:
+        copy.start()
+    for copy in own_w:
+        copy.wait()
+    for copy in to_core + relay:
+        copy.wait_recv()
+    w1t_l[...] = w_l[0].T
+    w1t_s[...] = w_s[0].T
+
+    def mix(kind, j, cols, w1t, w2t, b1, h, slope, m, outs, tx, rx, bss, brs):
+        for k in range(1, size):
+            source = swap.other(k)
+            swap.out(kind, j, me, source, tx, cols, *outs).wait_recv()
+        g, d = gelu_pair(matmul(w1t[...], cols[j]) + b1[...])
+        low = g.astype(BF)
+        h[j] = low
+        slope[j] = d.astype(BF)
+        m[j] = matmul(w2t, low).astype(BF)
+        for k in range(1, size):
+            swap.back(kind, j, me, swap.other(k), m, rx, bss, brs).start()
+        patches, per = (patches_l, per_l) if kind == "l" else (patches_s, per_s)
+        rx[me * per + j] = m[j, swap.rows(me, patches)]
+
+    for j in range(per_l):
+        mix("l", j, u_l, w1t_l, w_l[1], b1_l, h_l, sl_l, m_l, (out_ss_l, out_rs_l), tx_l, rx_l, bk_ss_l, bk_rs_l)
+    for j in range(per_s):
+        mix("s", j, u_s, w1t_s, w_s[1], b1_s, h_s, sl_s, m_s, (out_ss_s, out_rs_s), tx_s, rx_s, bk_ss_s, bk_rs_s)
+
+    small_rows = count_s * patches_s
+    rows = y.shape[0]
+    used = small_rows + count_l * patches_l
+    if rows > used:
+        y[used:rows, :] = jnp.zeros((rows - used, width), F32)
+
+    def arrived(kind, unit, m, rx, bss, brs):
+        per = per_l if kind == "l" else per_s
+        owner = unit // per
+
+        @pl.when(owner != me)
+        def _():
+            swap.back(kind, unit - owner * per, owner, me, m, rx, bss, brs).wait_recv()
+
+    def home_l(n, carry):
+        arrived("l", 2 * n, m_l, rx_l, bk_ss_l, bk_rs_l)
+        arrived("l", 2 * n + 1, m_l, rx_l, bk_ss_l, bk_rs_l)
+        at = pl.ds(pl.multiple_of(small_rows + n * patches_l, 16), patches_l)
+        y[at, :half] = xl[n, :, :half].astype(F32) + rx_l[2 * n].astype(F32) + b2_l[...]
+        y[at, half:] = xl[n, :, half:].astype(F32) + rx_l[2 * n + 1].astype(F32) + b2_l[...]
+        return carry
+
+    def home_s(n, carry):
+        arrived("s", n, m_s, rx_s, bk_ss_s, bk_rs_s)
+        at = pl.ds(pl.multiple_of(n * patches_s, 16), patches_s)
+        y[at, :] = xs[n].astype(F32) + rx_s[n].astype(F32) + b2_s[...]
+        return carry
+
+    lax.fori_loop(0, count_l, home_l, 0)
+    lax.fori_loop(0, count_s, home_s, 0)
+    y_out = pltpu.make_async_copy(y, y_hbm, y_sem.at[0])
+    y_out.start()
+    for copy in to_x + to_core + relay:
+        copy.wait_send()
+    for k in range(1, size):
+        there = swap.other(k)
+        for j in range(per_l):
+            swap.out("l", j, there, me, tx_l, u_l, out_ss_l, out_rs_l).wait_send()
+            swap.back("l", j, me, there, m_l, rx_l, bk_ss_l, bk_rs_l).wait_send()
+        for j in range(per_s):
+            swap.out("s", j, there, me, tx_s, u_s, out_ss_s, out_rs_s).wait_send()
+            swap.back("s", j, me, there, m_s, rx_s, bk_ss_s, bk_rs_s).wait_send()
+    y_out.wait()
+
+
+def token_forward(xl, xs, wq_l, wq_s, b1_l, b1_s, b2_l, b2_s, gain, bias, rows):
+    size = lax.axis_size("blk")
+    near, far = img_split(lax.axis_size("img"))
+    count_l, patches_l, width = xl.shape
+    count_s, patches_s, _ = xs.shape
+    token = wq_l.shape[2]
+    half = width // 2
+    per_l, per_s = count_l * 2 // size, count_s // size
+    vmem = pl.BlockSpec(memory_space=pltpu.VMEM)
+    V = pltpu.VMEM
+    DMA = pltpu.SemaphoreType.DMA
+    low = lambda *shape: jax.ShapeDtypeStruct(shape, BF)
+    return pl.pallas_call(
+        functools.partial(token_kernel, near, size),
+        out_shape=(
+            jax.ShapeDtypeStruct((rows, width), F32),
+            low(per_l, size * patches_l, half), low(per_s, size * patches_s, width),
+            low(per_l, token, half), low(per_s, token, width),
+            low(per_l, token, half), low(per_s, token, width),
+            low(2, size * patches_l, token), low(2, size * patches_s, token),
+        ),
+        in_specs=[vmem] * 10,
+        out_specs=(ANY,) + (vmem,) * 8,
+        scratch_shapes=[
+            V((count_l * 2, patches_l, half), BF), V((count_s, patches_s, width), BF),
+            V((token, size * patches_l), BF), V((token, size * patches_s), BF),
+            V((per_l, size * patches_l, half), BF), V((per_s, size * patches_s, width), BF),
+            V((count_l * 2, patches_l, half), BF), V((count_s, patches_s, width), BF),
+            V((rows, width), F32),
+            DMA((1,)), DMA((1,)), DMA((2,)), DMA((3, 2)), DMA((3, 2)),
+            DMA((count_l * 2,)), DMA((count_s,)), DMA((per_l, size)), DMA((per_s, size)),
+            DMA((per_l, size)), DMA((per_s, size)), DMA((count_l * 2,)), DMA((count_s,)),
+        ],
+        compiler_params=pltpu.CompilerParams(
+            collective_id=2, has_side_effects=True, vmem_limit_bytes=TOP
+        ),
+    )(
+        xl, xs, wq_l, wq_s, b1_l.reshape(-1, 1), b1_s.reshape(-1, 1), b2_l.reshape(-1, 1), b2_s.reshape(-1, 1),
+        gain.reshape(1, -1), bias.reshape(1, -1),
+    )
+
+
 GROUPS = 6
-
-
-def gather_kernel(near, far, far_inside, chunk_hbm, full_hbm, own_sem, x_ss, x_rs, far_ss, far_rs, near_ss, near_rs, core_ss, core_rs):
-    each, hidden = chunk_hbm.shape
+SLAB = 512
+
+
+def backward_kernel(
+    near, far, size, far_inside,
+    chunk_hbm, ey_hbm, xl, xs, u_l, u_s, h_l, h_s, sl_l, sl_s, w_l, w_s, small_in, gain_ref,
+    full_hbm, gx_hbm, tok_out, vec_out,
+    ey, tx_l, tx_s, e_l, e_s, w2_l, w2_s, ep_l, ep_s, eu_l, eu_s, rx_l, rx_s,
+    grads, tok_tx, tok_rx, tokx_tx, tokx_rx, tok_sum, tokn_tx, tokn_rx, tok_half, tokf_tx, tokf_rx,
+    vec, vec_rx, vecn_rx, vecf_rx,
+    ey_sem, gx_sem,
+    own_sem, gx_ss, gx_rs, gf_ss, gf_rs, gn_ss, gn_rs, gc_ss, gc_rs,
+    out_ss_l, out_ss_s, out_rs_l, out_rs_s, bk_ss_l, bk_ss_s, bk_rs_l, bk_rs_s,
+    tc_ss, tc_rs, tx_ss, tx_rs, tn_ss, tn_rs, tf_ss, tf_rs, taf_ss, taf_rs, tan_ss, tan_rs,
+    v_ss, v_rs, vn_ss, vn_rs, vf_ss, vf_rs,
+):
     peers = Peers(near)
-    f = far if far_inside else 1
-    f_place = peers.far if far_inside else 0
-    cols = hidden // GROUPS
-    axes = [("core", 2), ("near", near)] + ([("far", far)] if far_inside else []) + [("x", 2)]
-    base_n = peers.near * (each * 2 * f)
-    base_f = base_n + f_place * (each * 2)
-    base_x = base_f + peers.x * each
-
-    def block(start, size, k):
-        return full_hbm.at[peers.core, pl.ds(pl.multiple_of(start, each), size), pl.ds(k * cols, cols)]
+    me = peers.blk
+    count_l, patches_l, width = xl.shape
+    count_s, patches_s, _ = xs.shape
+    token = w_l.shape[2]
+    half = width // 2
+    per_l, per_s = count_l * 2 // size, count_s // size
+    swap = Swap(peers, size, per_l, per_s, patches_l, patches_s)
+    small_rows = count_s * patches_s
+    x_peer = peers.at("x", 1 - peers.x)
+    core_peer = peers.at("core", 1 - peers.core)
 
     def send(src, dst, ss, rs, device):
         return pltpu.make_async_remote_copy(
             src_ref=src, dst_ref=dst, send_sem=ss, recv_sem=rs, device_id=device, device_id_type=MESH
         )
 
-    def own(k):
+    def others(axis, count):
+        return [(j, peers.at(axis, lax.rem(peers.mine(axis) + j, count))) for j in range(1, count)]
+
+    near_peers = others("near", near)
+    far_peers = others("far", far)
+
+    each, hidden = chunk_hbm.shape
+    f = far if far_inside else 1
+    f_place = peers.far if far_inside else 0
+    cols = hidden // GROUPS
+    base_n = peers.near * (each * 2 * f)
+    base_f = base_n + f_place * (each * 2)
+    base_x = base_f + peers.x * each
+
+    def block(start, rows, k):
+        return full_hbm.at[peers.core, pl.ds(pl.multiple_of(start, each), rows), pl.ds(k * cols, cols)]
+
+    def g_own(k):
         return pltpu.make_async_copy(chunk_hbm.at[:, pl.ds(k * cols, cols)], block(base_x, each, k), own_sem.at[k])
 
-    def x_copy(k):
-        return send(chunk_hbm.at[:, pl.ds(k * cols, cols)], block(base_x, each, k), x_ss.at[k], x_rs.at[k], peers.at("x", 1 - peers.x))
-
-    def far_copy(k, j):
-        there = lax.rem(peers.far + j, far)
+    def g_x(k):
+        return send(chunk_hbm.at[:, pl.ds(k * cols, cols)], block(base_x, each, k), gx_ss.at[k], gx_rs.at[k], x_peer)
+
+    def g_far(k):
         span = block(base_f, each * 2, k)
-        return send(span, span, far_ss.at[k, j - 1], far_rs.at[k, j - 1], peers.at("far", there))
-
-    def near_copy(k, j):
-        there = lax.rem(peers.near + j, near)
+        return [
+            send(span, span, gf_ss.at[k, j - 1], gf_rs.at[k, j - 1], there) for j, there in far_peers
+        ] if far_inside else []
+
+    def g_near(k):
         span = block(base_n, each * 2 * f, k)
-        return send(span, span, near_ss.at[k, j - 1], near_rs.at[k, j - 1], peers.at("near", there))
-
-    def core_copy(k):
+        return [send(span, span, gn_ss.at[k, j - 1], gn_rs.at[k, j - 1], there) for j, there in near_peers]
+
+    def g_core(k):
         span = block(0, each * 2 * f * near, k)
-        return send(span, span, core_ss.at[k], core_rs.at[k], peers.at("core", 1 - peers.core))
-
-    greet(peers, axes)
+        return send(span, span, gc_ss.at[k], gc_rs.at[k], core_peer)
+
+    def tick_near(k):
+        for copy in g_far(k):
+            copy.wait_recv()
+        for copy in g_near(k):
+            copy.start()
+
+    def tick_core(k):
+        for copy in g_near(k):
+            copy.wait_recv()
+        g_core(k).start()
+
+    ey_in = pltpu.make_async_copy(ey_hbm, ey, ey_sem.at[0])
+    ey_in.start()
+    greet_all(peers, size, near, far)
     for k in range(GROUPS):
-        x_copy(k).start()
-        own(k).start()
-    for s in range(GROUPS + 2):
-        k = s
-        if 0 <= k < GROUPS:
-            own(k).wait()
-            x_copy(k).wait_recv()
-            if far_inside:
-                for j in range(1, far):
-                    far_copy(k, j).start()
-        k = s - 1
-        if 0 <= k < GROUPS:
-            if far_inside:
-                for j in range(1, far):
-                    far_copy(k, j).wait_recv()
-            for j in range(1, near):
-                near_copy(k, j).start()
-        k = s - 2
-        if 0 <= k < GROUPS:
-            for j in range(1, near):
-                near_copy(k, j).wait_recv()
-            core_copy(k).start()
+        g_x(k).start()
+        g_own(k).start()
+    ey_in.wait()
+    vec[...] = jnp.zeros_like(vec)
+    vec[0:8, :] = small_in[...]
+    ones = jnp.ones((8, width), BF)
+
+    def cast_l(n, total):
+        at = pl.ds(pl.multiple_of(small_rows + n * patches_l, 16), patches_l)
+        et = ey[at, :].astype(BF)
+        tx_l[2 * n] = et[:, :half]
+        tx_l[2 * n + 1] = et[:, half:]
+        return total + matmul_nt(ones, et)
+
+    def cast_s(n, total):
+        at = pl.ds(pl.multiple_of(n * patches_s, 16), patches_s)
+        et = ey[at, :].astype(BF)
+        tx_s[n] = et
+        return total + matmul_nt(ones, et)
+
+    total_l = lax.fori_loop(0, count_l, cast_l, jnp.zeros((8, patches_l), F32))
+    for j in range(per_l):
+        for k in range(1, size):
+            swap.out("l", j, swap.other(k), me, tx_l, e_l, out_ss_l, out_rs_l).start()
+    total_s = lax.fori_loop(0, count_s, cast_s, jnp.zeros((8, patches_s), F32))
+    for j in range(per_s):
+        for k in range(1, size):
+            swap.out("s", j, swap.other(k), me, tx_s, e_s, out_ss_s, out_rs_s).start()
+    vec[16:24, 0:patches_l] = total_l
+    vec[16:24, half:half + patches_s] = total_s
+    for j in range(per_l):
+        e_l[j, swap.rows(me, patches_l)] = tx_l[me * per_l + j]
+    for j in range(per_s):
+        e_s[j, swap.rows(me, patches_s)] = tx_s[me * per_s + j]
+    w2_l[...] = w_l[1].T
+    w2_s[...] = w_s[1].T
     for k in range(GROUPS):
-        core_copy(k).wait_recv()
+        g_own(k).wait()
+        g_x(k).wait_recv()
+        for copy in g_far(k):
+            copy.start()
+        if not far_inside:
+            tick_near(k)
+
+    def unmix(kind, j, e, w2, w1, slope, ep, eu, outs, tx, rx, bss, brs):
+        for k in range(1, size):
+            swap.out(kind, j, me, swap.other(k), tx, e, *outs).wait_recv()
+        low = (matmul(w2[...], e[j]) * slope[j].astype(F32)).astype(BF)
+        ep[j] = low
+        eu[j] = matmul(w1, low).astype(BF)
+        for k in range(1, size):
+            swap.back(kind, j, me, swap.other(k), eu, rx, bss, brs).start()
+        patches, per = (patches_l, per_l) if kind == "l" else (patches_s, per_s)
+        rx[me * per + j] = eu[j, swap.rows(me, patches)]
+
+    for j in range(per_l):
+        unmix("l", j, e_l, w2_l, w_l[0], sl_l, ep_l, eu_l, (out_ss_l, out_rs_l), tx_l, rx_l, bk_ss_l, bk_rs_l)
+    for j in range(per_s):
+        unmix("s", j, e_s, w2_s, w_s[0], sl_s, ep_s, eu_s, (out_ss_s, out_rs_s), tx_s, rx_s, bk_ss_s, bk_rs_s)
+    if far_inside:
+        tick_near(0)
+
+    ones_l = jnp.ones((8, half), BF)
+    vec[8:16, 0:half] = sum(matmul_nt(ones_l, ep_l[j]) for j in range(per_l))
+    ones_s = jnp.ones((8, width), BF)
+    vec[8:16, half:width] = sum(matmul_nt(ones_s, ep_s[j]) for j in range(per_s))
+    top = 2 * patches_l + 2 * patches_s
+    if SLAB > top:
+        grads[:, top:SLAB, :] = jnp.zeros((size, SLAB - top, token), F32)
+    begin = 0
+    for left, right, per, patches in (
+        (u_l, ep_l, per_l, patches_l), (e_l, h_l, per_l, patches_l),
+        (u_s, ep_s, per_s, patches_s), (e_s, h_s, per_s, patches_s),
+    ):
+        value = sum(matmul_nt(left[j], right[j]) for j in range(per))
+        for q in range(size):
+            grads[q, begin:begin + patches] = value[q * patches:(q + 1) * patches]
+        begin += patches
+    for p in range(2):
+        tok_tx[p] = grads[p * 2 + 1 - peers.core].astype(BF)
+    t_core = send(tok_tx, tok_rx, tc_ss.at[0], tc_rs.at[0], core_peer)
+    t_core.start()
+    if far_inside:
+        tick_near(1)
+    t_core.wait_recv()
+    there = 1 - peers.x
+    tokx_tx[...] = (grads[there * 2 + peers.core] + tok_rx[there].astype(F32)).astype(BF)
+    t_x = send(tokx_tx, tokx_rx, tx_ss.at[0], tx_rs.at[0], x_peer)
+    t_x.start()
+    tok_sum[...] = grads[me] + tok_rx[peers.x].astype(F32)
+    tick_core(0)
+
+    def arrived(kind, unit, eu, rx, bss, brs):
+        per = per_l if kind == "l" else per_s
+        owner = unit // per
+
+        @pl.when(owner != me)
+        def _():
+            swap.back(kind, unit - owner * per, owner, me, eu, rx, bss, brs).wait_recv()
+
+    def norm_back(x, eu, at):
+        unit, scale = unit_rows(x.astype(F32))
+        d = eu * gain_ref[...]
+        m1 = jnp.mean(d, axis=-1, keepdims=True)
+        m2 = jnp.mean(d * unit, axis=-1, keepdims=True)
+        ey[at, :] += scale * (d - m1 - unit * m2)
+        vec[7:8, :] += jnp.sum(eu * unit, axis=0, keepdims=True)
+        return jnp.sum(eu, axis=0, keepdims=True)
+
+    def home_l(n, total):
+        arrived("l", 2 * n, eu_l, rx_l, bk_ss_l, bk_rs_l)
+        arrived("l", 2 * n + 1, eu_l, rx_l, bk_ss_l, bk_rs_l)
+        at = pl.ds(pl.multiple_of(small_rows + n * patches_l, 16), patches_l)
+        eu = jnp.concatenate([rx_l[2 * n], rx_l[2 * n + 1]], axis=1).astype(F32)
+        return total + norm_back(xl[n], eu, at)
+
+    def home_s(n, total):
+        arrived("s", n, eu_s, rx_s, bk_ss_s, bk_rs_s)
+        at = pl.ds(pl.multiple_of(n * patches_s, 16), patches_s)
+        eu = rx_s[n].astype(F32)
+        return total + norm_back(xs[n], eu, at)
+
+    total = lax.fori_loop(0, count_l, home_l, jnp.zeros((1, width), F32))
+    total = lax.fori_loop(0, count_s, home_s, total)
+    vec[9:10, :] = total
+    gx_out = pltpu.make_async_copy(ey, gx_hbm, gx_sem.at[0])
+    gx_out.start()
+
+    both = vec.at[0:16]
+    v_core = send(both, vec_rx.at[0], v_ss.at[0], v_rs.at[0], core_peer)
+    v_core.start()
+    if far_inside:
+        tick_near(2)
+    tick_core(1)
+    t_x.wait_recv()
+    tok_sum[...] += tokx_rx[...].astype(F32)
+    t_near = []
+    part_n = SLAB // near
+    if far_inside:
+        for j, device in near_peers:
+            at = pl.ds(pl.multiple_of(lax.rem(peers.near + j, near) * part_n, part_n), part_n)
+            tokn_tx[j - 1] = tok_sum[at, :].astype(BF)
+            copy = send(tokn_tx.at[j - 1], tokn_rx.at[j - 1], tn_ss.at[j - 1], tn_rs.at[j - 1], device)
+            copy.start()
+            t_near.append(copy)
+    else:
+        tok_out[...] = tok_sum[...].astype(BF)
+    v_core.wait()
+    vec[0:16, :] += vec_rx[0]
+    v_x = send(both, vec_rx.at[1], v_ss.at[1], v_rs.at[1], x_peer)
+    v_x.start()
+    if far_inside:
+        tick_near(3)
+    tick_core(2)
+    t_far = []
+    part_f = part_n // far
+    if far_inside:
+        for copy in t_near:
+            copy.wait_recv()
+        mine = pl.ds(pl.multiple_of(peers.near * part_n, part_n), part_n)
+        tok_half[...] = tok_sum[mine, :]
+        for j in range(near - 1):
+            tok_half[...] += tokn_rx[j].astype(F32)
+        for j, device in far_peers:
+            at = pl.ds(pl.multiple_of(lax.rem(peers.far + j, far) * part_f, part_f), part_f)
+            tokf_tx[j - 1] = tok_half[at, :].astype(BF)
+            copy = send(tokf_tx.at[j - 1], tokf_rx.at[j - 1], tf_ss.at[j - 1], tf_rs.at[j - 1], device)
+            copy.start()
+            t_far.append(copy)
+    v_x.wait()
+    vec[0:16, :] += vec_rx[1]
+    v_near = [send(vec, vecn_rx.at[j - 1], vn_ss.at[j - 1], vn_rs.at[j - 1], device) for j, device in near_peers]
+    for copy in v_near:
+        copy.start()
+    if far_inside:
+        tick_near(4)
+    tick_core(3)
+    ta_far = []
+    if far_inside:
+        for copy in t_far:
+            copy.wait_recv()
+        value = tok_half[pl.ds(pl.multiple_of(peers.far * part_f, part_f), part_f), :]
+        for j in range(far - 1):
+            value = value + tokf_rx[j].astype(F32)
+        span = tok_out.at[pl.ds(pl.multiple_of(peers.near * part_n + peers.far * part_f, part_f), part_f)]
+        span[...] = value.astype(BF)
+        for j, device in far_peers:
+            copy = send(span, span, taf_ss.at[j - 1], taf_rs.at[j - 1], device)
+            copy.start()
+            ta_far.append(copy)
+    for copy in v_near:
+        copy.wait()
+    for j in range(near - 1):
+        vec[...] += vecn_rx[j]
+    v_far = [send(vec, vecf_rx.at[j - 1], vf_ss.at[j - 1], vf_rs.at[j - 1], device) for j, device in far_peers]
+    for copy in v_far:
+        copy.start()
+    ta_near = []
+    if far_inside:
+        for copy in ta_far:
+            copy.wait_recv()
+        span = tok_out.at[pl.ds(pl.multiple_of(peers.near * part_n, part_n), part_n)]
+        for j, device in near_peers:
+            copy = send(span, span, tan_ss.at[j - 1], tan_rs.at[j - 1], device)
+            copy.start()
+            ta_near.append(copy)
+        tick_near(5)
+    tick_core(4)
+    for copy in v_far:
+        copy.wait()
+    value = vec[...]
+    for j in range(far - 1):
+        value = value + vecf_rx[j]
+    vec_out[...] = value
+    for copy in ta_near:
+        copy.wait_recv()
+    tick_core(5)
+
+    for copy in [t_core, t_x] + t_near + t_far + ta_far + ta_near:
+        copy.wait_send()
+    for k in range(1, size):
+        there = swap.other(k)
+        for j in range(per_l):
+            swap.out("l", j, there, me, tx_l, e_l, out_ss_l, out_rs_l).wait_send()
+            swap.back("l", j, me, there, eu_l, rx_l, bk_ss_l, bk_rs_l).wait_send()
+        for j in range(per_s):
+            swap.out("s", j, there, me, tx_s, e_s, out_ss_s, out_rs_s).wait_send()
+            swap.back("s", j, me, there, eu_s, rx_s, bk_ss_s, bk_rs_s).wait_send()
     for k in range(GROUPS):
-        x_copy(k).wait_send()
-        if far_inside:
-            for j in range(1, far):
-                far_copy(k, j).wait_send()
-        for j in range(1, near):
-            near_copy(k, j).wait_send()
-        core_copy(k).wait_send()
-
-
-def gather(chunk, width):
+        g_x(k).wait_send()
+        for copy in g_far(k) + g_near(k):
+            copy.wait_send()
+        g_core(k).wait()
+    gx_out.wait()
+
+
+def backward(chunk, ey, xl, xs, saved, small, gain):
+    size = lax.axis_size("blk")
+    near, far = img_split(lax.axis_size("img"))
+    rows, width = ey.shape
+    far_inside = width % (near * far * 2 * 16) == 0
+    u_l, u_s, h_l, h_s, sl_l, sl_s, w_l, w_s = saved
+    count_l, patches_l, _ = xl.shape
+    count_s, patches_s, _ = xs.shape
+    token = w_l.shape[2]
+    half = width // 2
+    per_l, per_s = u_l.shape[0], u_s.shape[0]
     each, hidden = chunk.shape
-    near, far = img_split(lax.axis_size("img"))
-    far_inside = width % (near * far * 2 * 16) == 0
-    fm = far - 1
+    vmem = pl.BlockSpec(memory_space=pltpu.VMEM)
+    V = pltpu.VMEM
     DMA = pltpu.SemaphoreType.DMA
+    n1, f1 = near - 1, far - 1
+    part_n = SLAB // near
+    part_f = max(part_n // far, 16)
     return pl.pallas_call(
-        functools.partial(gather_kernel, near, far, far_inside),
-        out_shape=jax.ShapeDtypeStruct((2, width, hidden), BF),
-        in_specs=[ANY],
-        out_specs=ANY,
+        functools.partial(backward_kernel, near, far, size, far_inside),
+        out_shape=(
+            jax.ShapeDtypeStruct((2, width, hidden), BF),
+            jax.ShapeDtypeStruct((rows, width), F32),
+            jax.ShapeDtypeStruct((SLAB, token), BF),
+            jax.ShapeDtypeStruct((24, width), F32),
+        ),
+        in_specs=[ANY, ANY] + [vmem] * 12,
+        out_specs=(ANY, ANY, vmem, vmem),
         scratch_shapes=[
-            DMA((GROUPS,)), DMA((GROUPS,)), DMA((GROUPS,)), DMA((GROUPS, fm)), DMA((GROUPS, fm)),
-            DMA((GROUPS, near - 1)), DMA((GROUPS, near - 1)), DMA((GROUPS,)), DMA((GROUPS,)),
+            V((rows, width), F32),
+            V((count_l * 2, patches_l, half), BF), V((count_s, patches_s, width), BF),
+            V(u_l.shape, BF), V(u_s.shape, BF),
+            V((token, size * patches_l), BF), V((token, size * patches_s), BF),
+            V(h_l.shape, BF), V(h_s.shape, BF), V(u_l.shape, BF), V(u_s.shape, BF),
+            V((count_l * 2, patches_l, half), BF), V((count_s, patches_s, width), BF),
+            V((size, SLAB, token), F32), V((2, SLAB, token), BF), V((2, SLAB, token), BF),
+            V((SLAB, token), BF), V((SLAB, token), BF), V((SLAB, token), F32),
+            V((n1, part_n, token), BF), V((n1, part_n, token), BF), V((part_n, token), F32),
+            V((f1, part_f, token), BF), V((f1, part_f, token), BF),
+            V((24, width), F32), V((2, 16, width), F32), V((n1, 24, width), F32), V((f1, 24, width), F32),
+            DMA((1,)), DMA((1,)),
+            DMA((GROUPS,)), DMA((GROUPS,)), DMA((GROUPS,)), DMA((GROUPS, f1)), DMA((GROUPS, f1)),
+            DMA((GROUPS, n1)), DMA((GROUPS, n1)), DMA((GROUPS,)), DMA((GROUPS,)),
+            DMA((count_l * 2,)), DMA((count_s,)), DMA((per_l, size)), DMA((per_s, size)),
+            DMA((per_l, size)), DMA((per_s, size)), DMA((count_l * 2,)), DMA((count_s,)),
+            DMA((1,)), DMA((1,)), DMA((1,)), DMA((1,)), DMA((n1,)), DMA((n1,)), DMA((f1,)), DMA((f1,)),
+            DMA((f1,)), DMA((f1,)), DMA((n1,)), DMA((n1,)),
+            DMA((2,)), DMA((2,)), DMA((n1,)), DMA((n1,)), DMA((f1,)), DMA((f1,)),
         ],
-        compiler_params=pltpu.CompilerParams(collective_id=1, has_side_effects=True),
-    )(chunk)
+        compiler_params=pltpu.CompilerParams(
+            collective_id=1, has_side_effects=True, vmem_limit_bytes=TOP
+        ),
+    )(chunk, ey, xl, xs, u_l, u_s, h_l, h_s, sl_l, sl_s, w_l, w_s, small, gain.reshape(1, -1))
+
+
+def widen_kernel(first, second, out_first, out_second):
+    out_first[...] = first[0].astype(F32)
+    out_second[...] = second[0].astype(F32).T
+
+
+def widen(full):
+    _, width, hidden = full.shape
+    step = 384
+    return pl.pallas_call(
+        widen_kernel,
+        grid=(hidden // step,),
+        out_shape=(jax.ShapeDtypeStruct((width, hidden), F32), jax.ShapeDtypeStruct((hidden, width), F32)),
+        in_specs=[
+            pl.BlockSpec((1, width, step), lambda i: (0, 0, i)),
+            pl.BlockSpec((1, width, step), lambda i: (1, 0, i)),
+        ],
+        out_specs=(pl.BlockSpec((width, step), lambda i: (0, i)), pl.BlockSpec((step, width), lambda i: (i, 0))),
+        compiler_params=pltpu.CompilerParams(vmem_limit_bytes=TOP),
+    )(full, full)
 
 
 def local(
@@ -523,89 +1039,58 @@
     ln2_gain, ln2_bias, ch_w1, ch_b1, ch_w2, ch_b2, cot_small, cot_large,
 ):
     width = x_small.shape[2]
-    mask_small = (jnp.arange(x_small.shape[0]) < live_counts[0, 0]).astype(F32)
-    mask_large = (jnp.arange(x_large.shape[0]) < live_counts[0, 1]).astype(F32)
-    groups = []
-    for x, w1, b1, w2, b2 in (
-        (x_small, tok_w1_small, tok_b1_small, tok_w2_small, tok_b2_small),
-        (x_large, tok_w1_large, tok_b1_large, tok_w2_large, tok_b2_large),
-    ):
-        wide = x.astype(F32)
-        normed, back = jax.vjp(norm_rows, wide, ln1_gain, ln1_bias)
-        w1_all = lax.all_gather(w1, "blk", axis=0, tiled=True)
-        w2_all = lax.all_gather(w2, "blk", axis=1, tiled=True)
-        u_cols = to_columns(normed.astype(BF))
-        preact = mm("sj,sd->jd", w1_all, u_cols) + b1[:, None]
-        hidden = jax.nn.gelu(preact).astype(BF)
-        mixed = to_rows(mm("js,jd->sd", w2_all, hidden).astype(BF), x.shape)
-        mid = wide + mixed.astype(F32) + b2[:, None]
-        groups.append((x, mid, back, w1_all, w2_all, u_cols, preact, hidden))
-    pad_small = -x_small.shape[1] % 64
-    small_rows = x_small.shape[0] * (x_small.shape[1] + pad_small)
-    large_rows = x_large.shape[0] * x_large.shape[1]
-    spare = -(small_rows + large_rows) % (3 * LANES)
-
-    def join(small, large):
-        small = jnp.pad(small, ((0, 0), (0, pad_small), (0, 0))).reshape(-1, width)
-        return jnp.concatenate([small, large.reshape(-1, width), jnp.zeros((spare, width), small.dtype)])
+    token = tok_w1_large.shape[1]
+    patches_s, patches_l = x_small.shape[1], x_large.shape[1]
+    extra = -patches_s % 64
+    wide_s = patches_s + extra
+    small_rows = x_small.shape[0] * wide_s
+    large_rows = x_large.shape[0] * patches_l
+    rows = small_rows + large_rows
+    spare = -rows % (3 * LANES)
+
+    def widen_small(small):
+        return jnp.pad(small, ((0, 0), (0, extra), (0, 0)))
 
     def part(joined):
-        small = joined[:small_rows].reshape(x_small.shape[0], -1, width)[:, : x_small.shape[1]]
-        return small, joined[small_rows : small_rows + large_rows].reshape(x_large.shape)
-
-    mask_small = mask_small[:, None, None]
-    mask_large = mask_large[:, None, None]
-    ec = join(cot_small * mask_small.astype(BF), cot_large * mask_large.astype(BF))
-    out, ey, chunk, small_grads = channel(
-        join(groups[0][1], groups[1][1]), ec, ch_w1, ch_w2, ch_b1, ln2_gain, ln2_bias, ch_b2
+        small = joined[:small_rows].reshape(x_small.shape[0], wide_s, width)[:, :patches_s]
+        return small, joined[small_rows:rows].reshape(x_large.shape)
+
+    mask_small = (jnp.arange(x_small.shape[0]) < live_counts[0, 0]).astype(BF)[:, None, None]
+    mask_large = (jnp.arange(x_large.shape[0]) < live_counts[0, 1]).astype(BF)[:, None, None]
+    xs = widen_small(x_small)
+    wq_l = jnp.stack([tok_w1_large, tok_w2_large.T])
+    wq_s = widen_small(jnp.stack([tok_w1_small, tok_w2_small.T]))
+    y, *saved = token_forward(
+        x_large, xs, wq_l, wq_s, tok_b1_large, tok_b1_small, tok_b2_large, jnp.pad(tok_b2_small, (0, extra)),
+        ln1_gain, ln1_bias, rows + spare,
     )
-    out_small, out_large = part(out)
-    out_small = out_small * mask_small.astype(BF)
-    out_large = out_large * mask_large.astype(BF)
-    grad_ch_b1 = small_grads[:4].reshape(-1)
-    grad_ch_b2, grad_gain2, grad_bias2 = small_grads[4], small_grads[5], small_grads[6]
+    ec = jnp.concatenate([
+        widen_small(cot_small * mask_small).reshape(-1, width),
+        (cot_large * mask_large).reshape(-1, width),
+        jnp.zeros((spare, width), BF),
+    ])
+    out, ey, chunk, small_grads = channel(y, ec, ch_w1, ch_w2, ch_b1, ln2_gain, ln2_bias, ch_b2)
     near, far = img_split(lax.axis_size("img"))
-    if width % (near * far * 2 * 16):
+    far_inside = width % (near * far * 2 * 16) == 0
+    if not far_inside:
         same = [[a * near + b for a in range(far)] for b in range(near)]
         chunk = lax.psum(chunk.astype(F32), "img", axis_index_groups=same).astype(BF)
-    full = gather(chunk, width)
-    grad_ch_w1 = full[0].astype(F32)
-    grad_ch_w2 = full[1].T.astype(F32)
-    grads = []
-    gain1 = 0.0
-    bias1 = 0.0
-    for (x, mid, back, w1_all, w2_all, u_cols, preact, hidden), part_ey in zip(
-        groups, part(ey)
-    ):
-        et = part_ey.astype(BF)
-        grad_b2 = jnp.sum(et.astype(F32), axis=(0, 2))
-        et_cols = to_columns(et)
-        grad_w2 = mm("jd,sd->js", hidden, et_cols)
-        ep = gelu_back(preact, mm("js,sd->jd", w2_all, et_cols)).astype(BF)
-        grad_b1 = jnp.sum(ep.astype(F32), axis=1)
-        grad_w1 = mm("sd,jd->sj", u_cols, ep)
-        eu = to_rows(mm("sj,jd->sd", w1_all, ep).astype(BF), x.shape)
-        norm_grad, gain_part, bias_part = back(eu.astype(F32))
-        gain1 = gain1 + gain_part
-        bias1 = bias1 + bias_part
-        grads.append((part_ey + norm_grad, grad_w1, grad_b1, grad_w2, grad_b2))
-    scattered = [
-        (
-            lax.psum_scatter(grad_w1, "blk", scatter_dimension=0, tiled=True),
-            lax.psum_scatter(grad_w2, "blk", scatter_dimension=1, tiled=True),
-        )
-        for _, grad_w1, _, grad_w2, _ in grads
-    ]
-    (w1_s, w2_s), (w1_l, w2_l) = lax.psum(scattered, "img")
-    b2_s, b2_l = lax.psum((grads[0][4], grads[1][4]), "img")
-    both = ("img", "blk")
-    gain1, bias1, b1_s, b1_l, grad_gain2, grad_bias2, grad_ch_b1, grad_ch_b2 = lax.psum(
-        (gain1, bias1, grads[0][2], grads[1][2], grad_gain2, grad_bias2, grad_ch_b1, grad_ch_b2), both
-    )
+    full, gx, tok, vec = backward(chunk, ey, x_large, xs, saved, small_grads, ln1_gain)
+    tok = tok.astype(F32)
+    if not far_inside:
+        tok = lax.psum(tok, "img")
+    grad_ch_w1, grad_ch_w2 = widen(full)
+    out_small, out_large = part(out)
+    gx_small, gx_large = part(gx)
+    half = width // 2
+    b2_l = vec[16, :patches_l]
+    b2_s = vec[16, half:half + patches_s]
+    at = 2 * patches_l
     return (
-        out_small, out_large, grads[0][0], grads[1][0], gain1, bias1,
-        w1_s, b1_s, w2_s, b2_s, w1_l, b1_l, w2_l, b2_l,
-        grad_gain2, grad_bias2, grad_ch_w1, grad_ch_b1, grad_ch_w2, grad_ch_b2,
+        out_small * mask_small, out_large * mask_large, gx_small, gx_large, vec[7], vec[9],
+        tok[at:at + patches_s], vec[8, half:], tok[at + wide_s:at + wide_s + patches_s].T, b2_s,
+        tok[:patches_l], vec[8, :half], tok[patches_l:at].T, b2_l,
+        vec[5], vec[6], grad_ch_w1, vec[:4].reshape(-1), grad_ch_w2, vec[4],
     )
 
 

time: 598 us -> 304 us (0.51); the launches traced: 587 us -> 302 us
  blocking collectives: 126 us -> 0 us
  waiting for transfers between devices: 97.5 us -> 0 us
  Pallas kernels: 169 us -> 259 us
  local copies, waits for them, and re-layouts: 74 us -> 32 us
  starting transfers between devices: 37.5 us -> 0 us
  other arithmetic: 48 us -> 10.6 us
  matrix products: 19.2 us -> 0 us
  between operations: 16 us -> 0.79 us
    pallas_call x1 -> x3, Pallas kernels: 70 us -> 165 us  [the longest x1 101 us: backward(): pl.pallas_call(functools.partial(backward_kernel, near, far, size, far_in...]
    psum x1 -> x0, waiting for transfers between devices: 70.7 us -> none  [local(): (w1_s, w2_s), (w1_l, w2_l) = lax.psum(scattered, 'img')]
    psum x2 -> x0, blocking collectives: 66.2 us -> none  [the longest x1 38.2 us: local(): lax.psum((gain1, bias1, grads[0][2], grads[1][2], grad_gain2, grad_bias2,...]
    all_gather x4 -> x0, blocking collectives: 40.8 us -> none  [the longest x2 26.8 us: local(): w2_all = lax.all_gather(w2, 'blk', axis=1, tiled=True)]
    all_to_all x8 -> x0, starting transfers between devices: 30.9 us -> none  [the longest x4 15.8 us: to_rows(): moved = lax.all_to_all(blocks, 'blk', 0, 0, tiled=True)]
    unnamed x156 -> x9, local copies, waits for them, and re-layouts: 30.3 us -> 1.14 us
    all_to_all x8 -> x0, waiting for transfers between devices: 26.7 us -> none  [the longest x4 26.7 us: to_rows(): moved = lax.all_to_all(blocks, 'blk', 0, 0, tiled=True)]
    unnamed x1 -> x0, blocking collectives: 19.2 us -> none
  transfers between devices with their start and end apart: 13 -> 0, of which waited for: 4 -> 0; matrix products, arithmetic and copies ran while one was open for 20% -> 0% of each run, Pallas kernels for 12% -> 0%
where the time goes in v3:
time: 304 us; the launch traced here: 302 us
  Pallas kernels  259 us (85%)
  local copies, waits for them, and re-layouts  32 us (11%)
  other arithmetic  10.6 us (3%)
    pallas_call x1, Pallas kernels, backward(): pl.pallas_call(functools.partial(backward_kernel, near, far, size, far_in...  101 us
    pallas_call x1, Pallas kernels, channel(): pl.pallas_call(functools.partial(channel_kernel, near, far, far_inside),...  93.7 us
    pallas_call x1, Pallas kernels, token_forward(): pl.pallas_call(functools.partial(token_kernel, near, size), out_shape=(ja...  52.9 us
    pallas_call x1, Pallas kernels, widen(): pl.pallas_call(widen_kernel, grid=(hidden // step,), out_shape=(jax.Shape...  11.4 us

profile of v3, /device:TPU:0, one launch (start us, length us, event | category | flops | bytes accessed | tf_op | source)
XLA Modules:
  0.0 302.5 jit_solution(2943337763376825626)
XLA Ops:
  1.4 1.3 fusion.3
  4.0 1.3 reshape.106.gain_ref
  5.3 1.3 reshape.107.bias_ref
  6.5 1.3 reshape.111.gain_ref
  7.8 1.3 reshape.112.bias_ref
  9.1 1.3 reshape.113.b2_ref
  11.1 1.4 copy.49.b2_l
  12.5 1.5 fusion.2.wq_s
  14.0 1.5 reshape.120.b1_s
  15.5 1.5 reshape.119.b1_l
  17.0 1.7 pad_maximum_fusion.wq_l
  18.6 1.3 broadcast_multiply_fusion.2
  21.0 1.6 maximum_maximum_fusion.ec_hbm
  22.5 52.9 %shard_map.356 = (f32[1152,768]{1,0:T(8,128)}, bf16[3,576,384]{2,1,0:T(8,128)(2,1)}, bf16[1,256,768]{2,1,0:T(8,128)(2,1)}, bf16[3,384,384]{2,1,0:T(8,128)(2,1)},...) custom-call(bf16[6,144,768]{2,1,0:T(8,128)(2,1)} %xl.3, ...), custom_call_target="tpu_custom_call" | custom-call | tf_op jit(solution)/shard_map/pallas_call | solution.py:607
  75.4 93.7 %shard_map.357 = (bf16[1152,768]{1,0:T(8,128)(2,1)}, f32[1152,768]{1,0:T(8,128)}, bf16[48,3072]{1,0:T(8,128)(2,1)}, f32[8,768]{1,0:T(8,128)}) custom-call(f32[1152,768]{1,0:T(8,128)} %get-tuple-element.39.y_hbm, bf16[1152,768]{1,0:T(8,128)(2,1)} %maximum_maximum_fusion.ec_hbm, bf16[768,3072]{1,0:T(8,128)(2,1)} %w1_hbm.1, bf16[3072,768]{1,0:T(8,128)(2,1)} %w2_hbm.1, ...), custom_call_target="tpu_custom_call" | custom-call | tf_op jit(solution)/shard_map/pallas_call | solution.py:352
  170.2 1.4 slice.70
  173.8 101.0 %shard_map.358 = (bf16[2,768,3072]{2,1,0:T(8,128)(2,1)}, f32[1152,768]{1,0:T(8,128)}, bf16[512,384]{1,0:T(8,128)(2,1)}, f32[24,768]{1,0:T(8,128)}) custom-call(bf16[48,3072]{1,0:T(8,128)(2,1)} %get-tuple-element.41.chunk_hbm, f32[1152,768]{1,0:T(8,128)} %get-tuple-element.42.ey_hbm, bf16[6,144,768]{2,1,0:T(8,128)(2,1)} %xl.3, bf16[4,64,768]{2,1,0:T(8,128)(2,1)} %pad.15.xs, ...), custom_call_target="tpu_custom_call" | custom-call | tf_op jit(solution)/shard_map/pallas_call | solution.py:977
  276.0 1.3 slice.83
  277.2 1.3 slice_reduce_fusion.5
  279.3 1.6 slice_reduce_fusion
  281.5 1.4 slice.90
  282.9 1.7 slice.92
  288.3 1.7 slice.73
  291.0 11.4 %shard_map.359 = (f32[768,3072]{1,0:T(8,128)}, f32[3072,768]{1,0:T(8,128)}) custom-call(bf16[2,768,3072]{2,1,0:T(8,128)(2,1)} %get-tuple-element.55.first.second, bf16[2,768,3072]{2,1,0:T(8,128)(2,1)} %get-tuple-element.55.first.second), custom_call_target="tpu_custom_call" | custom-call | tf_op jit(solution)/shard_map/pallas_call | solution.py:1022
  (30 shorter events, 14.2 us)
Async XLA Ops:
  0.7 19.3 %copy-start.2 = (bf16[4,49,768]{2,0,1:T(4,128)(2,1)S(1)}, bf16[4,49,768]{2,0,1:T(4,128)(2,1)}, u32[]{:S(2)}) copy-start(bf16[4,49,768]{2,0,1:T(4,128)(2,1)} %param.21) | copy-start | bytes 903172
  18.6 2.2 copy-start.1
  282.9 5.3 %copy-start = (f32[1152,768]{1,0:T(8,128)S(1)}, f32[1152,768]{1,0:T(8,128)}, u32[]{:S(2)}) copy-start(f32[1152,768]{1,0:T(8,128)} %get-tuple-element.52) | copy-start | bytes 10616836

commit v4 on v3

--- a/solution.py
+++ b/solution.py
@@ -67,20 +67,39 @@
     pl.semaphore_wait(barrier, total)
 
 
+def row(ref):
+    return ref[...].reshape(1, -1)
+
+
+def column(ref, rows):
+    value = jnp.broadcast_to(ref[...].reshape(1, -1), (8, ref.shape[0])).T[:, :1]
+    return value if rows == ref.shape[0] else jnp.concatenate([value, jnp.zeros((rows - ref.shape[0], 1), F32)])
+
+
 def channel_kernel(
     near, far, far_inside,
-    y_hbm, ec_hbm, w1_hbm, w2_hbm, b1_ref, gain_ref, bias_ref, b2_ref,
-    out_hbm, ey_hbm, chunk_ref, small_ref,
+    y_hbm, live, cot_l, cot_s, w1_hbm, w2_hbm, b1_ref, gain_ref, bias_ref, b2_ref,
+    out_l, ey_hbm, chunk_ref, small_ref, out_s,
     y, ec, v, lt, rt, w1, w2, acc_out, acc_ev, out_low,
-    keep, core_tx, core_rx, keep_n, near_tx, near_rx, keep_f, far_tx, far_rx, keep_x, x_tx, x_rx,
-    in_sem, w_sem, out_sem, core_ss, core_rs, near_ss, near_rs, far_ss, far_rs, x_ss, x_rs,
+    keep, core_tx, core_rx,
+    a_keep_n, a_near_tx, a_near_rx, a_keep_f, a_far_tx, a_far_rx, a_keep_x, a_x_tx, a_x_rx,
+    b_keep_x, b_x_tx, b_x_rx, b_keep_n, b_near_tx, b_near_rx, b_keep_f, b_far_tx, b_far_rx,
+    in_sem, w_sem, out_sem, core_ss, core_rs,
+    a_near_ss, a_near_rs, a_far_ss, a_far_rs, a_x_ss, a_x_rs,
+    b_near_ss, b_near_rs, b_far_ss, b_far_rs, b_x_ss, b_x_rs,
 ):
     rows, width = y.shape
     tiles = w1.shape[0]
+    count_l, patches_l, _ = cot_l.shape
+    count_s, patches_s, _ = cot_s.shape
+    wide_s = patches_s + -patches_s % 64
+    small_rows = count_s * wide_s
     peers = Peers(near)
     core = peers.core
+    f_place = peers.far if far_inside else 0
     part = 128
     parts = rows // part
+    gain, bias, b2 = row(gain_ref), row(bias_ref), row(b2_ref)
 
     def w_copies(t):
         return (
@@ -89,9 +108,7 @@
         )
 
     y_in = pltpu.make_async_copy(y_hbm, y, in_sem.at[0])
-    ec_in = pltpu.make_async_copy(ec_hbm, ec, in_sem.at[1])
     y_in.start()
-    ec_in.start()
 
     def start_w(t, carry):
         for copy in w_copies(t):
@@ -101,18 +118,36 @@
     lax.fori_loop(0, tiles, start_w, 0)
     axes = [("core", 2), ("near", near)] + ([("far", far)] if far_inside else []) + [("x", 2)]
     greet(peers, axes)
+    small_ref[...] = jnp.zeros_like(small_ref)
+    used = small_rows + count_l * patches_l
+    ec[0:small_rows, :] = jnp.zeros((small_rows, width), BF)
+    if rows > used:
+        ec[used:rows, :] = jnp.zeros((rows - used, width), BF)
+
+    def live_l(n):
+        return jnp.where(n < live[0, 1], 1.0, 0.0).astype(F32)
+
+    def live_s(n):
+        return jnp.where(n < live[0, 0], 1.0, 0.0).astype(F32)
+
+    def mask_l(n, carry):
+        ec[pl.ds(pl.multiple_of(small_rows + n * patches_l, 16), patches_l), :] = (
+            cot_l[n].astype(F32) * live_l(n)
+        ).astype(BF)
+        return carry
+
+    def mask_s(n, carry):
+        ec[pl.ds(pl.multiple_of(n * wide_s, 16), patches_s), :] = (cot_s[n].astype(F32) * live_s(n)).astype(BF)
+        return carry
+
+    lax.fori_loop(0, count_l, mask_l, 0)
+    lax.fori_loop(0, count_s, mask_s, 0)
     y_in.wait()
-    ec_in.wait()
-    small_ref[...] = jnp.zeros_like(small_ref)
 
     def prepare(p, carry):
         at = pl.ds(pl.multiple_of(p * part, part), part)
-        row = y[at, :]
-        mean = jnp.mean(row, axis=-1, keepdims=True)
-        centered = row - mean
-        var = jnp.mean(centered * centered, axis=-1, keepdims=True)
-        normed = centered * lax.rsqrt(var + EPSILON) * gain_ref[...] + bias_ref[...]
-        low = normed.astype(BF)
+        unit, _ = unit_rows(y[at, :])
+        low = (unit * gain + bias).astype(BF)
         v[at, :] = low
         lt[0, :, at] = low.T
         own = ec[at, :]
@@ -133,211 +168,240 @@
         slot = lax.rem(t, 2)
         return send(core_tx.at[slot], core_rx.at[t], core_ss.at[slot], core_rs.at[t], peers.at("core", 1 - core))
 
-    def near_copy(t, j):
-        slot = lax.rem(t, 2)
-        there = lax.rem(peers.near + j, near)
-        return send(
-            near_tx.at[slot, j - 1], near_rx.at[t, j - 1], near_ss.at[slot, j - 1], near_rs.at[t, j - 1],
-            peers.at("near", there),
-        )
-
-    def far_copy(t, j):
-        slot = lax.rem(t, 2)
-        there = lax.rem(peers.far + j, far)
-        return send(
-            far_tx.at[slot, j - 1], far_rx.at[t, j - 1], far_ss.at[slot, j - 1], far_rs.at[t, j - 1],
-            peers.at("far", there),
-        )
-
-    def x_copy(t):
-        slot = lax.rem(t, 2)
-        return send(x_tx.at[slot], x_rx.at[t], x_ss.at[slot], x_rs.at[t], peers.at("x", 1 - peers.x))
-
-    step_rows = rows
+    def spread(tx, rx, ss, rs, axis, count, i):
+        slot = lax.rem(i, 2)
+        copies = []
+        for j in range(1, count):
+            there = lax.rem(peers.mine(axis) + j, count)
+            copies.append(
+                send(tx.at[slot, j - 1], rx.at[i, j - 1], ss.at[slot, j - 1], rs.at[i, j - 1], peers.at(axis, there))
+            )
+        return copies
+
+    f = far if far_inside else 1
+    a_near = lambda i: spread(a_near_tx, a_near_rx, a_near_ss, a_near_rs, "near", near, i)
+    a_far = lambda i: spread(a_far_tx, a_far_rx, a_far_ss, a_far_rs, "far", f, i)
+    a_x = lambda i: spread(a_x_tx, a_x_rx, a_x_ss, a_x_rs, "x", 2, i)
+    b_near = lambda i: spread(b_near_tx, b_near_rx, b_near_ss, b_near_rs, "near", near, i)
+    b_far = lambda i: spread(b_far_tx, b_far_rx, b_far_ss, b_far_rs, "far", f, i)
+    b_x = lambda i: spread(b_x_tx, b_x_rx, b_x_ss, b_x_rs, "x", 2, i)
+    each = width // near // f // 2
 
     def tile_step(t):
         for copy in w_copies(t):
             copy.wait()
         columns = pl.ds(pl.multiple_of(t * TILE, TILE), TILE)
-        bias = b1_ref[:, columns]
-
-        def act(p, total):
-            at = pl.ds(pl.multiple_of(p * step_rows, step_rows), step_rows)
-            a = jnp.dot(v[at, :], w1[t], preferred_element_type=F32) + bias
-            gh = lax.dot_general(ec[at, :], w2[t], (((1,), (1,)), ((), ())), preferred_element_type=F32)
-            g, slope = gelu_pair(a)
-            ea = (slope * gh).astype(BF)
-            rt[1, at, :] = g.astype(BF)
-            rt[0, at, :] = ea
-            return total + jnp.sum(ea.astype(F32), axis=0, keepdims=True)
-
-        total = lax.fori_loop(0, rows // step_rows, act, jnp.zeros((1, TILE), F32))
-        small_ref[lax.div(t, 3), pl.ds(pl.multiple_of(lax.rem(t, 3) * TILE, TILE), TILE)] = total[0]
-
+        a = matmul(v[...], w1[t]) + b1_ref[columns].reshape(1, -1)
+        gh = matmul_nt(ec[...], w2[t])
+        g, slope = gelu_pair(a)
+        ea = (slope * gh).astype(BF)
+        rt[1] = g.astype(BF)
+        rt[0] = ea
+        per = width // TILE
+        small_ref[lax.div(t, per), pl.ds(pl.multiple_of(lax.rem(t, per) * TILE, TILE), TILE)] = jnp.sum(
+            ea.astype(F32), axis=0
+        )
         slot = lax.rem(t, 2)
 
         @pl.when(t >= 2)
         def _():
             core_copy(t - 2).wait_send()
 
-        core_tx[slot] = jnp.dot(lt[1 - core], rt[1 - core], preferred_element_type=F32).astype(BF)
+        core_tx[slot] = matmul(lt[1 - core], rt[1 - core]).astype(BF).reshape(near, f, 2, each, TILE)
         core_copy(t).start()
-        keep[slot] = jnp.dot(lt[core], rt[core], preferred_element_type=F32)
-        def add(p, carry):
-            at = pl.ds(pl.multiple_of(p * step_rows, step_rows), step_rows)
-            acc_out[at, :] += jnp.dot(rt[1, at, :], w2[t], preferred_element_type=F32)
-            acc_ev[at, :] += lax.dot_general(
-                rt[0, at, :], w1[t], (((1,), (1,)), ((), ())), preferred_element_type=F32
-            )
+        keep[slot] = matmul(lt[core], rt[core]).reshape(near, f, 2, each, TILE)
+        acc_out[...] += matmul(rt[1], w2[t])
+        acc_ev[...] += matmul_nt(rt[0], w1[t])
+
+    def ey_copy(at, n):
+        return pltpu.make_async_copy(acc_ev.at[at], ey_hbm.at[at], out_sem.at[n])
+
+    def at_l(n):
+        return pl.ds(pl.multiple_of(small_rows + n * patches_l, 16), patches_l)
+
+    def at_s(n):
+        return pl.ds(pl.multiple_of(n * wide_s, 16), wide_s)
+
+    def out_copy(n):
+        return pltpu.make_async_copy(out_low.at[n], out_l.at[n], out_sem.at[count_l + count_s + n])
+
+    def finish_rows(at, live_here):
+        here = y[at, :]
+        result = ((here + acc_out[at, :] + b2) * live_here).astype(BF)
+        unit, scale = unit_rows(here)
+        ev = acc_ev[at, :]
+        small_ref[5:6, :] += jnp.sum(ev * unit, axis=0, keepdims=True)
+        small_ref[6:7, :] += jnp.sum(ev, axis=0, keepdims=True)
+        d = ev * gain
+        m1 = jnp.mean(d, axis=-1, keepdims=True)
+        m2 = jnp.mean(d * unit, axis=-1, keepdims=True)
+        acc_ev[at, :] = ec[at, :].astype(F32) + scale * (d - m1 - unit * m2)
+        return result
+
+    def finish(p):
+        def one_l(q, carry):
+            n = p + q * 4
+
+            @pl.when(n < count_l)
+            def _():
+                out_low[n] = finish_rows(at_l(n), live_l(n))
+                ey_copy(at_l(n), n).start()
+                out_copy(n).start()
+
             return carry
 
-        lax.fori_loop(0, rows // step_rows, add, 0)
-
-    share = rows // 4
-    piece = share // 3
-
-    def out_copies(p):
-        at = pl.ds(pl.multiple_of(p * share, share), share)
-        return (
-            pltpu.make_async_copy(out_low.at[at], out_hbm.at[at], out_sem.at[0, p]),
-            pltpu.make_async_copy(acc_ev.at[at], ey_hbm.at[at], out_sem.at[1, p]),
-        )
-
-    def finish(p):
-        def one(q, carry):
-            at = pl.ds(pl.multiple_of(p * share + q * piece, piece), piece)
-            row = y[at, :]
-            out_low[at, :] = (row + acc_out[at, :] + b2_ref[...]).astype(BF)
-            mean = jnp.mean(row, axis=-1, keepdims=True)
-            centered = row - mean
-            var = jnp.mean(centered * centered, axis=-1, keepdims=True)
-            scale = lax.rsqrt(var + EPSILON)
-            unit = centered * scale
-            ev = acc_ev[at, :]
-            small_ref[5:6, :] += jnp.sum(ev * unit, axis=0, keepdims=True)
-            small_ref[6:7, :] += jnp.sum(ev, axis=0, keepdims=True)
-            d = ev * gain_ref[...]
-            m1 = jnp.mean(d, axis=-1, keepdims=True)
-            m2 = jnp.mean(d * unit, axis=-1, keepdims=True)
-            acc_ev[at, :] = ec[at, :].astype(F32) + scale * (d - m1 - unit * m2)
+        def one_s(q, carry):
+            n = p + q * 4
+
+            @pl.when(n < count_s)
+            def _():
+                out_s[n] = finish_rows(at_s(n), live_s(n))[:patches_s]
+                ey_copy(at_s(n), count_l + n).start()
+
             return carry
 
-        lax.fori_loop(0, 3, one, 0)
-        for copy in out_copies(p):
-            copy.start()
-
-    def core_sum(t):
-        slot = lax.rem(t, 2)
+        lax.fori_loop(0, pl.cdiv(count_l, 4), one_l, 0)
+        lax.fori_loop(0, pl.cdiv(count_s, 4), one_s, 0)
+
+    def free(copies, i):
+        @pl.when(i >= 2)
+        def _():
+            for copy in copies(i - 2):
+                copy.wait_send()
+
+    def reduce(value, axis, count, place, tx, own, copies, i):
+        slot = lax.rem(i, 2)
+        free(copies, i)
+        made = copies(i)
+        for j in range(1, count + 1):
+            there = lax.rem(place + j, count)
+            piece = value(there)
+            if j < count:
+                tx[slot, j - 1] = piece.astype(BF)
+                made[j - 1].start()
+            else:
+                own(slot, piece)
+
+    def arrivals(copies, i):
+        for copy in copies(i):
+            copy.wait_recv()
+
+    def save(ref):
+        def put(slot, piece):
+            ref[slot] = piece
+        return put
+
+    def plus(base, rx, i, count, index):
+        value = base
+        for k in range(count - 1):
+            value = value + rx[(i, k) + index].astype(F32)
+        return value
+
+    def chunk_out(t, value):
+        chunk_ref[:, pl.ds(pl.multiple_of(t * TILE, TILE), TILE)] = value.astype(BF)
+
+    def even_core(t):
+        i = lax.div(t, 2)
         core_copy(t).wait_recv()
-
-        @pl.when(t >= 2)
-        def _():
-            for j in range(1, near):
-                near_copy(t - 2, j).wait_send()
-
-        each = width // near
-        for j in range(near):
-            there = lax.rem(peers.near + j, near)
-            at = pl.ds(pl.multiple_of(there * each, each), each)
-            value = keep[slot, at, :] + core_rx[t, at, :].astype(F32)
-            if j == 0:
-                keep_n[slot] = value
-            else:
-                near_tx[slot, j - 1] = value.astype(BF)
-                near_copy(t, j).start()
-
-    def near_sum(t):
-        slot = lax.rem(t, 2)
-        for j in range(1, near):
-            near_copy(t, j).wait_recv()
-
-        if far_inside:
-            @pl.when(t >= 2)
+        reduce(
+            lambda p: keep[0, p] + core_rx[t, p].astype(F32),
+            "near", near, peers.near, a_near_tx, save(a_keep_n), a_near, i,
+        )
+
+    def even_near(t):
+        i = lax.div(t, 2)
+        slot = lax.rem(i, 2)
+        arrivals(a_near, i)
+        reduce(
+            lambda p: plus(a_keep_n[slot, p], a_near_rx, i, near, (p,)),
+            "far", f, f_place, a_far_tx, save(a_keep_f), a_far, i,
+        )
+
+    def even_far(t):
+        i = lax.div(t, 2)
+        slot = lax.rem(i, 2)
+        arrivals(a_far, i)
+        reduce(
+            lambda p: plus(a_keep_f[slot, p], a_far_rx, i, f, (p,)),
+            "x", 2, peers.x, a_x_tx, save(a_keep_x), a_x, i,
+        )
+
+    def even_x(t):
+        i = lax.div(t, 2)
+        arrivals(a_x, i)
+        chunk_out(t, a_keep_x[lax.rem(i, 2)] + a_x_rx[i, 0].astype(F32))
+
+    def odd_core(t):
+        i = lax.div(t, 2)
+        core_copy(t).wait_recv()
+        reduce(
+            lambda p: keep[1, :, :, p] + core_rx[t, :, :, p].astype(F32),
+            "x", 2, peers.x, b_x_tx, save(b_keep_x), b_x, i,
+        )
+
+    def odd_x(t):
+        i = lax.div(t, 2)
+        slot = lax.rem(i, 2)
+        arrivals(b_x, i)
+        reduce(
+            lambda p: plus(b_keep_x[slot, p], b_x_rx, i, 2, (p,)),
+            "near", near, peers.near, b_near_tx, save(b_keep_n), b_near, i,
+        )
+
+    def odd_near(t):
+        i = lax.div(t, 2)
+        slot = lax.rem(i, 2)
+        arrivals(b_near, i)
+        reduce(
+            lambda p: plus(b_keep_n[slot, p], b_near_rx, i, near, (p,)),
+            "far", f, f_place, b_far_tx, save(b_keep_f), b_far, i,
+        )
+
+    def odd_far(t):
+        i = lax.div(t, 2)
+        arrivals(b_far, i)
+        slot = lax.rem(i, 2)
+        chunk_out(t, plus(b_keep_f[slot], b_far_rx, i, f, ()))
+
+    stages = ((even_core, even_near, even_far, even_x), (odd_core, odd_x, odd_near, odd_far))
+
+    def pair(s2, carry):
+        for parity in range(2):
+            s = s2 * 2 + parity
+
+            @pl.when(s < tiles)
             def _():
-                for j in range(1, far):
-                    far_copy(t - 2, j).wait_send()
-
-            each = width // near // far
-            for j in range(1, far + 1):
-                there = lax.rem(peers.far + j, far)
-                at = pl.ds(pl.multiple_of(there * each, each), each)
-                value = keep_n[slot, at, :]
-                for k in range(near - 1):
-                    value += near_rx[t, k, at, :].astype(F32)
-                if j == far:
-                    keep_f[slot] = value
-                else:
-                    far_tx[slot, j - 1] = value.astype(BF)
-                    far_copy(t, j).start()
-        else:
-            value = keep_n[slot]
-            for k in range(near - 1):
-                value += near_rx[t, k].astype(F32)
-            keep_f[slot] = value
-
-    def far_sum(t):
-        slot = lax.rem(t, 2)
-        if far_inside:
-            for j in range(1, far):
-                far_copy(t, j).wait_recv()
-
-        @pl.when(t >= 2)
-        def _():
-            x_copy(t - 2).wait_send()
-
-        each = chunk_ref.shape[0]
-        for there, own in ((peers.x, True), (1 - peers.x, False)):
-            at = pl.ds(pl.multiple_of(there * each, each), each)
-            value = keep_f[slot, at, :]
-            if far_inside:
-                for k in range(far - 1):
-                    value += far_rx[t, k, at, :].astype(F32)
-            if own:
-                keep_x[slot] = value
-            else:
-                x_tx[slot] = value.astype(BF)
-                x_copy(t).start()
-
-    def x_sum(t):
-        slot = lax.rem(t, 2)
-        x_copy(t).wait_recv()
-        columns = pl.ds(pl.multiple_of(t * TILE, TILE), TILE)
-        chunk_ref[:, columns] = (keep_x[slot] + x_rx[t].astype(F32)).astype(BF)
-
-    stages = (core_sum, near_sum, far_sum, x_sum)
-
-    def step(s, carry):
-        @pl.when(s < tiles)
-        def _():
-            tile_step(s)
-
-        for lag, stage in enumerate(stages):
-            t = s - lag
-            @pl.when((t >= 0) & (t < tiles))
-            def _(t=t, stage=stage):
-                stage(t)
-
-        @pl.when(s >= tiles)
-        def _():
-            finish(s - tiles)
+                tile_step(s)
+
+            for lag in range(1, 5):
+                t = s - lag
+                stage = stages[(parity - lag) % 2][lag - 1]
+
+                @pl.when((t >= 0) & (t < tiles))
+                def _(t=t, stage=stage):
+                    stage(t)
+
+            @pl.when(s >= tiles)
+            def _():
+                finish(s - tiles)
 
         return carry
 
-    lax.fori_loop(0, tiles + 4, step, 0)
+    lax.fori_loop(0, (tiles + 4) // 2, pair, 0)
     for t in (tiles - 2, tiles - 1):
         core_copy(t).wait_send()
-        for j in range(1, near):
-            near_copy(t, j).wait_send()
-        if far_inside:
-            for j in range(1, far):
-                far_copy(t, j).wait_send()
-        x_copy(t).wait_send()
-    for p in range(4):
-        for copy in out_copies(p):
-            copy.wait()
-
-
-def channel(y, ec, w1, w2, b1, gain, bias, b2):
+    for copies in (a_near, a_far, a_x, b_near, b_far, b_x):
+        for i in (tiles // 2 - 2, tiles // 2 - 1):
+            for copy in copies(i):
+                copy.wait_send()
+    for n in range(count_l):
+        ey_copy(at_l(n), n).wait()
+        out_copy(n).wait()
+    for n in range(count_s):
+        ey_copy(at_s(n), count_l + n).wait()
+
+
+def channel(y, live, cot_l, cot_s, w1, w2, b1, gain, bias, b2):
     rows, width = y.shape
     hidden = w1.shape[1]
     tiles = hidden // TILE
@@ -349,36 +413,42 @@
     V = pltpu.VMEM
     DMA = pltpu.SemaphoreType.DMA
     fm = max(f - 1, 1)
+    nm = near - 1
+    pairs = tiles // 2
+    count = cot_l.shape[0] + cot_s.shape[0]
     return pl.pallas_call(
         functools.partial(channel_kernel, near, far, far_inside),
         out_shape=(
-            jax.ShapeDtypeStruct((rows, width), BF),
+            jax.ShapeDtypeStruct(cot_l.shape, BF),
             jax.ShapeDtypeStruct((rows, width), F32),
             jax.ShapeDtypeStruct((chunk, hidden), BF),
             jax.ShapeDtypeStruct((8, width), F32),
+            jax.ShapeDtypeStruct(cot_s.shape, BF),
         ),
-        in_specs=[ANY] * 4 + [vmem] * 4,
-        out_specs=(ANY, ANY, vmem, vmem),
+        in_specs=[ANY, pl.BlockSpec(memory_space=pltpu.SMEM), vmem, vmem, ANY, ANY] + [vmem] * 4,
+        out_specs=(ANY, ANY, vmem, vmem, vmem),
         scratch_shapes=[
             V((rows, width), F32), V((rows, width), BF), V((rows, width), BF),
             V((2, width, rows), BF), V((2, rows, TILE), BF),
             V((tiles, width, TILE), BF), V((tiles, TILE, width), BF),
-            V((rows, width), F32), V((rows, width), F32), V((rows, width), BF),
-            V((2, width, TILE), F32), V((2, width, TILE), BF), V((tiles, width, TILE), BF),
-            V((2, width // near, TILE), F32), V((2, near - 1, width // near, TILE), BF),
-            V((tiles, near - 1, width // near, TILE), BF),
-            V((2, chunk * 2, TILE), F32), V((2, fm, chunk * 2, TILE), BF), V((tiles, fm, chunk * 2, TILE), BF),
-            V((2, chunk, TILE), F32), V((2, chunk, TILE), BF), V((tiles, chunk, TILE), BF),
-            DMA((2,)), DMA((2, tiles)), DMA((2, 4)),
-            DMA((2,)), DMA((tiles,)),
-            DMA((2, near - 1)), DMA((tiles, near - 1)),
-            DMA((2, fm)), DMA((tiles, fm)),
-            DMA((2,)), DMA((tiles,)),
+            V((rows, width), F32), V((rows, width), F32), V(cot_l.shape, BF),
+            V((2, near, f, 2, chunk, TILE), F32), V((2, near, f, 2, chunk, TILE), BF),
+            V((tiles, near, f, 2, chunk, TILE), BF),
+            V((2, f, 2, chunk, TILE), F32), V((2, nm, f, 2, chunk, TILE), BF), V((pairs, nm, f, 2, chunk, TILE), BF),
+            V((2, 2, chunk, TILE), F32), V((2, fm, 2, chunk, TILE), BF), V((pairs, fm, 2, chunk, TILE), BF),
+            V((2, chunk, TILE), F32), V((2, 1, chunk, TILE), BF), V((pairs, 1, chunk, TILE), BF),
+            V((2, near, f, chunk, TILE), F32), V((2, 1, near, f, chunk, TILE), BF),
+            V((pairs, 1, near, f, chunk, TILE), BF),
+            V((2, f, chunk, TILE), F32), V((2, nm, f, chunk, TILE), BF), V((pairs, nm, f, chunk, TILE), BF),
+            V((2, chunk, TILE), F32), V((2, fm, chunk, TILE), BF), V((pairs, fm, chunk, TILE), BF),
+            DMA((1,)), DMA((2, tiles)), DMA((2 * count,)), DMA((2,)), DMA((tiles,)),
+            DMA((2, nm)), DMA((pairs, nm)), DMA((2, fm)), DMA((pairs, fm)), DMA((2, 1)), DMA((pairs, 1)),
+            DMA((2, nm)), DMA((pairs, nm)), DMA((2, fm)), DMA((pairs, fm)), DMA((2, 1)), DMA((pairs, 1)),
         ],
         compiler_params=pltpu.CompilerParams(
             collective_id=0, has_side_effects=True, vmem_limit_bytes=TOP
         ),
-    )(y, ec, w1, w2, b1.reshape(1, -1), gain.reshape(1, -1), bias.reshape(1, -1), b2.reshape(1, -1))
+    )(y, live, cot_l, cot_s, w1, w2, b1, gain, bias, b2)
 
 
 NT = (((1,), (1,)), ((), ()))
@@ -450,18 +520,25 @@
 
 def token_kernel(
     near, size,
-    xl, xs, wq_l, wq_s, b1_l, b1_s, b2_l, b2_s, gain_ref, bias_ref,
+    xl, xs, w1_l, w1_s, w2_l, w2_s, b1_l_ref, b1_s_ref, b2_l_ref, b2_s_ref, gain_ref, bias_ref,
     y_hbm, u_l, u_s, h_l, h_s, sl_l, sl_s, w_l, w_s,
-    tx_l, tx_s, w1t_l, w1t_s, m_l, m_s, rx_l, rx_s, y,
+    wq_l, wq_s, tx_l, tx_s, w1t_l, w1t_s, m_l, m_s, rx_l, rx_s, y,
     y_sem, own_sem, wown, w_ss, w_rs, out_ss_l, out_ss_s, out_rs_l, out_rs_s, bk_ss_l, bk_ss_s, bk_rs_l, bk_rs_s,
 ):
     peers = Peers(near)
     me = peers.blk
     count_l, patches_l, width = xl.shape
-    count_s, patches_s, _ = xs.shape
+    count_s, real_s, _ = xs.shape
+    patches_s = tx_s.shape[1]
+    token = w1_l.shape[1]
     half = width // 2
     per_l, per_s = count_l * 2 // size, count_s // size
     swap = Swap(peers, size, per_l, per_s, patches_l, patches_s)
+    wq_l[0] = w1_l[...]
+    wq_l[1] = w2_l[...].astype(F32).T.astype(BF)
+    wq_s[...] = jnp.zeros_like(wq_s)
+    wq_s[0, :real_s] = w1_s[...]
+    wq_s[1, :real_s] = w2_s[...].astype(F32).T.astype(BF)
 
     barrier = pltpu.get_barrier_semaphore()
     for j in range(1, size):
@@ -490,9 +567,11 @@
     for copy in own_w:
         copy.start()
 
-    def norm(row):
-        unit, _ = unit_rows(row.astype(F32))
-        return (unit * gain_ref[...] + bias_ref[...]).astype(BF)
+    gain, bias = row(gain_ref), row(bias_ref)
+
+    def norm(values):
+        unit, _ = unit_rows(values.astype(F32))
+        return (unit * gain + bias).astype(BF)
 
     def norm_l(n, carry):
         u = norm(xl[n])
@@ -500,8 +579,10 @@
         tx_l[2 * n + 1] = u[:, half:]
         return carry
 
+    tx_s[...] = jnp.zeros_like(tx_s)
+
     def norm_s(n, carry):
-        tx_s[n] = norm(xs[n])
+        tx_s[n, :real_s] = norm(xs[n])
         return carry
 
     lax.fori_loop(0, count_l, norm_l, 0)
@@ -525,6 +606,8 @@
         copy.wait()
     for copy in to_core + relay:
         copy.wait_recv()
+    b1_l, b1_s = column(b1_l_ref, token), column(b1_s_ref, token)
+    b2_l, b2_s = column(b2_l_ref, patches_l), column(b2_s_ref, real_s)
     w1t_l[...] = w_l[0].T
     w1t_s[...] = w_s[0].T
 
@@ -532,7 +615,7 @@
         for k in range(1, size):
             source = swap.other(k)
             swap.out(kind, j, me, source, tx, cols, *outs).wait_recv()
-        g, d = gelu_pair(matmul(w1t[...], cols[j]) + b1[...])
+        g, d = gelu_pair(matmul(w1t[...], cols[j]) + b1)
         low = g.astype(BF)
         h[j] = low
         slope[j] = d.astype(BF)
@@ -550,6 +633,7 @@
     small_rows = count_s * patches_s
     rows = y.shape[0]
     used = small_rows + count_l * patches_l
+    y[0:small_rows, :] = jnp.zeros((small_rows, width), F32)
     if rows > used:
         y[used:rows, :] = jnp.zeros((rows - used, width), F32)
 
@@ -565,14 +649,14 @@
         arrived("l", 2 * n, m_l, rx_l, bk_ss_l, bk_rs_l)
         arrived("l", 2 * n + 1, m_l, rx_l, bk_ss_l, bk_rs_l)
         at = pl.ds(pl.multiple_of(small_rows + n * patches_l, 16), patches_l)
-        y[at, :half] = xl[n, :, :half].astype(F32) + rx_l[2 * n].astype(F32) + b2_l[...]
-        y[at, half:] = xl[n, :, half:].astype(F32) + rx_l[2 * n + 1].astype(F32) + b2_l[...]
+        y[at, :half] = xl[n, :, :half].astype(F32) + rx_l[2 * n].astype(F32) + b2_l
+        y[at, half:] = xl[n, :, half:].astype(F32) + rx_l[2 * n + 1].astype(F32) + b2_l
         return carry
 
     def home_s(n, carry):
         arrived("s", n, m_s, rx_s, bk_ss_s, bk_rs_s)
-        at = pl.ds(pl.multiple_of(n * patches_s, 16), patches_s)
-        y[at, :] = xs[n].astype(F32) + rx_s[n].astype(F32) + b2_s[...]
+        at = pl.ds(pl.multiple_of(n * patches_s, 16), real_s)
+        y[at, :] = xs[n].astype(F32) + rx_s[n, :real_s].astype(F32) + b2_s
         return carry
 
     lax.fori_loop(0, count_l, home_l, 0)
@@ -592,12 +676,13 @@
     y_out.wait()
 
 
-def token_forward(xl, xs, wq_l, wq_s, b1_l, b1_s, b2_l, b2_s, gain, bias, rows):
+def token_forward(xl, xs, w1_l, w1_s, w2_l, w2_s, b1_l, b1_s, b2_l, b2_s, gain, bias, rows):
     size = lax.axis_size("blk")
     near, far = img_split(lax.axis_size("img"))
     count_l, patches_l, width = xl.shape
     count_s, patches_s, _ = xs.shape
-    token = wq_l.shape[2]
+    patches_s += -patches_s % 64
+    token = w1_l.shape[1]
     half = width // 2
     per_l, per_s = count_l * 2 // size, count_s // size
     vmem = pl.BlockSpec(memory_space=pltpu.VMEM)
@@ -613,9 +698,10 @@
             low(per_l, token, half), low(per_s, token, width),
             low(2, size * patches_l, token), low(2, size * patches_s, token),
         ),
-        in_specs=[vmem] * 10,
+        in_specs=[vmem] * 12,
         out_specs=(ANY,) + (vmem,) * 8,
         scratch_shapes=[
+            V((2, patches_l, token), BF), V((2, patches_s, token), BF),
             V((count_l * 2, patches_l, half), BF), V((count_s, patches_s, width), BF),
             V((token, size * patches_l), BF), V((token, size * patches_s), BF),
             V((per_l, size * patches_l, half), BF), V((per_s, size * patches_s, width), BF),
@@ -628,20 +714,18 @@
         compiler_params=pltpu.CompilerParams(
             collective_id=2, has_side_effects=True, vmem_limit_bytes=TOP
         ),
-    )(
-        xl, xs, wq_l, wq_s, b1_l.reshape(-1, 1), b1_s.reshape(-1, 1), b2_l.reshape(-1, 1), b2_s.reshape(-1, 1),
-        gain.reshape(1, -1), bias.reshape(1, -1),
-    )
-
-
-GROUPS = 6
+    )(xl, xs, w1_l, w1_s, w2_l, w2_s, b1_l, b1_s, b2_l, b2_s, gain, bias)
+
+
+GROUPS = 12
+DEPTH = 3
 SLAB = 512
 
 
 def backward_kernel(
     near, far, size, far_inside,
     chunk_hbm, ey_hbm, xl, xs, u_l, u_s, h_l, h_s, sl_l, sl_s, w_l, w_s, small_in, gain_ref,
-    full_hbm, gx_hbm, tok_out, vec_out,
+    full_hbm, gx_hbm, tok_out, vec_out, gx_s,
     ey, tx_l, tx_s, e_l, e_s, w2_l, w2_s, ep_l, ep_s, eu_l, eu_s, rx_l, rx_s,
     grads, tok_tx, tok_rx, tokx_tx, tokx_rx, tok_sum, tokn_tx, tokn_rx, tok_half, tokf_tx, tokf_rx,
     vec, vec_rx, vecn_rx, vecf_rx,
@@ -654,8 +738,10 @@
     peers = Peers(near)
     me = peers.blk
     count_l, patches_l, width = xl.shape
-    count_s, patches_s, _ = xs.shape
+    count_s, real_s, _ = xs.shape
+    patches_s = tx_s.shape[1]
     token = w_l.shape[2]
+    gain = row(gain_ref)
     half = width // 2
     per_l, per_s = count_l * 2 // size, count_s // size
     swap = Swap(peers, size, per_l, per_s, patches_l, patches_s)
@@ -705,16 +791,26 @@
         span = block(0, each * 2 * f * near, k)
         return send(span, span, gc_ss.at[k], gc_rs.at[k], core_peer)
 
-    def tick_near(k):
+    def g_open(k):
+        if k < GROUPS:
+            g_own(k).wait()
+            g_x(k).wait_recv()
+            for copy in g_far(k):
+                copy.start()
+
+    def g_close(k):
+        for copy in g_near(k):
+            copy.wait_recv()
+        g_core(k).start()
+
+    def tick(k):
         for copy in g_far(k):
             copy.wait_recv()
         for copy in g_near(k):
             copy.start()
-
-    def tick_core(k):
-        for copy in g_near(k):
-            copy.wait_recv()
-        g_core(k).start()
+        g_open(k + DEPTH)
+        if k >= 1:
+            g_close(k - 1)
 
     ey_in = pltpu.make_async_copy(ey_hbm, ey, ey_sem.at[0])
     ey_in.start()
@@ -756,13 +852,8 @@
         e_s[j, swap.rows(me, patches_s)] = tx_s[me * per_s + j]
     w2_l[...] = w_l[1].T
     w2_s[...] = w_s[1].T
-    for k in range(GROUPS):
-        g_own(k).wait()
-        g_x(k).wait_recv()
-        for copy in g_far(k):
-            copy.start()
-        if not far_inside:
-            tick_near(k)
+    for k in range(DEPTH):
+        g_open(k)
 
     def unmix(kind, j, e, w2, w1, slope, ep, eu, outs, tx, rx, bss, brs):
         for k in range(1, size):
@@ -777,10 +868,10 @@
 
     for j in range(per_l):
         unmix("l", j, e_l, w2_l, w_l[0], sl_l, ep_l, eu_l, (out_ss_l, out_rs_l), tx_l, rx_l, bk_ss_l, bk_rs_l)
+        tick(j)
     for j in range(per_s):
         unmix("s", j, e_s, w2_s, w_s[0], sl_s, ep_s, eu_s, (out_ss_s, out_rs_s), tx_s, rx_s, bk_ss_s, bk_rs_s)
-    if far_inside:
-        tick_near(0)
+    tick(3)
 
     ones_l = jnp.ones((8, half), BF)
     vec[8:16, 0:half] = sum(matmul_nt(ones_l, ep_l[j]) for j in range(per_l))
@@ -802,15 +893,15 @@
         tok_tx[p] = grads[p * 2 + 1 - peers.core].astype(BF)
     t_core = send(tok_tx, tok_rx, tc_ss.at[0], tc_rs.at[0], core_peer)
     t_core.start()
-    if far_inside:
-        tick_near(1)
+    tick(4)
     t_core.wait_recv()
     there = 1 - peers.x
     tokx_tx[...] = (grads[there * 2 + peers.core] + tok_rx[there].astype(F32)).astype(BF)
     t_x = send(tokx_tx, tokx_rx, tx_ss.at[0], tx_rs.at[0], x_peer)
     t_x.start()
     tok_sum[...] = grads[me] + tok_rx[peers.x].astype(F32)
-    tick_core(0)
+    tick(5)
+    tick(6)
 
     def arrived(kind, unit, eu, rx, bss, brs):
         per = per_l if kind == "l" else per_s
@@ -822,42 +913,47 @@
 
     def norm_back(x, eu, at):
         unit, scale = unit_rows(x.astype(F32))
-        d = eu * gain_ref[...]
+        d = eu * gain
         m1 = jnp.mean(d, axis=-1, keepdims=True)
         m2 = jnp.mean(d * unit, axis=-1, keepdims=True)
-        ey[at, :] += scale * (d - m1 - unit * m2)
         vec[7:8, :] += jnp.sum(eu * unit, axis=0, keepdims=True)
-        return jnp.sum(eu, axis=0, keepdims=True)
-
-    def home_l(n, total):
+        vec[9:10, :] += jnp.sum(eu, axis=0, keepdims=True)
+        return ey[at, :] + scale * (d - m1 - unit * m2)
+
+    def gx_copy(n):
+        at = pl.ds(pl.multiple_of(small_rows + n * patches_l, 16), patches_l)
+        return pltpu.make_async_copy(ey.at[at], gx_hbm.at[n], gx_sem.at[n])
+
+    def home_l(n, carry):
         arrived("l", 2 * n, eu_l, rx_l, bk_ss_l, bk_rs_l)
         arrived("l", 2 * n + 1, eu_l, rx_l, bk_ss_l, bk_rs_l)
         at = pl.ds(pl.multiple_of(small_rows + n * patches_l, 16), patches_l)
         eu = jnp.concatenate([rx_l[2 * n], rx_l[2 * n + 1]], axis=1).astype(F32)
-        return total + norm_back(xl[n], eu, at)
-
-    def home_s(n, total):
+        ey[at, :] = norm_back(xl[n], eu, at)
+        gx_copy(n).start()
+        return carry
+
+    def home_s(n, carry):
         arrived("s", n, eu_s, rx_s, bk_ss_s, bk_rs_s)
-        at = pl.ds(pl.multiple_of(n * patches_s, 16), patches_s)
-        eu = rx_s[n].astype(F32)
-        return total + norm_back(xs[n], eu, at)
-
-    total = lax.fori_loop(0, count_l, home_l, jnp.zeros((1, width), F32))
-    total = lax.fori_loop(0, count_s, home_s, total)
-    vec[9:10, :] = total
-    gx_out = pltpu.make_async_copy(ey, gx_hbm, gx_sem.at[0])
-    gx_out.start()
+        at = pl.ds(pl.multiple_of(n * patches_s, 16), real_s)
+        gx_s[n] = norm_back(xs[n], rx_s[n, :real_s].astype(F32), at)
+        return carry
+
+    vec[9:10, :] = jnp.zeros((1, width), F32)
+    lax.fori_loop(0, count_l // 2, home_l, 0)
+    tick(7)
+    lax.fori_loop(count_l // 2, count_l, home_l, 0)
+    tick(8)
+    lax.fori_loop(0, count_s, home_s, 0)
 
     both = vec.at[0:16]
     v_core = send(both, vec_rx.at[0], v_ss.at[0], v_rs.at[0], core_peer)
     v_core.start()
-    if far_inside:
-        tick_near(2)
-    tick_core(1)
     t_x.wait_recv()
     tok_sum[...] += tokx_rx[...].astype(F32)
-    t_near = []
     part_n = SLAB // near
+    part_f = part_n // far
+    t_near, t_far, ta_far, ta_near = [], [], [], []
     if far_inside:
         for j, device in near_peers:
             at = pl.ds(pl.multiple_of(lax.rem(peers.near + j, near) * part_n, part_n), part_n)
@@ -871,11 +967,12 @@
     vec[0:16, :] += vec_rx[0]
     v_x = send(both, vec_rx.at[1], v_ss.at[1], v_rs.at[1], x_peer)
     v_x.start()
-    if far_inside:
-        tick_near(3)
-    tick_core(2)
-    t_far = []
-    part_f = part_n // far
+    tick(9)
+    v_x.wait()
+    vec[0:16, :] += vec_rx[1]
+    v_near = [send(vec, vecn_rx.at[j - 1], vn_ss.at[j - 1], vn_rs.at[j - 1], device) for j, device in near_peers]
+    for copy in v_near:
+        copy.start()
     if far_inside:
         for copy in t_near:
             copy.wait_recv()
@@ -889,15 +986,14 @@
             copy = send(tokf_tx.at[j - 1], tokf_rx.at[j - 1], tf_ss.at[j - 1], tf_rs.at[j - 1], device)
             copy.start()
             t_far.append(copy)
-    v_x.wait()
-    vec[0:16, :] += vec_rx[1]
-    v_near = [send(vec, vecn_rx.at[j - 1], vn_ss.at[j - 1], vn_rs.at[j - 1], device) for j, device in near_peers]
+    tick(10)
     for copy in v_near:
+        copy.wait()
+    for j in range(near - 1):
+        vec[...] += vecn_rx[j]
+    v_far = [send(vec, vecf_rx.at[j - 1], vf_ss.at[j - 1], vf_rs.at[j - 1], device) for j, device in far_peers]
+    for copy in v_far:
         copy.start()
-    if far_inside:
-        tick_near(4)
-    tick_core(3)
-    ta_far = []
     if far_inside:
         for copy in t_far:
             copy.wait_recv()
@@ -910,14 +1006,13 @@
             copy = send(span, span, taf_ss.at[j - 1], taf_rs.at[j - 1], device)
             copy.start()
             ta_far.append(copy)
-    for copy in v_near:
+    tick(11)
+    for copy in v_far:
         copy.wait()
-    for j in range(near - 1):
-        vec[...] += vecn_rx[j]
-    v_far = [send(vec, vecf_rx.at[j - 1], vf_ss.at[j - 1], vf_rs.at[j - 1], device) for j, device in far_peers]
-    for copy in v_far:
-        copy.start()
-    ta_near = []
+    value = vec[...]
+    for j in range(far - 1):
+        value = value + vecf_rx[j]
+    vec_out[...] = value
     if far_inside:
         for copy in ta_far:
             copy.wait_recv()
@@ -926,17 +1021,9 @@
             copy = send(span, span, tan_ss.at[j - 1], tan_rs.at[j - 1], device)
             copy.start()
             ta_near.append(copy)
-        tick_near(5)
-    tick_core(4)
-    for copy in v_far:
-        copy.wait()
-    value = vec[...]
-    for j in range(far - 1):
-        value = value + vecf_rx[j]
-    vec_out[...] = value
+    g_close(GROUPS - 1)
     for copy in ta_near:
         copy.wait_recv()
-    tick_core(5)
 
     for copy in [t_core, t_x] + t_near + t_far + ta_far + ta_near:
         copy.wait_send()
@@ -953,7 +1040,8 @@
         for copy in g_far(k) + g_near(k):
             copy.wait_send()
         g_core(k).wait()
-    gx_out.wait()
+    for n in range(count_l):
+        gx_copy(n).wait()
 
 
 def backward(chunk, ey, xl, xs, saved, small, gain):
@@ -964,6 +1052,7 @@
     u_l, u_s, h_l, h_s, sl_l, sl_s, w_l, w_s = saved
     count_l, patches_l, _ = xl.shape
     count_s, patches_s, _ = xs.shape
+    patches_s += -patches_s % 64
     token = w_l.shape[2]
     half = width // 2
     per_l, per_s = u_l.shape[0], u_s.shape[0]
@@ -978,12 +1067,13 @@
         functools.partial(backward_kernel, near, far, size, far_inside),
         out_shape=(
             jax.ShapeDtypeStruct((2, width, hidden), BF),
-            jax.ShapeDtypeStruct((rows, width), F32),
+            jax.ShapeDtypeStruct(xl.shape, F32),
             jax.ShapeDtypeStruct((SLAB, token), BF),
             jax.ShapeDtypeStruct((24, width), F32),
+            jax.ShapeDtypeStruct(xs.shape, F32),
         ),
         in_specs=[ANY, ANY] + [vmem] * 12,
-        out_specs=(ANY, ANY, vmem, vmem),
+        out_specs=(ANY, ANY, vmem, vmem, vmem),
         scratch_shapes=[
             V((rows, width), F32),
             V((count_l * 2, patches_l, half), BF), V((count_s, patches_s, width), BF),
@@ -996,7 +1086,7 @@
             V((n1, part_n, token), BF), V((n1, part_n, token), BF), V((part_n, token), F32),
             V((f1, part_f, token), BF), V((f1, part_f, token), BF),
             V((24, width), F32), V((2, 16, width), F32), V((n1, 24, width), F32), V((f1, 24, width), F32),
-            DMA((1,)), DMA((1,)),
+            DMA((1,)), DMA((count_l,)),
             DMA((GROUPS,)), DMA((GROUPS,)), DMA((GROUPS,)), DMA((GROUPS, f1)), DMA((GROUPS, f1)),
             DMA((GROUPS, n1)), DMA((GROUPS, n1)), DMA((GROUPS,)), DMA((GROUPS,)),
             DMA((count_l * 2,)), DMA((count_s,)), DMA((per_l, size)), DMA((per_s, size)),
@@ -1008,28 +1098,68 @@
         compiler_params=pltpu.CompilerParams(
             collective_id=1, has_side_effects=True, vmem_limit_bytes=TOP
         ),
-    )(chunk, ey, xl, xs, u_l, u_s, h_l, h_s, sl_l, sl_s, w_l, w_s, small, gain.reshape(1, -1))
-
-
-def widen_kernel(first, second, out_first, out_second):
+    )(chunk, ey, xl, xs, u_l, u_s, h_l, h_s, sl_l, sl_s, w_l, w_s, small, gain)
+
+
+def widen_kernel(
+    first, second, tok, vec,
+    out_first, out_second, gain1, bias1, w1_s, b1_s, w2_s, b2_s, w1_l, b1_l, w2_l, b2_l, gain2, bias2, b1, b2,
+):
     out_first[...] = first[0].astype(F32)
     out_second[...] = second[0].astype(F32).T
 
-
-def widen(full):
+    @pl.when(pl.program_id(0) == 0)
+    def _():
+        width = vec.shape[1]
+        half = width // 2
+        large, small = w1_l.shape[0], w1_s.shape[0]
+        wide = small + -small % 64
+        at = 2 * large
+        w1_l[...] = tok[0:large, :].astype(F32)
+        w2_l[...] = tok[large:at, :].astype(F32).T
+        w1_s[...] = tok[at:at + wide, :].astype(F32)[:small]
+        w2_s[...] = tok[at + wide:at + 2 * wide, :].astype(F32).T[:, :small]
+        gain1[...] = vec[7, :]
+        bias1[...] = vec[9, :]
+        b1_l[...] = vec[8, 0:half]
+        b1_s[...] = vec[8, half:width]
+        b2_l[...] = vec[16, 0:large]
+        b2_s[...] = vec[16, half:half + small]
+        gain2[...] = vec[5, :]
+        bias2[...] = vec[6, :]
+        for k in range(b1.shape[0] // width):
+            b1[k * width:(k + 1) * width] = vec[k, :]
+        b2[...] = vec[4, :]
+
+
+def widen(full, tok, vec, patches_s, patches_l):
     _, width, hidden = full.shape
+    token = tok.shape[1]
     step = 384
+    shapes = (
+        (width,), (width,), (patches_s, token), (token,), (token, patches_s), (patches_s,),
+        (patches_l, token), (token,), (token, patches_l), (patches_l,), (width,), (width,), (hidden,), (width,),
+    )
+
+    def whole(shape):
+        return pl.BlockSpec(shape, lambda i: (0,) * len(shape))
+
     return pl.pallas_call(
         widen_kernel,
         grid=(hidden // step,),
-        out_shape=(jax.ShapeDtypeStruct((width, hidden), F32), jax.ShapeDtypeStruct((hidden, width), F32)),
+        out_shape=(
+            jax.ShapeDtypeStruct((width, hidden), F32), jax.ShapeDtypeStruct((hidden, width), F32),
+        ) + tuple(jax.ShapeDtypeStruct(shape, F32) for shape in shapes),
         in_specs=[
             pl.BlockSpec((1, width, step), lambda i: (0, 0, i)),
             pl.BlockSpec((1, width, step), lambda i: (1, 0, i)),
+            whole(tok.shape), whole(vec.shape),
         ],
-        out_specs=(pl.BlockSpec((width, step), lambda i: (0, i)), pl.BlockSpec((step, width), lambda i: (i, 0))),
+        out_specs=(
+            pl.BlockSpec((width, step), lambda i: (0, i)), pl.BlockSpec((step, width), lambda i: (i, 0)),
+        ) + tuple(whole(shape) for shape in shapes),
         compiler_params=pltpu.CompilerParams(vmem_limit_bytes=TOP),
-    )(full, full)
+    )(full, full, tok, vec)
 
 
 def local(
@@ -1039,58 +1169,33 @@
     ln2_gain, ln2_bias, ch_w1, ch_b1, ch_w2, ch_b2, cot_small, cot_large,
 ):
     width = x_small.shape[2]
-    token = tok_w1_large.shape[1]
     patches_s, patches_l = x_small.shape[1], x_large.shape[1]
-    extra = -patches_s % 64
-    wide_s = patches_s + extra
-    small_rows = x_small.shape[0] * wide_s
-    large_rows = x_large.shape[0] * patches_l
-    rows = small_rows + large_rows
-    spare = -rows % (3 * LANES)
-
-    def widen_small(small):
-        return jnp.pad(small, ((0, 0), (0, extra), (0, 0)))
-
-    def part(joined):
-        small = joined[:small_rows].reshape(x_small.shape[0], wide_s, width)[:, :patches_s]
-        return small, joined[small_rows:rows].reshape(x_large.shape)
-
-    mask_small = (jnp.arange(x_small.shape[0]) < live_counts[0, 0]).astype(BF)[:, None, None]
-    mask_large = (jnp.arange(x_large.shape[0]) < live_counts[0, 1]).astype(BF)[:, None, None]
-    xs = widen_small(x_small)
-    wq_l = jnp.stack([tok_w1_large, tok_w2_large.T])
-    wq_s = widen_small(jnp.stack([tok_w1_small, tok_w2_small.T]))
+    rows = x_small.shape[0] * (patches_s + -patches_s % 64) + x_large.shape[0] * patches_l
     y, *saved = token_forward(
-        x_large, xs, wq_l, wq_s, tok_b1_large, tok_b1_small, tok_b2_large, jnp.pad(tok_b2_small, (0, extra)),
-        ln1_gain, ln1_bias, rows + spare,
+        x_large, x_small, tok_w1_large, tok_w1_small, tok_w2_large, tok_w2_small,
+        tok_b1_large, tok_b1_small, tok_b2_large, tok_b2_small, ln1_gain, ln1_bias, rows + -rows % (3 * LANES),
     )
-    ec = jnp.concatenate([
-        widen_small(cot_small * mask_small).reshape(-1, width),
-        (cot_large * mask_large).reshape(-1, width),
-        jnp.zeros((spare, width), BF),
-    ])
-    out, ey, chunk, small_grads = channel(y, ec, ch_w1, ch_w2, ch_b1, ln2_gain, ln2_bias, ch_b2)
+    out_large, ey, chunk, small_grads, out_small = channel(
+        y, live_counts, cot_large, cot_small, ch_w1, ch_w2, ch_b1, ln2_gain, ln2_bias, ch_b2
+    )
     near, far = img_split(lax.axis_size("img"))
     far_inside = width % (near * far * 2 * 16) == 0
     if not far_inside:
         same = [[a * near + b for a in range(far)] for b in range(near)]
         chunk = lax.psum(chunk.astype(F32), "img", axis_index_groups=same).astype(BF)
-    full, gx, tok, vec = backward(chunk, ey, x_large, xs, saved, small_grads, ln1_gain)
-    tok = tok.astype(F32)
+    full, gx_large, tok, vec, gx_small = backward(
+        chunk, ey, x_large, x_small, saved, small_grads, ln1_gain
+    )
     if not far_inside:
-        tok = lax.psum(tok, "img")
-    grad_ch_w1, grad_ch_w2 = widen(full)
-    out_small, out_large = part(out)
-    gx_small, gx_large = part(gx)
-    half = width // 2
-    b2_l = vec[16, :patches_l]
-    b2_s = vec[16, half:half + patches_s]
-    at = 2 * patches_l
+        tok = lax.psum(tok.astype(F32), "img")
+    (
+        grad_ch_w1, grad_ch_w2, gain1, bias1, w1_s, b1_s, w2_s, b2_s, w1_l, b1_l, w2_l, b2_l,
+        gain2, bias2, grad_b1, grad_b2,
+    ) = widen(full, tok, vec, patches_s, patches_l)
     return (
-        out_small * mask_small, out_large * mask_large, gx_small, gx_large, vec[7], vec[9],
-        tok[at:at + patches_s], vec[8, half:], tok[at + wide_s:at + wide_s + patches_s].T, b2_s,
-        tok[:patches_l], vec[8, :half], tok[patches_l:at].T, b2_l,
-        vec[5], vec[6], grad_ch_w1, vec[:4].reshape(-1), grad_ch_w2, vec[4],
+        out_small, out_large, gx_small, gx_large, gain1, bias1,
+        w1_s, b1_s, w2_s, b2_s, w1_l, b1_l, w2_l, b2_l,
+        gain2, bias2, grad_ch_w1, grad_b1, grad_ch_w2, grad_b2,
     )
 
 

time: 304 us -> 277 us (0.911)
  local copies, waits for them, and re-layouts: 32 us -> 18.3 us
  other arithmetic: 10.6 us -> 0 us
    unnamed x9 -> x12, local copies, waits for them, and re-layouts: 1.14 us -> 18.3 us
    slice x13 -> x0, local copies, waits for them, and re-layouts: 14.7 us -> none  [the longest x2 3.08 us: part(): return (small, joined[small_rows:rows].reshape(x_large.shape))]
    reshape x11 -> x0, local copies, waits for them, and re-layouts: 12.7 us -> none  [the longest x1 1.47 us: token_forward(): b1_s.reshape(-1, 1)]
    pallas_call x1, Pallas kernels: 101 us -> 90.8 us  [backward(): pl.pallas_call(functools.partial(backward_kernel, near, far, size, far_in...]
    pallas_call x1, Pallas kernels: 93.7 us -> 101 us  [channel(): pl.pallas_call(functools.partial(channel_kernel, near, far, far_inside),...]
    mul x4 -> x0, other arithmetic: 3.55 us -> none  [the longest x1 1.26 us: local(): cot_small * mask_small]
    another operation x2 -> x0, other arithmetic: 3.12 us -> none  [the longest x1 1.66 us: local(): wq_l = jnp.stack([tok_w1_large, tok_w2_large.T])]
where the time goes in v4:
time: 277 us; the launch traced here: 276 us
  Pallas kernels  257 us (93%)
  local copies, waits for them, and re-layouts  18.3 us (7%)
    pallas_call x1, Pallas kernels, channel(): pl.pallas_call(functools.partial(channel_kernel, near, far, far_inside),...  101 us
    pallas_call x1, Pallas kernels, backward(): pl.pallas_call(functools.partial(backward_kernel, near, far, size, far_in...  90.8 us
    pallas_call x1, Pallas kernels, token_forward(): pl.pallas_call(functools.partial(token_kernel, near, size), out_shape=(ja...  52.9 us
    unnamed x12, local copies, waits for them, and re-layouts  18.3 us
    pallas_call x1, Pallas kernels, widen(): pl.pallas_call(widen_kernel, grid=(hidden // step,), out_shape=(jax.Shape...  12 us

profile of v4, /device:TPU:0, one launch (start us, length us, event | category | flops | bytes accessed | tf_op | source)
XLA Modules:
  0.0 276.1 jit_solution(10588302215378636445)
XLA Ops:
  0.7 1.5 copy.43.w2_s
  2.2 1.7 copy.42.w2_l
  3.9 1.7 copy.41.xs
  5.6 1.7 copy.44.cot_s
  7.4 52.9 %shard_map.356 = (f32[1152,768]{1,0:T(8,128)}, bf16[3,576,384]{2,1,0:T(8,128)(2,1)}, bf16[1,256,768]{2,1,0:T(8,128)(2,1)}, bf16[3,384,384]{2,1,0:T(8,128)(2,1)},...) custom-call(bf16[6,144,768]{2,1,0:T(8,128)(2,1)} %xl.3, ...), custom_call_target="tpu_custom_call" | custom-call | tf_op jit(solution)/shard_map/pallas_call | solution.py:692
  60.3 101.4 %shard_map.357 = (bf16[6,144,768]{2,1,0:T(8,128)(2,1)}, f32[1152,768]{1,0:T(8,128)}, bf16[48,3072]{1,0:T(8,128)(2,1)}, f32[8,768]{1,0:T(8,128)}, bf16[4,49,768]{2,1,0:T(8,128)(2,1)}) custom-call(f32[1152,768]{1,0:T(8,128)} %get-tuple-element.55.y_hbm, s32[1,2]{1,0:T(1,128)} %live.1, bf16[6,144,768]{2,1,0:T(8,128)(2,1)} %cot_l.1, ...), custom_call_target="tpu_custom_call" | custom-call | tf_op jit(solution)/shard_map/pallas_call | solution.py:419
  161.7 1.8 copy.46
  163.5 90.8 %shard_map.358 = (bf16[2,768,3072]{2,1,0:T(8,128)(2,1)}, f32[6,144,768]{2,1,0:T(8,128)}, bf16[512,384]{1,0:T(8,128)(2,1)}, f32[24,768]{1,0:T(8,128)}, f32[4,49,768]{2,1,0:T(8,128)}) custom-call(bf16[48,3072]{1,0:T(8,128)(2,1)} %get-tuple-element.58.chunk_hbm, f32[1152,768]{1,0:T(8,128)} %get-tuple-element.59.ey_hbm, bf16[6,144,768]{2,1,0:T(8,128)(2,1)} %xl.3, ...), custom_call_target="tpu_custom_call" | custom-call | tf_op jit(solution)/shard_map/pallas_call | solution.py:1066
  254.3 2.2 copy.47
  256.4 12.0 %shard_map.359 = (f32[768,3072]{1,0:T(8,128)}, f32[3072,768]{1,0:T(8,128)}, f32[768]{0:T(1024)}, f32[768]{0:T(1024)}, f32[49,384]{1,0:T(8,128)}, /*index=5*/f32[...) custom-call(bf16[2,768,3072]{2,1,0:T(8,128)(2,1)} %get-tuple-element, ...), custom_call_target="tpu_custom_call" | custom-call | tf_op jit(solution)/shard_map/pallas_call | solution.py:1147
  268.5 0.0 copy-start
  268.5 1.8 copy.48
  270.3 1.8 copy.49
  272.1 2.5 copy.52
  274.6 0.0 copy-done
  274.6 1.5 copy.53
Async XLA Ops:
  268.5 6.1 %copy-start = (f32[6,144,768]{2,1,0:T(8,128)S(1)}, f32[6,144,768]{2,1,0:T(8,128)}, u32[]{:S(2)}) copy-start(f32[6,144,768]{2,1,0:T(8,128)} %get-tuple-element.133) | copy-start | bytes 7962628

commit v5 on v4

--- a/solution.py
+++ b/solution.py
@@ -16,6 +16,7 @@
 MESH = pl.DeviceIdType.MESH
 ANY = pl.BlockSpec(memory_space=pl.ANY)
 TILE = 256
+LAGS = (1, 3, 5, 7)
 TOP = 62 * 1024 * 1024
 
 
@@ -67,6 +68,89 @@
     pl.semaphore_wait(barrier, total)
 
 
+class Gather:
+    def __init__(self, peers, near, far, far_inside, chunk, full, sems):
+        self.peers, self.near, self.far, self.far_inside = peers, near, far, far_inside
+        self.chunk, self.full = chunk, full
+        self.each = each = chunk.shape[1]
+        self.f = far if far_inside else 1
+        self.own_sem, self.x_ss, self.x_rs, self.f_ss, self.f_rs, self.n_ss, self.n_rs, self.c_ss, self.c_rs = sems
+        self.base_n = peers.near * (each * 2 * self.f)
+        self.base_f = self.base_n + (peers.far if far_inside else 0) * (each * 2)
+        self.base_x = self.base_f + peers.x * each
+
+    def block(self, start, rows, k):
+        return self.full.at[self.peers.core, k, pl.ds(pl.multiple_of(start, self.each), rows)]
+
+    def send(self, src, dst, ss, rs, device):
+        return pltpu.make_async_remote_copy(
+            src_ref=src, dst_ref=dst, send_sem=ss, recv_sem=rs, device_id=device, device_id_type=MESH
+        )
+
+    def own(self, k):
+        return pltpu.make_async_copy(self.chunk.at[k], self.block(self.base_x, self.each, k), self.own_sem.at[k])
+
+    def to_x(self, k):
+        there = self.peers.at("x", 1 - self.peers.x)
+        return self.send(
+            self.chunk.at[k], self.block(self.base_x, self.each, k), self.x_ss.at[k], self.x_rs.at[k], there
+        )
+
+    def spread(self, axis, count, span, ss, rs, k):
+        copies = []
+        for j in range(1, count):
+            there = self.peers.at(axis, lax.rem(self.peers.mine(axis) + j, count))
+            copies.append(self.send(span, span, ss.at[k, j - 1], rs.at[k, j - 1], there))
+        return copies
+
+    def to_far(self, k):
+        return self.spread("far", self.f, self.block(self.base_f, self.each * 2, k), self.f_ss, self.f_rs, k)
+
+    def to_near(self, k):
+        return self.spread(
+            "near", self.near, self.block(self.base_n, self.each * 2 * self.f, k), self.n_ss, self.n_rs, k
+        )
+
+    def to_core(self, k):
+        span = self.block(0, self.each * 2 * self.f * self.near, k)
+        return self.send(span, span, self.c_ss.at[k], self.c_rs.at[k], self.peers.at("core", 1 - self.peers.core))
+
+    def first(self, k):
+        self.to_x(k).start()
+        self.own(k).start()
+
+    def second(self, k, begun):
+        if not begun:
+            self.own(k).wait()
+            self.to_x(k).wait_recv()
+        for copy in self.to_far(k):
+            copy.start()
+
+    def third(self, k):
+        for copy in self.to_far(k):
+            copy.wait_recv()
+        for copy in self.to_near(k):
+            copy.start()
+
+    def fourth(self, k):
+        for copy in self.to_near(k):
+            copy.wait_recv()
+        self.to_core(k).start()
+
+    def drain(self, k, begun):
+        if not begun:
+            self.to_x(k).wait_send()
+        for copy in self.to_far(k) + self.to_near(k):
+            copy.wait_send()
+        self.to_core(k).wait()
+
+    @staticmethod
+    def sems(groups, near, far):
+        DMA = pltpu.SemaphoreType.DMA
+        n1, f1 = near - 1, max(far - 1, 1)
+        return [DMA((groups,))] * 3 + [DMA((groups, f1))] * 2 + [DMA((groups, n1))] * 2 + [DMA((groups,))] * 2
+
+
 def row(ref):
     return ref[...].reshape(1, -1)
 
@@ -79,14 +163,14 @@
 def channel_kernel(
     near, far, far_inside,
     y_hbm, live, cot_l, cot_s, w1_hbm, w2_hbm, b1_ref, gain_ref, bias_ref, b2_ref,
-    out_l, ey_hbm, chunk_ref, small_ref, out_s,
+    out_l, ey_hbm, chunk_ref, small_ref, out_s, full_hbm,
     y, ec, v, lt, rt, w1, w2, acc_out, acc_ev, out_low,
     keep, core_tx, core_rx,
     a_keep_n, a_near_tx, a_near_rx, a_keep_f, a_far_tx, a_far_rx, a_keep_x, a_x_tx, a_x_rx,
     b_keep_x, b_x_tx, b_x_rx, b_keep_n, b_near_tx, b_near_rx, b_keep_f, b_far_tx, b_far_rx,
     in_sem, w_sem, out_sem, core_ss, core_rs,
     a_near_ss, a_near_rs, a_far_ss, a_far_rs, a_x_ss, a_x_rs,
-    b_near_ss, b_near_rs, b_far_ss, b_far_rs, b_x_ss, b_x_rs,
+    b_near_ss, b_near_rs, b_far_ss, b_far_rs, b_x_ss, b_x_rs, *gather_sems,
 ):
     rows, width = y.shape
     tiles = w1.shape[0]
@@ -97,6 +181,7 @@
     peers = Peers(near)
     core = peers.core
     f_place = peers.far if far_inside else 0
+    gather = Gather(peers, near, far, far_inside, chunk_ref, full_hbm, gather_sems)
     part = 128
     parts = rows // part
     gain, bias, b2 = row(gain_ref), row(bias_ref), row(b2_ref)
@@ -190,6 +275,12 @@
     def tile_step(t):
         for copy in w_copies(t):
             copy.wait()
+
+        @pl.when(t >= 2)
+        def _():
+            core_copy(t - 2).wait_send()
+
+        slot = lax.rem(t, 2)
         columns = pl.ds(pl.multiple_of(t * TILE, TILE), TILE)
         a = matmul(v[...], w1[t]) + b1_ref[columns].reshape(1, -1)
         gh = matmul_nt(ec[...], w2[t])
@@ -201,17 +292,11 @@
         small_ref[lax.div(t, per), pl.ds(pl.multiple_of(lax.rem(t, per) * TILE, TILE), TILE)] = jnp.sum(
             ea.astype(F32), axis=0
         )
-        slot = lax.rem(t, 2)
-
-        @pl.when(t >= 2)
-        def _():
-            core_copy(t - 2).wait_send()
-
         core_tx[slot] = matmul(lt[1 - core], rt[1 - core]).astype(BF).reshape(near, f, 2, each, TILE)
-        core_copy(t).start()
         keep[slot] = matmul(lt[core], rt[core]).reshape(near, f, 2, each, TILE)
         acc_out[...] += matmul(rt[1], w2[t])
         acc_ev[...] += matmul_nt(rt[0], w1[t])
+        core_copy(t).start()
 
     def ey_copy(at, n):
         return pltpu.make_async_copy(acc_ev.at[at], ey_hbm.at[at], out_sem.at[n])
@@ -298,7 +383,9 @@
         return value
 
     def chunk_out(t, value):
-        chunk_ref[:, pl.ds(pl.multiple_of(t * TILE, TILE), TILE)] = value.astype(BF)
+        chunk_ref[t] = value.astype(BF)
+        if far_inside:
+            gather.first(t)
 
     def even_core(t):
         i = lax.div(t, 2)
@@ -373,21 +460,25 @@
             def _():
                 tile_step(s)
 
-            for lag in range(1, 5):
+            for place, lag in enumerate(LAGS):
                 t = s - lag
-                stage = stages[(parity - lag) % 2][lag - 1]
+                stage = stages[(parity - lag) % 2][place]
 
                 @pl.when((t >= 0) & (t < tiles))
                 def _(t=t, stage=stage):
                     stage(t)
 
-            @pl.when(s >= tiles)
+            @pl.when((s >= tiles) & (s < tiles + 4))
             def _():
                 finish(s - tiles)
 
         return carry
 
-    lax.fori_loop(0, (tiles + 4) // 2, pair, 0)
+    lax.fori_loop(0, (tiles + LAGS[-1] + 1) // 2, pair, 0)
+    if far_inside:
+        for k in range(tiles):
+            gather.own(k).wait()
+            gather.to_x(k).wait()
     for t in (tiles - 2, tiles - 1):
         core_copy(t).wait_send()
     for copies in (a_near, a_far, a_x, b_near, b_far, b_x):
@@ -421,12 +512,13 @@
         out_shape=(
             jax.ShapeDtypeStruct(cot_l.shape, BF),
             jax.ShapeDtypeStruct((rows, width), F32),
-            jax.ShapeDtypeStruct((chunk, hidden), BF),
+            jax.ShapeDtypeStruct((tiles, chunk, TILE), BF),
             jax.ShapeDtypeStruct((8, width), F32),
             jax.ShapeDtypeStruct(cot_s.shape, BF),
+            jax.ShapeDtypeStruct((2, tiles, width, TILE), BF),
         ),
         in_specs=[ANY, pl.BlockSpec(memory_space=pltpu.SMEM), vmem, vmem, ANY, ANY] + [vmem] * 4,
-        out_specs=(ANY, ANY, vmem, vmem, vmem),
+        out_specs=(ANY, ANY, vmem, vmem, vmem, ANY),
         scratch_shapes=[
             V((rows, width), F32), V((rows, width), BF), V((rows, width), BF),
             V((2, width, rows), BF), V((2, rows, TILE), BF),
@@ -444,7 +536,7 @@
             DMA((1,)), DMA((2, tiles)), DMA((2 * count,)), DMA((2,)), DMA((tiles,)),
             DMA((2, nm)), DMA((pairs, nm)), DMA((2, fm)), DMA((pairs, fm)), DMA((2, 1)), DMA((pairs, 1)),
             DMA((2, nm)), DMA((pairs, nm)), DMA((2, fm)), DMA((pairs, fm)), DMA((2, 1)), DMA((pairs, 1)),
-        ],
+        ] + Gather.sems(tiles, near, f),
         compiler_params=pltpu.CompilerParams(
             collective_id=0, has_side_effects=True, vmem_limit_bytes=TOP
         ),
@@ -535,10 +627,10 @@
     per_l, per_s = count_l * 2 // size, count_s // size
     swap = Swap(peers, size, per_l, per_s, patches_l, patches_s)
     wq_l[0] = w1_l[...]
-    wq_l[1] = w2_l[...].astype(F32).T.astype(BF)
+    wq_l[1] = w2_l[...]
     wq_s[...] = jnp.zeros_like(wq_s)
     wq_s[0, :real_s] = w1_s[...]
-    wq_s[1, :real_s] = w2_s[...].astype(F32).T.astype(BF)
+    wq_s[1, :real_s] = w2_s[...]
 
     barrier = pltpu.get_barrier_semaphore()
     for j in range(1, size):
@@ -717,23 +809,23 @@
     )(xl, xs, w1_l, w1_s, w2_l, w2_s, b1_l, b1_s, b2_l, b2_s, gain, bias)
 
 
-GROUPS = 12
 DEPTH = 3
 SLAB = 512
 
 
 def backward_kernel(
     near, far, size, far_inside,
-    chunk_hbm, ey_hbm, xl, xs, u_l, u_s, h_l, h_s, sl_l, sl_s, w_l, w_s, small_in, gain_ref,
+    chunk_hbm, begun_hbm, ey_hbm,
+    xl_in, xs_in, u_l_in, u_s_in, h_l_in, h_s_in, sl_l_in, sl_s_in, w_l_in, w_s_in, small_in, gain_ref,
     full_hbm, gx_hbm, tok_out, vec_out, gx_s,
+    xl, xs, u_l, u_s, h_l, h_s, sl_l, sl_s, w_l, w_s, in_sem,
     ey, tx_l, tx_s, e_l, e_s, w2_l, w2_s, ep_l, ep_s, eu_l, eu_s, rx_l, rx_s,
-    grads, tok_tx, tok_rx, tokx_tx, tokx_rx, tok_sum, tokn_tx, tokn_rx, tok_half, tokf_tx, tokf_rx,
+    grads, tok_tx, tok_rx, tok_sum, tokn_tx, tokn_rx, tok_half, tokf_tx, tokf_rx, tokx_tx, tokx_rx,
     vec, vec_rx, vecn_rx, vecf_rx,
     ey_sem, gx_sem,
-    own_sem, gx_ss, gx_rs, gf_ss, gf_rs, gn_ss, gn_rs, gc_ss, gc_rs,
     out_ss_l, out_ss_s, out_rs_l, out_rs_s, bk_ss_l, bk_ss_s, bk_rs_l, bk_rs_s,
     tc_ss, tc_rs, tx_ss, tx_rs, tn_ss, tn_rs, tf_ss, tf_rs, taf_ss, taf_rs, tan_ss, tan_rs,
-    v_ss, v_rs, vn_ss, vn_rs, vf_ss, vf_rs,
+    v_ss, v_rs, vn_ss, vn_rs, vf_ss, vf_rs, *gather_sems,
 ):
     peers = Peers(near)
     me = peers.blk
@@ -760,100 +852,75 @@
     near_peers = others("near", near)
     far_peers = others("far", far)
 
-    each, hidden = chunk_hbm.shape
-    f = far if far_inside else 1
-    f_place = peers.far if far_inside else 0
-    cols = hidden // GROUPS
-    base_n = peers.near * (each * 2 * f)
-    base_f = base_n + f_place * (each * 2)
-    base_x = base_f + peers.x * each
-
-    def block(start, rows, k):
-        return full_hbm.at[peers.core, pl.ds(pl.multiple_of(start, each), rows), pl.ds(k * cols, cols)]
-
-    def g_own(k):
-        return pltpu.make_async_copy(chunk_hbm.at[:, pl.ds(k * cols, cols)], block(base_x, each, k), own_sem.at[k])
-
-    def g_x(k):
-        return send(chunk_hbm.at[:, pl.ds(k * cols, cols)], block(base_x, each, k), gx_ss.at[k], gx_rs.at[k], x_peer)
-
-    def g_far(k):
-        span = block(base_f, each * 2, k)
-        return [
-            send(span, span, gf_ss.at[k, j - 1], gf_rs.at[k, j - 1], there) for j, there in far_peers
-        ] if far_inside else []
-
-    def g_near(k):
-        span = block(base_n, each * 2 * f, k)
-        return [send(span, span, gn_ss.at[k, j - 1], gn_rs.at[k, j - 1], there) for j, there in near_peers]
-
-    def g_core(k):
-        span = block(0, each * 2 * f * near, k)
-        return send(span, span, gc_ss.at[k], gc_rs.at[k], core_peer)
-
-    def g_open(k):
-        if k < GROUPS:
-            g_own(k).wait()
-            g_x(k).wait_recv()
-            for copy in g_far(k):
-                copy.start()
-
-    def g_close(k):
-        for copy in g_near(k):
-            copy.wait_recv()
-        g_core(k).start()
-
-    def tick(k):
-        for copy in g_far(k):
-            copy.wait_recv()
-        for copy in g_near(k):
-            copy.start()
-        g_open(k + DEPTH)
-        if k >= 1:
-            g_close(k - 1)
+    groups = chunk_hbm.shape[0]
+    gather = Gather(peers, near, far, far_inside, chunk_hbm, full_hbm, gather_sems)
+    waiting = list(range(groups))
+
+    def tick():
+        if waiting:
+            k = waiting.pop(0)
+            gather.third(k)
+            if k + DEPTH < groups:
+                gather.second(k + DEPTH, far_inside)
+            if k > 0:
+                gather.fourth(k - 1)
 
     ey_in = pltpu.make_async_copy(ey_hbm, ey, ey_sem.at[0])
     ey_in.start()
+    inputs = [
+        pltpu.make_async_copy(src, dst, in_sem.at[n])
+        for n, (src, dst) in enumerate((
+            (w_l_in, w_l), (w_s_in, w_s), (sl_l_in, sl_l), (sl_s_in, sl_s), (u_l_in, u_l), (u_s_in, u_s),
+            (h_l_in, h_l), (h_s_in, h_s), (xl_in, xl), (xs_in, xs),
+        ))
+    ]
+    for copy in inputs:
+        copy.start()
     greet_all(peers, size, near, far)
-    for k in range(GROUPS):
-        g_x(k).start()
-        g_own(k).start()
+    if not far_inside:
+        for k in range(groups):
+            gather.first(k)
+    for k in range(DEPTH):
+        gather.second(k, far_inside)
     ey_in.wait()
     vec[...] = jnp.zeros_like(vec)
     vec[0:8, :] = small_in[...]
-    ones = jnp.ones((8, width), BF)
-
-    def cast_l(n, total):
+    def cast_l(n, carry):
         at = pl.ds(pl.multiple_of(small_rows + n * patches_l, 16), patches_l)
         et = ey[at, :].astype(BF)
         tx_l[2 * n] = et[:, :half]
         tx_l[2 * n + 1] = et[:, half:]
-        return total + matmul_nt(ones, et)
-
-    def cast_s(n, total):
+        return carry
+
+    def cast_s(n, carry):
         at = pl.ds(pl.multiple_of(n * patches_s, 16), patches_s)
-        et = ey[at, :].astype(BF)
-        tx_s[n] = et
-        return total + matmul_nt(ones, et)
-
-    total_l = lax.fori_loop(0, count_l, cast_l, jnp.zeros((8, patches_l), F32))
+        tx_s[n] = ey[at, :].astype(BF)
+        return carry
+
+    lax.fori_loop(0, count_l, cast_l, 0)
     for j in range(per_l):
         for k in range(1, size):
             swap.out("l", j, swap.other(k), me, tx_l, e_l, out_ss_l, out_rs_l).start()
-    total_s = lax.fori_loop(0, count_s, cast_s, jnp.zeros((8, patches_s), F32))
+    lax.fori_loop(0, count_s, cast_s, 0)
     for j in range(per_s):
         for k in range(1, size):
             swap.out("s", j, swap.other(k), me, tx_s, e_s, out_ss_s, out_rs_s).start()
-    vec[16:24, 0:patches_l] = total_l
-    vec[16:24, half:half + patches_s] = total_s
     for j in range(per_l):
         e_l[j, swap.rows(me, patches_l)] = tx_l[me * per_l + j]
     for j in range(per_s):
         e_s[j, swap.rows(me, patches_s)] = tx_s[me * per_s + j]
+    for copy in inputs:
+        copy.wait()
     w2_l[...] = w_l[1].T
     w2_s[...] = w_s[1].T
-    for k in range(DEPTH):
-        g_open(k)
+    ones_l = jnp.ones((8, half), BF)
+    ones_s = jnp.ones((8, width), BF)
+    vec[16:24, 0:patches_l] = lax.fori_loop(
+        0, 2 * count_l, lambda n, total: total + matmul_nt(ones_l, tx_l[n]), jnp.zeros((8, patches_l), F32)
+    )
+    vec[16:24, half:half + patches_s] = lax.fori_loop(
+        0, count_s, lambda n, total: total + matmul_nt(ones_s, tx_s[n]), jnp.zeros((8, patches_s), F32)
+    )
 
     def unmix(kind, j, e, w2, w1, slope, ep, eu, outs, tx, rx, bss, brs):
         for k in range(1, size):
@@ -867,15 +934,13 @@
         rx[me * per + j] = eu[j, swap.rows(me, patches)]
 
     for j in range(per_l):
+        tick()
         unmix("l", j, e_l, w2_l, w_l[0], sl_l, ep_l, eu_l, (out_ss_l, out_rs_l), tx_l, rx_l, bk_ss_l, bk_rs_l)
-        tick(j)
+    tick()
     for j in range(per_s):
         unmix("s", j, e_s, w2_s, w_s[0], sl_s, ep_s, eu_s, (out_ss_s, out_rs_s), tx_s, rx_s, bk_ss_s, bk_rs_s)
-    tick(3)
-
-    ones_l = jnp.ones((8, half), BF)
+
     vec[8:16, 0:half] = sum(matmul_nt(ones_l, ep_l[j]) for j in range(per_l))
-    ones_s = jnp.ones((8, width), BF)
     vec[8:16, half:width] = sum(matmul_nt(ones_s, ep_s[j]) for j in range(per_s))
     top = 2 * patches_l + 2 * patches_s
     if SLAB > top:
@@ -893,15 +958,18 @@
         tok_tx[p] = grads[p * 2 + 1 - peers.core].astype(BF)
     t_core = send(tok_tx, tok_rx, tc_ss.at[0], tc_rs.at[0], core_peer)
     t_core.start()
-    tick(4)
+    tick()
     t_core.wait_recv()
     there = 1 - peers.x
     tokx_tx[...] = (grads[there * 2 + peers.core] + tok_rx[there].astype(F32)).astype(BF)
     t_x = send(tokx_tx, tokx_rx, tx_ss.at[0], tx_rs.at[0], x_peer)
     t_x.start()
     tok_sum[...] = grads[me] + tok_rx[peers.x].astype(F32)
-    tick(5)
-    tick(6)
+    tick()
+    tick()
+
+    def piece(place, size):
+        return pl.ds(pl.multiple_of(place * size, size), size)
 
     def arrived(kind, unit, eu, rx, bss, brs):
         per = per_l if kind == "l" else per_s
@@ -941,14 +1009,13 @@
 
     vec[9:10, :] = jnp.zeros((1, width), F32)
     lax.fori_loop(0, count_l // 2, home_l, 0)
-    tick(7)
+    tick()
     lax.fori_loop(count_l // 2, count_l, home_l, 0)
-    tick(8)
     lax.fori_loop(0, count_s, home_s, 0)
-
     both = vec.at[0:16]
     v_core = send(both, vec_rx.at[0], v_ss.at[0], v_rs.at[0], core_peer)
     v_core.start()
+    tick()
     t_x.wait_recv()
     tok_sum[...] += tokx_rx[...].astype(F32)
     part_n = SLAB // near
@@ -956,8 +1023,7 @@
     t_near, t_far, ta_far, ta_near = [], [], [], []
     if far_inside:
         for j, device in near_peers:
-            at = pl.ds(pl.multiple_of(lax.rem(peers.near + j, near) * part_n, part_n), part_n)
-            tokn_tx[j - 1] = tok_sum[at, :].astype(BF)
+            tokn_tx[j - 1] = tok_sum[piece(lax.rem(peers.near + j, near), part_n), :].astype(BF)
             copy = send(tokn_tx.at[j - 1], tokn_rx.at[j - 1], tn_ss.at[j - 1], tn_rs.at[j - 1], device)
             copy.start()
             t_near.append(copy)
@@ -967,7 +1033,7 @@
     vec[0:16, :] += vec_rx[0]
     v_x = send(both, vec_rx.at[1], v_ss.at[1], v_rs.at[1], x_peer)
     v_x.start()
-    tick(9)
+    tick()
     v_x.wait()
     vec[0:16, :] += vec_rx[1]
     v_near = [send(vec, vecn_rx.at[j - 1], vn_ss.at[j - 1], vn_rs.at[j - 1], device) for j, device in near_peers]
@@ -976,17 +1042,15 @@
     if far_inside:
         for copy in t_near:
             copy.wait_recv()
-        mine = pl.ds(pl.multiple_of(peers.near * part_n, part_n), part_n)
-        tok_half[...] = tok_sum[mine, :]
+        tok_half[...] = tok_sum[piece(peers.near, part_n), :]
         for j in range(near - 1):
             tok_half[...] += tokn_rx[j].astype(F32)
         for j, device in far_peers:
-            at = pl.ds(pl.multiple_of(lax.rem(peers.far + j, far) * part_f, part_f), part_f)
-            tokf_tx[j - 1] = tok_half[at, :].astype(BF)
+            tokf_tx[j - 1] = tok_half[piece(lax.rem(peers.far + j, far), part_f), :].astype(BF)
             copy = send(tokf_tx.at[j - 1], tokf_rx.at[j - 1], tf_ss.at[j - 1], tf_rs.at[j - 1], device)
             copy.start()
             t_far.append(copy)
-    tick(10)
+    tick()
     for copy in v_near:
         copy.wait()
     for j in range(near - 1):
@@ -997,16 +1061,16 @@
     if far_inside:
         for copy in t_far:
             copy.wait_recv()
-        value = tok_half[pl.ds(pl.multiple_of(peers.far * part_f, part_f), part_f), :]
+        value = tok_half[piece(peers.far, part_f), :]
         for j in range(far - 1):
             value = value + tokf_rx[j].astype(F32)
-        span = tok_out.at[pl.ds(pl.multiple_of(peers.near * part_n + peers.far * part_f, part_f), part_f)]
+        span = tok_out.at[piece(peers.near * far + peers.far, part_f)]
         span[...] = value.astype(BF)
         for j, device in far_peers:
             copy = send(span, span, taf_ss.at[j - 1], taf_rs.at[j - 1], device)
             copy.start()
             ta_far.append(copy)
-    tick(11)
+    tick()
     for copy in v_far:
         copy.wait()
     value = vec[...]
@@ -1016,12 +1080,14 @@
     if far_inside:
         for copy in ta_far:
             copy.wait_recv()
-        span = tok_out.at[pl.ds(pl.multiple_of(peers.near * part_n, part_n), part_n)]
+        span = tok_out.at[piece(peers.near, part_n)]
         for j, device in near_peers:
             copy = send(span, span, tan_ss.at[j - 1], tan_rs.at[j - 1], device)
             copy.start()
             ta_near.append(copy)
-    g_close(GROUPS - 1)
+    while waiting:
+        tick()
+    gather.fourth(groups - 1)
     for copy in ta_near:
         copy.wait_recv()
 
@@ -1035,16 +1101,13 @@
         for j in range(per_s):
             swap.out("s", j, there, me, tx_s, e_s, out_ss_s, out_rs_s).wait_send()
             swap.back("s", j, me, there, eu_s, rx_s, bk_ss_s, bk_rs_s).wait_send()
-    for k in range(GROUPS):
-        g_x(k).wait_send()
-        for copy in g_far(k) + g_near(k):
-            copy.wait_send()
-        g_core(k).wait()
+    for k in range(groups):
+        gather.drain(k, far_inside)
     for n in range(count_l):
         gx_copy(n).wait()
 
 
-def backward(chunk, ey, xl, xs, saved, small, gain):
+def backward(chunk, begun, ey, xl, xs, saved, small, gain):
     size = lax.axis_size("blk")
     near, far = img_split(lax.axis_size("img"))
     rows, width = ey.shape
@@ -1056,7 +1119,7 @@
     token = w_l.shape[2]
     half = width // 2
     per_l, per_s = u_l.shape[0], u_s.shape[0]
-    each, hidden = chunk.shape
+    groups, each, _ = chunk.shape
     vmem = pl.BlockSpec(memory_space=pltpu.VMEM)
     V = pltpu.VMEM
     DMA = pltpu.SemaphoreType.DMA
@@ -1066,47 +1129,48 @@
     return pl.pallas_call(
         functools.partial(backward_kernel, near, far, size, far_inside),
         out_shape=(
-            jax.ShapeDtypeStruct((2, width, hidden), BF),
+            jax.ShapeDtypeStruct((2, groups, width, TILE), BF),
             jax.ShapeDtypeStruct(xl.shape, F32),
             jax.ShapeDtypeStruct((SLAB, token), BF),
             jax.ShapeDtypeStruct((24, width), F32),
             jax.ShapeDtypeStruct(xs.shape, F32),
         ),
-        in_specs=[ANY, ANY] + [vmem] * 12,
+        in_specs=[ANY] * 13 + [vmem] * 2,
         out_specs=(ANY, ANY, vmem, vmem, vmem),
         scratch_shapes=[
+            V(xl.shape, BF), V(xs.shape, BF), V(u_l.shape, BF), V(u_s.shape, BF), V(h_l.shape, BF), V(h_s.shape, BF),
+            V(sl_l.shape, BF), V(sl_s.shape, BF), V(w_l.shape, BF), V(w_s.shape, BF), DMA((10,)),
             V((rows, width), F32),
             V((count_l * 2, patches_l, half), BF), V((count_s, patches_s, width), BF),
             V(u_l.shape, BF), V(u_s.shape, BF),
             V((token, size * patches_l), BF), V((token, size * patches_s), BF),
             V(h_l.shape, BF), V(h_s.shape, BF), V(u_l.shape, BF), V(u_s.shape, BF),
             V((count_l * 2, patches_l, half), BF), V((count_s, patches_s, width), BF),
-            V((size, SLAB, token), F32), V((2, SLAB, token), BF), V((2, SLAB, token), BF),
-            V((SLAB, token), BF), V((SLAB, token), BF), V((SLAB, token), F32),
+            V((size, SLAB, token), F32), V((2, SLAB, token), BF), V((2, SLAB, token), BF), V((SLAB, token), F32),
             V((n1, part_n, token), BF), V((n1, part_n, token), BF), V((part_n, token), F32),
-            V((f1, part_f, token), BF), V((f1, part_f, token), BF),
+            V((f1, part_f, token), BF), V((f1, part_f, token), BF), V((SLAB, token), BF), V((SLAB, token), BF),
             V((24, width), F32), V((2, 16, width), F32), V((n1, 24, width), F32), V((f1, 24, width), F32),
             DMA((1,)), DMA((count_l,)),
-            DMA((GROUPS,)), DMA((GROUPS,)), DMA((GROUPS,)), DMA((GROUPS, f1)), DMA((GROUPS, f1)),
-            DMA((GROUPS, n1)), DMA((GROUPS, n1)), DMA((GROUPS,)), DMA((GROUPS,)),
             DMA((count_l * 2,)), DMA((count_s,)), DMA((per_l, size)), DMA((per_s, size)),
             DMA((per_l, size)), DMA((per_s, size)), DMA((count_l * 2,)), DMA((count_s,)),
             DMA((1,)), DMA((1,)), DMA((1,)), DMA((1,)), DMA((n1,)), DMA((n1,)), DMA((f1,)), DMA((f1,)),
             DMA((f1,)), DMA((f1,)), DMA((n1,)), DMA((n1,)),
             DMA((2,)), DMA((2,)), DMA((n1,)), DMA((n1,)), DMA((f1,)), DMA((f1,)),
-        ],
+        ] + Gather.sems(groups, near, far),
+        input_output_aliases={1: 0},
         compiler_params=pltpu.CompilerParams(
             collective_id=1, has_side_effects=True, vmem_limit_bytes=TOP
         ),
-    )(chunk, ey, xl, xs, u_l, u_s, h_l, h_s, sl_l, sl_s, w_l, w_s, small, gain)
+    )(chunk, begun, ey, xl, xs, u_l, u_s, h_l, h_s, sl_l, sl_s, w_l, w_s, small, gain)
 
 
 def widen_kernel(
     first, second, tok, vec,
     out_first, out_second, gain1, bias1, w1_s, b1_s, w2_s, b2_s, w1_l, b1_l, w2_l, b2_l, gain2, bias2, b1, b2,
 ):
-    out_first[...] = first[0].astype(F32)
-    out_second[...] = second[0].astype(F32).T
+    for k in range(first.shape[1]):
+        out_first[:, k * TILE:(k + 1) * TILE] = first[0, k].astype(F32)
+        out_second[k * TILE:(k + 1) * TILE, :] = second[0, k].astype(F32).T
 
     @pl.when(pl.program_id(0) == 0)
     def _():
@@ -1116,9 +1180,9 @@
         wide = small + -small % 64
         at = 2 * large
         w1_l[...] = tok[0:large, :].astype(F32)
-        w2_l[...] = tok[large:at, :].astype(F32).T
+        w2_l[...] = tok[large:at, :].astype(F32)
         w1_s[...] = tok[at:at + wide, :].astype(F32)[:small]
-        w2_s[...] = tok[at + wide:at + 2 * wide, :].astype(F32).T[:, :small]
+        w2_s[...] = tok[at + wide:at + 2 * wide, :].astype(F32)[:small]
         gain1[...] = vec[7, :]
         bias1[...] = vec[9, :]
         b1_l[...] = vec[8, 0:half]
@@ -1133,12 +1197,13 @@
 
 
 def widen(full, tok, vec, patches_s, patches_l):
-    _, width, hidden = full.shape
+    _, groups, width, _ = full.shape
+    hidden = groups * TILE
     token = tok.shape[1]
-    step = 384
+    step = 2 * TILE
     shapes = (
-        (width,), (width,), (patches_s, token), (token,), (token, patches_s), (patches_s,),
-        (patches_l, token), (token,), (token, patches_l), (patches_l,), (width,), (width,), (hidden,), (width,),
+        (width,), (width,), (patches_s, token), (token,), (patches_s, token), (patches_s,),
+        (patches_l, token), (token,), (patches_l, token), (patches_l,), (width,), (width,), (hidden,), (width,),
     )
 
     def whole(shape):
@@ -1151,8 +1216,8 @@
             jax.ShapeDtypeStruct((width, hidden), F32), jax.ShapeDtypeStruct((hidden, width), F32),
         ) + tuple(jax.ShapeDtypeStruct(shape, F32) for shape in shapes),
         in_specs=[
-            pl.BlockSpec((1, width, step), lambda i: (0, 0, i)),
-            pl.BlockSpec((1, width, step), lambda i: (1, 0, i)),
+            pl.BlockSpec((1, 2, width, TILE), lambda i: (0, i, 0, 0)),
+            pl.BlockSpec((1, 2, width, TILE), lambda i: (1, i, 0, 0)),
             whole(tok.shape), whole(vec.shape),
         ],
         out_specs=(
@@ -1172,10 +1237,10 @@
     patches_s, patches_l = x_small.shape[1], x_large.shape[1]
     rows = x_small.shape[0] * (patches_s + -patches_s % 64) + x_large.shape[0] * patches_l
     y, *saved = token_forward(
-        x_large, x_small, tok_w1_large, tok_w1_small, tok_w2_large, tok_w2_small,
+        x_large, x_small, tok_w1_large, tok_w1_small, tok_w2_large.T, tok_w2_small.T,
         tok_b1_large, tok_b1_small, tok_b2_large, tok_b2_small, ln1_gain, ln1_bias, rows + -rows % (3 * LANES),
     )
-    out_large, ey, chunk, small_grads, out_small = channel(
+    out_large, ey, chunk, small_grads, out_small, begun = channel(
         y, live_counts, cot_large, cot_small, ch_w1, ch_w2, ch_b1, ln2_gain, ln2_bias, ch_b2
     )
     near, far = img_split(lax.axis_size("img"))
@@ -1184,7 +1249,7 @@
         same = [[a * near + b for a in range(far)] for b in range(near)]
         chunk = lax.psum(chunk.astype(F32), "img", axis_index_groups=same).astype(BF)
     full, gx_large, tok, vec, gx_small = backward(
-        chunk, ey, x_large, x_small, saved, small_grads, ln1_gain
+        chunk, begun, ey, x_large, x_small, saved, small_grads, ln1_gain
     )
     if not far_inside:
         tok = lax.psum(tok.astype(F32), "img")
@@ -1194,7 +1259,7 @@
     ) = widen(full, tok, vec, patches_s, patches_l)
     return (
         out_small, out_large, gx_small, gx_large, gain1, bias1,
-        w1_s, b1_s, w2_s, b2_s, w1_l, b1_l, w2_l, b2_l,
+        w1_s, b1_s, w2_s.T, b2_s, w1_l, b1_l, w2_l.T, b2_l,
         gain2, bias2, grad_ch_w1, grad_b1, grad_ch_w2, grad_b2,
     )
 

time: 277 us -> 242 us (0.87)
  Pallas kernels: 257 us -> 228 us
  local copies, waits for them, and re-layouts: 18.3 us -> 11.1 us
    pallas_call x1, Pallas kernels: 101 us -> 79.6 us  [channel(): pl.pallas_call(functools.partial(channel_kernel, near, far, far_inside),...]
    pallas_call x1, Pallas kernels: 90.8 us -> 83.3 us  [backward(): pl.pallas_call(functools.partial(backward_kernel, near, far, size, far_in...]
    unnamed x12 -> x10, local copies, waits for them, and re-layouts: 18.3 us -> 11.1 us
where the time goes in v5:
time: 242 us; the launch traced here: 239 us
  Pallas kernels  228 us (94%)
  local copies, waits for them, and re-layouts  11.1 us (5%)
    pallas_call x1, Pallas kernels, backward(): pl.pallas_call(functools.partial(backward_kernel, near, far, size, far_in...  83.3 us
    pallas_call x1, Pallas kernels, channel(): pl.pallas_call(functools.partial(channel_kernel, near, far, far_inside),...  79.6 us
    pallas_call x1, Pallas kernels, token_forward(): pl.pallas_call(functools.partial(token_kernel, near, size), out_shape=(ja...  52.9 us
    pallas_call x1, Pallas kernels, widen(): pl.pallas_call(widen_kernel, grid=(hidden // step,), out_shape=(jax.Shape...  11.7 us
    unnamed x10, local copies, waits for them, and re-layouts  11.1 us

profile of v5, /device:TPU:0, one launch (start us, length us, event | category | flops | bytes accessed | tf_op | source)
XLA Modules:
  0.0 239.4 jit_solution(3474958307756278528)
XLA Ops:
  0.7 1.7 copy.42.xs.xs_in
  2.4 1.7 copy.43.cot_s
  4.1 52.9 %shard_map.356 = (f32[1152,768]{1,0:T(8,128)}, bf16[3,576,384]{2,1,0:T(8,128)(2,1)}, bf16[1,256,768]{2,1,0:T(8,128)(2,1)}, bf16[3,384,384]{2,1,0:T(8,128)(2,1)},...) custom-call(bf16[6,144,768]{2,1,0:T(8,128)(2,1)} %xl_in.1, ...), custom_call_target="tpu_custom_call" | custom-call | tf_op jit(solution)/shard_map/pallas_call | solution.py:784
  57.0 79.6 %shard_map.357 = (bf16[6,144,768]{2,1,0:T(8,128)(2,1)}, f32[1152,768]{1,0:T(8,128)}, bf16[12,48,256]{2,1,0:T(8,128)(2,1)}, f32[8,768]{1,0:T(8,128)}, bf16[4,49,7...) custom-call(f32[1152,768]{1,0:T(8,128)} %get-tuple-element.56.y_hbm, s32[1,2]{1,0:T(1,128)} %live.1, ...), custom_call_target="tpu_custom_call" | custom-call | tf_op jit(solution)/shard_map/pallas_call | solution.py:510
  136.7 1.8 copy.45
  138.5 83.3 %shard_map.358 = (bf16[2,12,768,256]{3,2,1,0:T(8,128)(2,1)}, f32[6,144,768]{2,1,0:T(8,128)}, bf16[512,384]{1,0:T(8,128)(2,1)}, f32[24,768]{1,0:T(8,128)}, f32[4,49,768]{2,1,0:T(8,128)}) custom-call(bf16[12,48,256]{2,1,0:T(8,128)(2,1)} %get-tuple-element.59.chunk_hbm, ...), custom_call_target="tpu_custom_call", output_to_operand_aliasing={{0}: (1, {})} | custom-call | tf_op jit(solution)/shard_map/pallas_call | solution.py:1129
  221.8 2.2 copy.46
  224.0 0.0 copy-start.1
  224.0 11.7 %shard_map.359 = (f32[768,3072]{1,0:T(8,128)}, f32[3072,768]{1,0:T(8,128)}, f32[768]{0:T(1024)}, f32[768]{0:T(1024)}, f32[49,384]{1,0:T(8,128)}, /*index=5*/f32[...) custom-call(bf16[2,12,768,256]{3,2,1,0:T(8,128)(2,1)} %get-tuple-ele, ...), custom_call_target="tpu_custom_call" | custom-call | tf_op jit(solution)/shard_map/pallas_call | solution.py:1212
  235.7 0.0 copy-start
  235.7 0.0 copy-done.1
  235.7 1.1 copy.50
  236.7 1.1 copy-done
  237.9 1.5 copy.51
Async XLA Ops:
  224.0 11.7 %copy-start.1 = (bf16[6,144,768]{2,1,0:T(8,128)(2,1)S(1)}, bf16[6,144,768]{2,1,0:T(8,128)(2,1)}, u32[]{:S(2)}) copy-start(bf16[6,144,768]{2,1,0:T(8,128)(2,1)} %get-tuple-element.133) | copy-start | bytes 3981316
  235.7 2.2 copy-start

commit v6 on v5

--- a/solution.py
+++ b/solution.py
@@ -17,6 +17,7 @@
 ANY = pl.BlockSpec(memory_space=pl.ANY)
 TILE = 256
 LAGS = (1, 3, 5, 7)
+LATE = 3
 TOP = 62 * 1024 * 1024
 
 
@@ -65,22 +66,28 @@
             there = lax.rem(peers.mine(axis) + j, count)
             pl.semaphore_signal(barrier, inc=1, device_id=peers.at(axis, there), device_id_type=MESH)
             total += 1
-    pl.semaphore_wait(barrier, total)
+    return total
+
+
+def greeted(total):
+    pl.semaphore_wait(pltpu.get_barrier_semaphore(), total)
 
 
 class Gather:
     def __init__(self, peers, near, far, far_inside, chunk, full, sems):
-        self.peers, self.near, self.far, self.far_inside = peers, near, far, far_inside
+        self.peers, self.near, self.far_inside = peers, near, far_inside
+        self.f = far if far_inside else 1
         self.chunk, self.full = chunk, full
-        self.each = each = chunk.shape[1]
-        self.f = far if far_inside else 1
+        self.tiles = chunk.shape[0]
+        self.late = self.tiles - LATE if far_inside else self.tiles
         self.own_sem, self.x_ss, self.x_rs, self.f_ss, self.f_rs, self.n_ss, self.n_rs, self.c_ss, self.c_rs = sems
-        self.base_n = peers.near * (each * 2 * self.f)
-        self.base_f = self.base_n + (peers.far if far_inside else 0) * (each * 2)
-        self.base_x = self.base_f + peers.x * each
-
-    def block(self, start, rows, k):
-        return self.full.at[self.peers.core, k, pl.ds(pl.multiple_of(start, self.each), rows)]
+        self.place = (peers.near, peers.far if far_inside else 0, peers.x)
+
+    def span(self, k, axes):
+        index = tuple(p if a in axes else slice(None) for p, a in zip(self.place, "nfx"))
+        while index and isinstance(index[-1], slice):
+            index = index[:-1]
+        return self.full.at[(self.peers.core, k) + index]
 
     def send(self, src, dst, ss, rs, device):
         return pltpu.make_async_remote_copy(
@@ -88,13 +95,15 @@
         )
 
     def own(self, k):
-        return pltpu.make_async_copy(self.chunk.at[k], self.block(self.base_x, self.each, k), self.own_sem.at[k])
-
-    def to_x(self, k):
+        return pltpu.make_async_copy(self.chunk.at[k], self.span(k, "nfx"), self.own_sem.at[k])
+
+    def x_first(self, k):
         there = self.peers.at("x", 1 - self.peers.x)
-        return self.send(
-            self.chunk.at[k], self.block(self.base_x, self.each, k), self.x_ss.at[k], self.x_rs.at[k], there
-        )
+        return self.send(self.chunk.at[k], self.span(k, "nfx"), self.x_ss.at[k], self.x_rs.at[k], there)
+
+    def x_last(self, k):
+        there = self.peers.at("x", 1 - self.peers.x)
+        return self.send(self.span(k, "x"), self.span(k, "x"), self.x_ss.at[k], self.x_rs.at[k], there)
 
     def spread(self, axis, count, span, ss, rs, k):
         copies = []
@@ -104,25 +113,28 @@
         return copies
 
     def to_far(self, k):
-        return self.spread("far", self.f, self.block(self.base_f, self.each * 2, k), self.f_ss, self.f_rs, k)
+        return self.spread("far", self.f, self.span(k, "nf" if k < self.late else "nfx"), self.f_ss, self.f_rs, k)
 
     def to_near(self, k):
-        return self.spread(
-            "near", self.near, self.block(self.base_n, self.each * 2 * self.f, k), self.n_ss, self.n_rs, k
-        )
+        return self.spread("near", self.near, self.span(k, "n" if k < self.late else "nx"), self.n_ss, self.n_rs, k)
 
     def to_core(self, k):
-        span = self.block(0, self.each * 2 * self.f * self.near, k)
+        span = self.span(k, "")
         return self.send(span, span, self.c_ss.at[k], self.c_rs.at[k], self.peers.at("core", 1 - self.peers.core))
 
     def first(self, k):
-        self.to_x(k).start()
         self.own(k).start()
 
-    def second(self, k, begun):
-        if not begun:
-            self.own(k).wait()
-            self.to_x(k).wait_recv()
+        @pl.when(k < self.late)
+        def _():
+            self.x_first(k).start()
+
+    def end_first(self, k):
+        self.own(k).wait()
+        if k < self.late:
+            self.x_first(k).wait()
+
+    def second(self, k):
         for copy in self.to_far(k):
             copy.start()
 
@@ -135,13 +147,18 @@
     def fourth(self, k):
         for copy in self.to_near(k):
             copy.wait_recv()
-        self.to_core(k).start()
-
-    def drain(self, k, begun):
-        if not begun:
-            self.to_x(k).wait_send()
+        (self.to_core(k) if k < self.late else self.x_last(k)).start()
+
+    def fifth(self, k):
+        if k >= self.late:
+            self.x_last(k).wait_recv()
+            self.to_core(k).start()
+
+    def drain(self, k):
         for copy in self.to_far(k) + self.to_near(k):
             copy.wait_send()
+        if k >= self.late:
+            self.x_last(k).wait_send()
         self.to_core(k).wait()
 
     @staticmethod
@@ -162,9 +179,9 @@
 
 def channel_kernel(
     near, far, far_inside,
-    y_hbm, live, cot_l, cot_s, w1_hbm, w2_hbm, b1_ref, gain_ref, bias_ref, b2_ref,
-    out_l, ey_hbm, chunk_ref, small_ref, out_s, full_hbm,
-    y, ec, v, lt, rt, w1, w2, acc_out, acc_ev, out_low,
+    y_hbm, live, cot_l, cot_s_in, w1_hbm, w2_hbm, b1_ref, gain_ref, bias_ref, b2_ref,
+    out_l, ey_hbm, chunk_ref, small_ref, out_s_t, full_hbm,
+    cot_s, out_s, y, ec, v, lt, rt, w1, w2, acc_out, acc_ev, out_low,
     keep, core_tx, core_rx,
     a_keep_n, a_near_tx, a_near_rx, a_keep_f, a_far_tx, a_far_rx, a_keep_x, a_x_tx, a_x_rx,
     b_keep_x, b_x_tx, b_x_rx, b_keep_n, b_near_tx, b_near_rx, b_keep_f, b_far_tx, b_far_rx,
@@ -202,7 +219,7 @@
 
     lax.fori_loop(0, tiles, start_w, 0)
     axes = [("core", 2), ("near", near)] + ([("far", far)] if far_inside else []) + [("x", 2)]
-    greet(peers, axes)
+    greetings = greet(peers, axes)
     small_ref[...] = jnp.zeros_like(small_ref)
     used = small_rows + count_l * patches_l
     ec[0:small_rows, :] = jnp.zeros((small_rows, width), BF)
@@ -226,6 +243,8 @@
         return carry
 
     lax.fori_loop(0, count_l, mask_l, 0)
+    for n in range(count_s):
+        cot_s[n] = cot_s_in[:, n, :]
     lax.fori_loop(0, count_s, mask_s, 0)
     y_in.wait()
 
@@ -243,6 +262,7 @@
         return carry
 
     lax.fori_loop(0, parts, prepare, 0)
+    greeted(greetings)
 
     def send(src, dst, ss, rs, device):
         return pltpu.make_async_remote_copy(
@@ -477,14 +497,15 @@
     lax.fori_loop(0, (tiles + LAGS[-1] + 1) // 2, pair, 0)
     if far_inside:
         for k in range(tiles):
-            gather.own(k).wait()
-            gather.to_x(k).wait()
+            gather.end_first(k)
     for t in (tiles - 2, tiles - 1):
         core_copy(t).wait_send()
     for copies in (a_near, a_far, a_x, b_near, b_far, b_x):
         for i in (tiles // 2 - 2, tiles // 2 - 1):
             for copy in copies(i):
                 copy.wait_send()
+    for n in range(count_s):
+        out_s_t[:, n, :] = out_s[n]
     for n in range(count_l):
         ey_copy(at_l(n), n).wait()
         out_copy(n).wait()
@@ -506,7 +527,8 @@
     fm = max(f - 1, 1)
     nm = near - 1
     pairs = tiles // 2
-    count = cot_l.shape[0] + cot_s.shape[0]
+    real_s, count_s, _ = cot_s.shape
+    count = cot_l.shape[0] + count_s
     return pl.pallas_call(
         functools.partial(channel_kernel, near, far, far_inside),
         out_shape=(
@@ -515,11 +537,12 @@
             jax.ShapeDtypeStruct((tiles, chunk, TILE), BF),
             jax.ShapeDtypeStruct((8, width), F32),
             jax.ShapeDtypeStruct(cot_s.shape, BF),
-            jax.ShapeDtypeStruct((2, tiles, width, TILE), BF),
+            jax.ShapeDtypeStruct((2, tiles, near, f, 2, chunk, TILE), BF),
         ),
         in_specs=[ANY, pl.BlockSpec(memory_space=pltpu.SMEM), vmem, vmem, ANY, ANY] + [vmem] * 4,
         out_specs=(ANY, ANY, vmem, vmem, vmem, ANY),
         scratch_shapes=[
+            V((count_s, real_s, width), BF), V((count_s, real_s, width), BF),
             V((rows, width), F32), V((rows, width), BF), V((rows, width), BF),
             V((2, width, rows), BF), V((2, rows, TILE), BF),
             V((tiles, width, TILE), BF), V((tiles, TILE, width), BF),
@@ -612,9 +635,9 @@
 
 def token_kernel(
     near, size,
-    xl, xs, w1_l, w1_s, w2_l, w2_s, b1_l_ref, b1_s_ref, b2_l_ref, b2_s_ref, gain_ref, bias_ref,
+    xl, xs_in, w1_l, w1_s, w2_l, w2_s, b1_l_ref, b1_s_ref, b2_l_ref, b2_s_ref, gain_ref, bias_ref,
     y_hbm, u_l, u_s, h_l, h_s, sl_l, sl_s, w_l, w_s,
-    wq_l, wq_s, tx_l, tx_s, w1t_l, w1t_s, m_l, m_s, rx_l, rx_s, y,
+    xs, wq_l, wq_s, tx_l, tx_s, w1t_l, w1t_s, m_l, m_s, rx_l, rx_s, y,
     y_sem, own_sem, wown, w_ss, w_rs, out_ss_l, out_ss_s, out_rs_l, out_rs_s, bk_ss_l, bk_ss_s, bk_rs_l, bk_rs_s,
 ):
     peers = Peers(near)
@@ -635,7 +658,6 @@
     barrier = pltpu.get_barrier_semaphore()
     for j in range(1, size):
         pl.semaphore_signal(barrier, inc=1, device_id=(peers.img, swap.other(j)), device_id_type=MESH)
-    pl.semaphore_wait(barrier, size - 1)
 
     def weights(src_l, src_s, quarter, n, place):
         return (
@@ -650,8 +672,6 @@
     relay = weights(
         w_l.at[:, swap.rows(x_peer, patches_l)], w_s.at[:, swap.rows(x_peer, patches_s)], x_peer, 2, core_peer
     )
-    for copy in to_x + to_core:
-        copy.start()
     own_w = (
         pltpu.make_async_copy(wq_l, w_l.at[:, swap.rows(me, patches_l)], wown.at[0]),
         pltpu.make_async_copy(wq_s, w_s.at[:, swap.rows(me, patches_s)], wown.at[1]),
@@ -671,16 +691,21 @@
         tx_l[2 * n + 1] = u[:, half:]
         return carry
 
-    tx_s[...] = jnp.zeros_like(tx_s)
 
     def norm_s(n, carry):
         tx_s[n, :real_s] = norm(xs[n])
         return carry
 
     lax.fori_loop(0, count_l, norm_l, 0)
+    greeted(size - 1)
+    for copy in to_x + to_core:
+        copy.start()
     for j in range(per_l):
         for k in range(1, size):
             swap.out("l", j, swap.other(k), me, tx_l, u_l, out_ss_l, out_rs_l).start()
+    tx_s[...] = jnp.zeros_like(tx_s)
+    for n in range(count_s):
+        xs[n] = xs_in[:, n, :]
     lax.fori_loop(0, count_s, norm_s, 0)
     for j in range(per_s):
         for k in range(1, size):
@@ -772,8 +797,8 @@
     size = lax.axis_size("blk")
     near, far = img_split(lax.axis_size("img"))
     count_l, patches_l, width = xl.shape
-    count_s, patches_s, _ = xs.shape
-    patches_s += -patches_s % 64
+    real_s, count_s, _ = xs.shape
+    patches_s = real_s + -real_s % 64
     token = w1_l.shape[1]
     half = width // 2
     per_l, per_s = count_l * 2 // size, count_s // size
@@ -793,7 +818,7 @@
         in_specs=[vmem] * 12,
         out_specs=(ANY,) + (vmem,) * 8,
         scratch_shapes=[
-            V((2, patches_l, token), BF), V((2, patches_s, token), BF),
+            V((count_s, real_s, width), BF), V((2, patches_l, token), BF), V((2, patches_s, token), BF),
             V((count_l * 2, patches_l, half), BF), V((count_s, patches_s, width), BF),
             V((token, size * patches_l), BF), V((token, size * patches_s), BF),
             V((per_l, size * patches_l, half), BF), V((per_s, size * patches_s, width), BF),
@@ -817,8 +842,8 @@
     near, far, size, far_inside,
     chunk_hbm, begun_hbm, ey_hbm,
     xl_in, xs_in, u_l_in, u_s_in, h_l_in, h_s_in, sl_l_in, sl_s_in, w_l_in, w_s_in, small_in, gain_ref,
-    full_hbm, gx_hbm, tok_out, vec_out, gx_s,
-    xl, xs, u_l, u_s, h_l, h_s, sl_l, sl_s, w_l, w_s, in_sem,
+    full_hbm, gx_hbm, tok_out, vec_out, gx_out,
+    xl, xs_in_v, u_l, u_s, h_l, h_s, sl_l, sl_s, w_l, w_s, in_sem, xs, gx_s,
     ey, tx_l, tx_s, e_l, e_s, w2_l, w2_s, ep_l, ep_s, eu_l, eu_s, rx_l, rx_s,
     grads, tok_tx, tok_rx, tok_sum, tokn_tx, tokn_rx, tok_half, tokf_tx, tokf_rx, tokx_tx, tokx_rx,
     vec, vec_rx, vecn_rx, vecf_rx,
@@ -861,9 +886,11 @@
             k = waiting.pop(0)
             gather.third(k)
             if k + DEPTH < groups:
-                gather.second(k + DEPTH, far_inside)
+                gather.second(k + DEPTH)
             if k > 0:
                 gather.fourth(k - 1)
+            if k > 1:
+                gather.fifth(k - 2)
 
     ey_in = pltpu.make_async_copy(ey_hbm, ey, ey_sem.at[0])
     ey_in.start()
@@ -871,7 +898,7 @@
         pltpu.make_async_copy(src, dst, in_sem.at[n])
         for n, (src, dst) in enumerate((
             (w_l_in, w_l), (w_s_in, w_s), (sl_l_in, sl_l), (sl_s_in, sl_s), (u_l_in, u_l), (u_s_in, u_s),
-            (h_l_in, h_l), (h_s_in, h_s), (xl_in, xl), (xs_in, xs),
+            (h_l_in, h_l), (h_s_in, h_s), (xl_in, xl), (xs_in, xs_in_v),
         ))
     ]
     for copy in inputs:
@@ -880,8 +907,10 @@
     if not far_inside:
         for k in range(groups):
             gather.first(k)
+        for k in range(groups):
+            gather.end_first(k)
     for k in range(DEPTH):
-        gather.second(k, far_inside)
+        gather.second(k)
     ey_in.wait()
     vec[...] = jnp.zeros_like(vec)
     vec[0:8, :] = small_in[...]
@@ -911,6 +940,8 @@
         e_s[j, swap.rows(me, patches_s)] = tx_s[me * per_s + j]
     for copy in inputs:
         copy.wait()
+    for n in range(count_s):
+        xs[n] = xs_in_v[:, n, :]
     w2_l[...] = w_l[1].T
     w2_s[...] = w_s[1].T
     ones_l = jnp.ones((8, half), BF)
@@ -943,8 +974,6 @@
     vec[8:16, 0:half] = sum(matmul_nt(ones_l, ep_l[j]) for j in range(per_l))
     vec[8:16, half:width] = sum(matmul_nt(ones_s, ep_s[j]) for j in range(per_s))
     top = 2 * patches_l + 2 * patches_s
-    if SLAB > top:
-        grads[:, top:SLAB, :] = jnp.zeros((size, SLAB - top, token), F32)
     begin = 0
     for left, right, per, patches in (
         (u_l, ep_l, per_l, patches_l), (e_l, h_l, per_l, patches_l),
@@ -955,16 +984,18 @@
             grads[q, begin:begin + patches] = value[q * patches:(q + 1) * patches]
         begin += patches
     for p in range(2):
-        tok_tx[p] = grads[p * 2 + 1 - peers.core].astype(BF)
+        tok_tx[p] = grads[p * 2 + 1 - peers.core, 0:top].astype(BF)
     t_core = send(tok_tx, tok_rx, tc_ss.at[0], tc_rs.at[0], core_peer)
     t_core.start()
     tick()
     t_core.wait_recv()
     there = 1 - peers.x
-    tokx_tx[...] = (grads[there * 2 + peers.core] + tok_rx[there].astype(F32)).astype(BF)
+    tokx_tx[...] = (grads[there * 2 + peers.core, 0:top] + tok_rx[there].astype(F32)).astype(BF)
     t_x = send(tokx_tx, tokx_rx, tx_ss.at[0], tx_rs.at[0], x_peer)
     t_x.start()
-    tok_sum[...] = grads[me] + tok_rx[peers.x].astype(F32)
+    if SLAB > top:
+        tok_sum[top:SLAB, :] = jnp.zeros((SLAB - top, token), F32)
+    tok_sum[0:top, :] = grads[me, 0:top] + tok_rx[peers.x].astype(F32)
     tick()
     tick()
 
@@ -1012,12 +1043,14 @@
     tick()
     lax.fori_loop(count_l // 2, count_l, home_l, 0)
     lax.fori_loop(0, count_s, home_s, 0)
+    for n in range(count_s):
+        gx_out[:, n, :] = gx_s[n]
     both = vec.at[0:16]
     v_core = send(both, vec_rx.at[0], v_ss.at[0], v_rs.at[0], core_peer)
     v_core.start()
     tick()
     t_x.wait_recv()
-    tok_sum[...] += tokx_rx[...].astype(F32)
+    tok_sum[0:top, :] += tokx_rx[...].astype(F32)
     part_n = SLAB // near
     part_f = part_n // far
     t_near, t_far, ta_far, ta_near = [], [], [], []
@@ -1088,6 +1121,8 @@
     while waiting:
         tick()
     gather.fourth(groups - 1)
+    for k in (groups - 2, groups - 1):
+        gather.fifth(k)
     for copy in ta_near:
         copy.wait_recv()
 
@@ -1102,7 +1137,7 @@
             swap.out("s", j, there, me, tx_s, e_s, out_ss_s, out_rs_s).wait_send()
             swap.back("s", j, me, there, eu_s, rx_s, bk_ss_s, bk_rs_s).wait_send()
     for k in range(groups):
-        gather.drain(k, far_inside)
+        gather.drain(k)
     for n in range(count_l):
         gx_copy(n).wait()
 
@@ -1114,8 +1149,8 @@
     far_inside = width % (near * far * 2 * 16) == 0
     u_l, u_s, h_l, h_s, sl_l, sl_s, w_l, w_s = saved
     count_l, patches_l, _ = xl.shape
-    count_s, patches_s, _ = xs.shape
-    patches_s += -patches_s % 64
+    real_s, count_s, _ = xs.shape
+    patches_s = real_s + -real_s % 64
     token = w_l.shape[2]
     half = width // 2
     per_l, per_s = u_l.shape[0], u_s.shape[0]
@@ -1124,12 +1159,13 @@
     V = pltpu.VMEM
     DMA = pltpu.SemaphoreType.DMA
     n1, f1 = near - 1, far - 1
+    top = 2 * patches_l + 2 * patches_s
     part_n = SLAB // near
     part_f = max(part_n // far, 16)
     return pl.pallas_call(
         functools.partial(backward_kernel, near, far, size, far_inside),
         out_shape=(
-            jax.ShapeDtypeStruct((2, groups, width, TILE), BF),
+            jax.ShapeDtypeStruct(begun.shape, BF),
             jax.ShapeDtypeStruct(xl.shape, F32),
             jax.ShapeDtypeStruct((SLAB, token), BF),
             jax.ShapeDtypeStruct((24, width), F32),
@@ -1140,15 +1176,16 @@
         scratch_shapes=[
             V(xl.shape, BF), V(xs.shape, BF), V(u_l.shape, BF), V(u_s.shape, BF), V(h_l.shape, BF), V(h_s.shape, BF),
             V(sl_l.shape, BF), V(sl_s.shape, BF), V(w_l.shape, BF), V(w_s.shape, BF), DMA((10,)),
+            V((count_s, real_s, width), BF), V((count_s, real_s, width), F32),
             V((rows, width), F32),
             V((count_l * 2, patches_l, half), BF), V((count_s, patches_s, width), BF),
             V(u_l.shape, BF), V(u_s.shape, BF),
             V((token, size * patches_l), BF), V((token, size * patches_s), BF),
             V(h_l.shape, BF), V(h_s.shape, BF), V(u_l.shape, BF), V(u_s.shape, BF),
             V((count_l * 2, patches_l, half), BF), V((count_s, patches_s, width), BF),
-            V((size, SLAB, token), F32), V((2, SLAB, token), BF), V((2, SLAB, token), BF), V((SLAB, token), F32),
+            V((size, top, token), F32), V((2, top, token), BF), V((2, top, token), BF), V((SLAB, token), F32),
             V((n1, part_n, token), BF), V((n1, part_n, token), BF), V((part_n, token), F32),
-            V((f1, part_f, token), BF), V((f1, part_f, token), BF), V((SLAB, token), BF), V((SLAB, token), BF),
+            V((f1, part_f, token), BF), V((f1, part_f, token), BF), V((top, token), BF), V((top, token), BF),
             V((24, width), F32), V((2, 16, width), F32), V((n1, 24, width), F32), V((f1, 24, width), F32),
             DMA((1,)), DMA((count_l,)),
             DMA((count_l * 2,)), DMA((count_s,)), DMA((per_l, size)), DMA((per_s, size)),
@@ -1165,15 +1202,19 @@
 
 
 def widen_kernel(
-    first, second, tok, vec,
-    out_first, out_second, gain1, bias1, w1_s, b1_s, w2_s, b2_s, w1_l, b1_l, w2_l, b2_l, gain2, bias2, b1, b2,
+    first, second, tok, vec, out_l_in, gx_l_in, out_s_in, gx_s_in,
+    out_l, gx_l, out_s, gx_s, out_first, out_second, gain1, bias1, w1_s, b1_s, w2_s, b2_s, w1_l, b1_l, w2_l, b2_l, gain2, bias2, b1, b2,
 ):
+    out_l[...] = out_l_in[...]
+    gx_l[...] = gx_l_in[...]
     for k in range(first.shape[1]):
         out_first[:, k * TILE:(k + 1) * TILE] = first[0, k].astype(F32)
         out_second[k * TILE:(k + 1) * TILE, :] = second[0, k].astype(F32).T
 
     @pl.when(pl.program_id(0) == 0)
     def _():
+        out_s[...] = out_s_in[...]
+        gx_s[...] = gx_s_in[...]
         width = vec.shape[1]
         half = width // 2
         large, small = w1_l.shape[0], w1_s.shape[0]
@@ -1196,8 +1237,11 @@
         b2[...] = vec[4, :]
 
 
-def widen(full, tok, vec, patches_s, patches_l):
+def widen(full, tok, vec, out_l, gx_l, out_s, gx_s):
+    full = full.reshape(full.shape[0], full.shape[1], -1, TILE)
     _, groups, width, _ = full.shape
+    count_l, patches_l, _ = out_l.shape
+    patches_s = out_s.shape[0]
     hidden = groups * TILE
     token = tok.shape[1]
     step = 2 * TILE
@@ -1209,22 +1253,24 @@
     def whole(shape):
         return pl.BlockSpec(shape, lambda i: (0,) * len(shape))
 
+    image = pl.BlockSpec((1, patches_l, width), lambda i: (jnp.minimum(i, count_l - 1), 0, 0))
     return pl.pallas_call(
         widen_kernel,
         grid=(hidden // step,),
-        out_shape=(
+        out_shape=tuple(jax.ShapeDtypeStruct(a.shape, a.dtype) for a in (out_l, gx_l, out_s, gx_s)) + (
             jax.ShapeDtypeStruct((width, hidden), F32), jax.ShapeDtypeStruct((hidden, width), F32),
         ) + tuple(jax.ShapeDtypeStruct(shape, F32) for shape in shapes),
         in_specs=[
             pl.BlockSpec((1, 2, width, TILE), lambda i: (0, i, 0, 0)),
             pl.BlockSpec((1, 2, width, TILE), lambda i: (1, i, 0, 0)),
-            whole(tok.shape), whole(vec.shape),
+            whole(tok.shape), whole(vec.shape), image, image, whole(out_s.shape), whole(gx_s.shape),
         ],
         out_specs=(
+            image, image, whole(out_s.shape), whole(gx_s.shape),
             pl.BlockSpec((width, step), lambda i: (0, i)), pl.BlockSpec((step, width), lambda i: (i, 0)),
         ) + tuple(whole(shape) for shape in shapes),
         compiler_params=pltpu.CompilerParams(vmem_limit_bytes=TOP),
-    )(full, full, tok, vec)
+    )(full, full, tok, vec, out_l, gx_l, out_s, gx_s)
 
 
 def local(
@@ -1236,12 +1282,13 @@
     width = x_small.shape[2]
     patches_s, patches_l = x_small.shape[1], x_large.shape[1]
     rows = x_small.shape[0] * (patches_s + -patches_s % 64) + x_large.shape[0] * patches_l
+    xs = x_small.transpose(1, 0, 2)
     y, *saved = token_forward(
-        x_large, x_small, tok_w1_large, tok_w1_small, tok_w2_large.T, tok_w2_small.T,
+        x_large, xs, tok_w1_large, tok_w1_small, tok_w2_large.T, tok_w2_small.T,
         tok_b1_large, tok_b1_small, tok_b2_large, tok_b2_small, ln1_gain, ln1_bias, rows + -rows % (3 * LANES),
     )
     out_large, ey, chunk, small_grads, out_small, begun = channel(
-        y, live_counts, cot_large, cot_small, ch_w1, ch_w2, ch_b1, ln2_gain, ln2_bias, ch_b2
+        y, live_counts, cot_large, cot_small.transpose(1, 0, 2), ch_w1, ch_w2, ch_b1, ln2_gain, ln2_bias, ch_b2
     )
     near, far = img_split(lax.axis_size("img"))
     far_inside = width % (near * far * 2 * 16) == 0
@@ -1249,16 +1296,16 @@
         same = [[a * near + b for a in range(far)] for b in range(near)]
         chunk = lax.psum(chunk.astype(F32), "img", axis_index_groups=same).astype(BF)
     full, gx_large, tok, vec, gx_small = backward(
-        chunk, begun, ey, x_large, x_small, saved, small_grads, ln1_gain
+        chunk, begun, ey, x_large, xs, saved, small_grads, ln1_gain
     )
     if not far_inside:
         tok = lax.psum(tok.astype(F32), "img")
     (
-        grad_ch_w1, grad_ch_w2, gain1, bias1, w1_s, b1_s, w2_s, b2_s, w1_l, b1_l, w2_l, b2_l,
+        out_large, gx_large, out_small, gx_small, grad_ch_w1, grad_ch_w2, gain1, bias1, w1_s, b1_s, w2_s, b2_s, w1_l, b1_l, w2_l, b2_l,
         gain2, bias2, grad_b1, grad_b2,
-    ) = widen(full, tok, vec, patches_s, patches_l)
+    ) = widen(full, tok, vec, out_large, gx_large, out_small, gx_small)
     return (
-        out_small, out_large, gx_small, gx_large, gain1, bias1,
+        out_small.transpose(1, 0, 2), out_large, gx_small.transpose(1, 0, 2), gx_large, gain1, bias1,
         w1_s, b1_s, w2_s.T, b2_s, w1_l, b1_l, w2_l.T, b2_l,
         gain2, bias2, grad_ch_w1, grad_b1, grad_ch_w2, grad_b2,
     )

time: 242 us -> 232 us (0.959)
  local copies, waits for them, and re-layouts: 11.1 us -> 0 us
  Pallas kernels: 228 us -> 231 us
    unnamed x10 -> x0, local copies, waits for them, and re-layouts: 11.1 us -> none
    pallas_call x1, Pallas kernels: 11.7 us -> 15.1 us  [widen(): pl.pallas_call(widen_kernel, grid=(hidden // step,), out_shape=tuple((jax...]
    pallas_call x1, Pallas kernels: 79.6 us -> 76.9 us  [channel(): pl.pallas_call(functools.partial(channel_kernel, near, far, far_inside),...]
where the time goes in v6:
time: 232 us
  Pallas kernels  231 us (100%)
    pallas_call x1, Pallas kernels, backward(): pl.pallas_call(functools.partial(backward_kernel, near, far, size, far_in...  84.4 us
    pallas_call x1, Pallas kernels, channel(): pl.pallas_call(functools.partial(channel_kernel, near, far, far_inside),...  76.9 us
    pallas_call x1, Pallas kernels, token_forward(): pl.pallas_call(functools.partial(token_kernel, near, size), out_shape=(ja...  54.5 us
    pallas_call x1, Pallas kernels, widen(): pl.pallas_call(widen_kernel, grid=(hidden // step,), out_shape=tuple((jax...  15.1 us

profile of v6, /device:TPU:0, one launch (start us, length us, event | category | flops | bytes accessed | tf_op | source)
XLA Modules:
  0.0 231.8 jit_solution(6656293658913205338)
XLA Ops:
  0.7 54.5 %shard_map.356 = (f32[1152,768]{1,0:T(8,128)}, bf16[3,576,384]{2,1,0:T(8,128)(2,1)}, bf16[1,256,768]{2,1,0:T(8,128)(2,1)}, bf16[3,384,384]{2,1,0:T(8,128)(2,1)},...) custom-call(bf16[6,144,768]{2,1,0:T(8,128)(2,1)} %xl_in.1, ...), custom_call_target="tpu_custom_call" | custom-call | tf_op jit(solution)/shard_map/pallas_call | solution.py:809
  55.2 76.9 %shard_map.357 = (bf16[6,144,768]{2,1,0:T(8,128)(2,1)}, f32[1152,768]{1,0:T(8,128)}, bf16[12,48,256]{2,1,0:T(8,128)(2,1)}, f32[8,768]{1,0:T(8,128)}, bf16[49,4,7...) custom-call(f32[1152,768]{1,0:T(8,128)} %get-tuple-element.60.y_hbm, s32[1,2]{1,0:T(1,128)} %live.1, ...), custom_call_target="tpu_custom_call" | custom-call | tf_op jit(solution)/shard_map/pallas_call | solution.py:532
  132.0 84.4 %shard_map.358 = (bf16[2,12,2,4,2,48,256]{6,5,4,3,2,1,0:T(8,128)(2,1)}, f32[6,144,768]{2,1,0:T(8,128)}, bf16[512,384]{1,0:T(8,128)(2,1)}, f32[24,768]{1,0:T(8,128)}, f32[49,4,768]{2,1,0:T(4,128)}) custom-call(bf16[12,48,256]{2,1,0:T(8,128)(2,1)} %get-tuple-element.61.chunk_hbm, ...), custom_call_target="tpu_custom_call", output_to_operand_aliasing={{0}: (1, {})} | custom-call | tf_op jit(solution)/shard_map/pallas_call | solution.py:1165
  216.5 15.1 %shard_map.359 = (bf16[6,144,768]{2,1,0:T(8,128)(2,1)}, f32[6,144,768]{2,1,0:T(8,128)}, bf16[49,4,768]{2,1,0:T(4,128)(2,1)}, f32[49,4,768]{2,1,0:T(4,128)}, f32[...) custom-call(bf16[2,12,768,256]{3,2,1,0:T(8,128)(2,1)} %bitcast.9, ...), custom_call_target="tpu_custom_call" | custom-call | tf_op jit(solution)/shard_map/pallas_call | solution.py:1257

commit v7 on v6

--- a/solution.py
+++ b/solution.py
@@ -622,7 +622,7 @@
             there = lax.rem(peers.mine(axis) + j, count)
             pl.semaphore_signal(barrier, inc=1, device_id=peers.at(axis, there), device_id_type=MESH)
             total += 1
-    pl.semaphore_wait(barrier, total)
+    return total
 
 
 def unit_rows(row):
@@ -633,12 +633,19 @@
     return centered * scale, scale
 
 
+def weights_shared(near, far, patches_l, patches_s):
+    if near != 2 or far < 2 or patches_l % (16 * (far - 1)):
+        return False
+    return patches_l // (far - 1) <= patches_s
+
+
 def token_kernel(
-    near, size,
+    near, far, size,
     xl, xs_in, w1_l, w1_s, w2_l, w2_s, b1_l_ref, b1_s_ref, b2_l_ref, b2_s_ref, gain_ref, bias_ref,
     y_hbm, u_l, u_s, h_l, h_s, sl_l, sl_s, w_l, w_s,
-    xs, wq_l, wq_s, tx_l, tx_s, w1t_l, w1t_s, m_l, m_s, rx_l, rx_s, y,
+    xs, wq, mine_w, theirs_w, tx_l, tx_s, w1t_l, w1t_s, m_l, m_s, rx_l, rx_s, y,
     y_sem, own_sem, wown, w_ss, w_rs, out_ss_l, out_ss_s, out_rs_l, out_rs_s, bk_ss_l, bk_ss_s, bk_rs_l, bk_rs_s,
+    sx_sem, sf_ss, sf_rs, sn_ss, sn_rs, sc_sem,
 ):
     peers = Peers(near)
     me = peers.blk
@@ -649,15 +656,16 @@
     half = width // 2
     per_l, per_s = count_l * 2 // size, count_s // size
     swap = Swap(peers, size, per_l, per_s, patches_l, patches_s)
-    wq_l[0] = w1_l[...]
-    wq_l[1] = w2_l[...]
-    wq_s[...] = jnp.zeros_like(wq_s)
-    wq_s[0, :real_s] = w1_s[...]
-    wq_s[1, :real_s] = w2_s[...]
-
-    barrier = pltpu.get_barrier_semaphore()
-    for j in range(1, size):
-        pl.semaphore_signal(barrier, inc=1, device_id=(peers.img, swap.other(j)), device_id_type=MESH)
+    shared = weights_shared(near, far, patches_l, patches_s)
+    total = patches_l + patches_s
+    for k, (large, small) in enumerate(((w1_l, w1_s), (w2_l, w2_s))):
+        wq[k, :patches_l] = large[...]
+        wq[k, patches_l:] = jnp.zeros((patches_s, token), BF)
+        wq[k, patches_l:patches_l + real_s] = small[...]
+    wq_l = wq.at[:, pl.ds(0, patches_l)]
+    wq_s = wq.at[:, pl.ds(patches_l, patches_s)]
+
+    greetings = greet_all(peers, size, near if shared else 1, far if shared else 1)
 
     def weights(src_l, src_s, quarter, n, place):
         return (
@@ -667,9 +675,30 @@
 
     x_peer = (1 - peers.x) * 2 + peers.core
     core_peer = peers.x * 2 + 1 - peers.core
-    to_x = weights(wq_l, wq_s, me, 0, x_peer)
+    diagonal = (1 - peers.x) * 2 + 1 - peers.core
+    if shared:
+        stride = patches_l // (far - 1)
+
+        def share(src, dst, ss, rs, device):
+            return pltpu.make_async_remote_copy(
+                src_ref=src, dst_ref=dst, send_sem=ss, recv_sem=rs, device_id=device, device_id_type=MESH
+            )
+
+        n, f = peers.near, peers.far
+        first = pl.ds(pl.multiple_of(f * stride, 16), patches_s)
+        over_x = share(wq.at[n, first], mine_w.at[n, f], sx_sem.at[0], sx_sem.at[1], (peers.img, x_peer))
+        over_far = [
+            share(
+                mine_w.at[n, f], mine_w.at[n, f], sf_ss.at[j - 1], sf_rs.at[j - 1],
+                peers.at("far", lax.rem(f + j, far)),
+            )
+            for j in range(1, far)
+        ]
+        over_near = share(mine_w.at[n], mine_w.at[n], sn_ss.at[0], sn_rs.at[0], peers.at("near", 1 - n))
+        over_core = share(mine_w, theirs_w, sc_sem.at[0], sc_sem.at[1], (peers.img, core_peer))
+    to_x = (over_x,) if shared else weights(wq_l, wq_s, me, 0, x_peer)
     to_core = weights(wq_l, wq_s, me, 1, core_peer)
-    relay = weights(
+    relay = () if shared else weights(
         w_l.at[:, swap.rows(x_peer, patches_l)], w_s.at[:, swap.rows(x_peer, patches_s)], x_peer, 2, core_peer
     )
     own_w = (
@@ -697,7 +726,7 @@
         return carry
 
     lax.fori_loop(0, count_l, norm_l, 0)
-    greeted(size - 1)
+    greeted(greetings)
     for copy in to_x + to_core:
         copy.start()
     for j in range(per_l):
@@ -721,6 +750,21 @@
         copy.start()
     for copy in own_w:
         copy.wait()
+    if shared:
+        for copy in over_far:
+            copy.start()
+        for copy in over_far:
+            copy.wait_recv()
+        over_near.start()
+        over_near.wait_recv()
+        over_core.start()
+        over_core.wait_recv()
+        for k in range(2):
+            for pieces, quarter in ((mine_w, x_peer), (theirs_w, diagonal)):
+                for p in range(far - 1):
+                    at = pl.ds(pl.multiple_of(quarter * patches_l + p * stride, 16), stride)
+                    w_l[k, at] = pieces[k, p, :stride]
+                w_s[k, swap.rows(quarter, patches_s)] = pieces[k, far - 1]
     for copy in to_core + relay:
         copy.wait_recv()
     b1_l, b1_s = column(b1_l_ref, token), column(b1_s_ref, token)
@@ -782,6 +826,9 @@
     y_out.start()
     for copy in to_x + to_core + relay:
         copy.wait_send()
+    if shared:
+        for copy in over_far + [over_near, over_core]:
+            copy.wait_send()
     for k in range(1, size):
         there = swap.other(k)
         for j in range(per_l):
@@ -807,7 +854,7 @@
     DMA = pltpu.SemaphoreType.DMA
     low = lambda *shape: jax.ShapeDtypeStruct(shape, BF)
     return pl.pallas_call(
-        functools.partial(token_kernel, near, size),
+        functools.partial(token_kernel, near, far, size),
         out_shape=(
             jax.ShapeDtypeStruct((rows, width), F32),
             low(per_l, size * patches_l, half), low(per_s, size * patches_s, width),
@@ -818,7 +865,8 @@
         in_specs=[vmem] * 12,
         out_specs=(ANY,) + (vmem,) * 8,
         scratch_shapes=[
-            V((count_s, real_s, width), BF), V((2, patches_l, token), BF), V((2, patches_s, token), BF),
+            V((count_s, real_s, width), BF), V((2, patches_l + patches_s, token), BF),
+            V((2, far, patches_s, token), BF), V((2, far, patches_s, token), BF),
             V((count_l * 2, patches_l, half), BF), V((count_s, patches_s, width), BF),
             V((token, size * patches_l), BF), V((token, size * patches_s), BF),
             V((per_l, size * patches_l, half), BF), V((per_s, size * patches_s, width), BF),
@@ -827,6 +875,7 @@
             DMA((1,)), DMA((1,)), DMA((2,)), DMA((3, 2)), DMA((3, 2)),
             DMA((count_l * 2,)), DMA((count_s,)), DMA((per_l, size)), DMA((per_s, size)),
             DMA((per_l, size)), DMA((per_s, size)), DMA((count_l * 2,)), DMA((count_s,)),
+            DMA((2,)), DMA((far - 1,)), DMA((far - 1,)), DMA((1,)), DMA((1,)), DMA((2,)),
         ],
         compiler_params=pltpu.CompilerParams(
             collective_id=2, has_side_effects=True, vmem_limit_bytes=TOP
@@ -903,7 +952,7 @@
     ]
     for copy in inputs:
         copy.start()
-    greet_all(peers, size, near, far)
+    greeted(greet_all(peers, size, near, far))
     if not far_inside:
         for k in range(groups):
             gather.first(k)

time: 232 us -> 227 us (0.978)
  Pallas kernels: 231 us -> 226 us
    pallas_call x1, Pallas kernels: 54.5 us -> 50.7 us  [token_forward(): pl.pallas_call(functools.partial(token_kernel, near, far, size), out_shap...]
where the time goes in v7:
time: 227 us
  Pallas kernels  226 us (100%)
    pallas_call x1, Pallas kernels, backward(): pl.pallas_call(functools.partial(backward_kernel, near, far, size, far_in...  85 us
    pallas_call x1, Pallas kernels, channel(): pl.pallas_call(functools.partial(channel_kernel, near, far, far_inside),...  74.8 us
    pallas_call x1, Pallas kernels, token_forward(): pl.pallas_call(functools.partial(token_kernel, near, far, size), out_shap...  50.7 us
    pallas_call x1, Pallas kernels, widen(): pl.pallas_call(widen_kernel, grid=(hidden // step,), out_shape=tuple((jax...  15.1 us

profile of v7, /device:TPU:0, one launch (start us, length us, event | category | flops | bytes accessed | tf_op | source)
XLA Modules:
  0.0 226.5 jit_solution(16992463350496082297)
XLA Ops:
  0.7 50.7 %shard_map.356 = (f32[1152,768]{1,0:T(8,128)}, bf16[3,576,384]{2,1,0:T(8,128)(2,1)}, bf16[1,256,768]{2,1,0:T(8,128)(2,1)}, bf16[3,384,384]{2,1,0:T(8,128)(2,1)},...) custom-call(bf16[6,144,768]{2,1,0:T(8,128)(2,1)} %xl_in.1, ...), custom_call_target="tpu_custom_call" | custom-call | tf_op jit(solution)/shard_map/pallas_call | solution.py:856
  51.4 74.8 %shard_map.357 = (bf16[6,144,768]{2,1,0:T(8,128)(2,1)}, f32[1152,768]{1,0:T(8,128)}, bf16[12,48,256]{2,1,0:T(8,128)(2,1)}, f32[8,768]{1,0:T(8,128)}, bf16[49,4,7...) custom-call(f32[1152,768]{1,0:T(8,128)} %get-tuple-element.60.y_hbm, s32[1,2]{1,0:T(1,128)} %live.1, ...), custom_call_target="tpu_custom_call" | custom-call | tf_op jit(solution)/shard_map/pallas_call | solution.py:532
  126.2 85.0 %shard_map.358 = (bf16[2,12,2,4,2,48,256]{6,5,4,3,2,1,0:T(8,128)(2,1)}, f32[6,144,768]{2,1,0:T(8,128)}, bf16[512,384]{1,0:T(8,128)(2,1)}, f32[24,768]{1,0:T(8,128)}, f32[49,4,768]{2,1,0:T(4,128)}) custom-call(bf16[12,48,256]{2,1,0:T(8,128)(2,1)} %get-tuple-element.61.chunk_hbm, ...), custom_call_target="tpu_custom_call", output_to_operand_aliasing={{0}: (1, {})} | custom-call | tf_op jit(solution)/shard_map/pallas_call | solution.py:1214
  211.2 15.1 %shard_map.359 = (bf16[6,144,768]{2,1,0:T(8,128)(2,1)}, f32[6,144,768]{2,1,0:T(8,128)}, bf16[49,4,768]{2,1,0:T(4,128)(2,1)}, f32[49,4,768]{2,1,0:T(4,128)}, f32[...) custom-call(bf16[2,12,768,256]{3,2,1,0:T(8,128)(2,1)} %bitcast.9, ...), custom_call_target="tpu_custom_call" | custom-call | tf_op jit(solution)/shard_map/pallas_call | solution.py:1306

commit v8 on v7

--- a/solution.py
+++ b/solution.py
@@ -17,7 +17,7 @@
 ANY = pl.BlockSpec(memory_space=pl.ANY)
 TILE = 256
 LAGS = (1, 3, 5, 7)
-LATE = 3
+LATE = 4
 TOP = 62 * 1024 * 1024
 
 
@@ -797,6 +797,10 @@
     y[0:small_rows, :] = jnp.zeros((small_rows, width), F32)
     if rows > used:
         y[used:rows, :] = jnp.zeros((rows - used, width), F32)
+        spare = pltpu.make_async_copy(
+            y.at[pl.ds(used, rows - used)], y_hbm.at[pl.ds(used, rows - used)], y_sem.at[count_l + count_s]
+        )
+        spare.start()
 
     def arrived(kind, unit, m, rx, bss, brs):
         per = per_l if kind == "l" else per_s
@@ -805,6 +809,16 @@
         @pl.when(owner != me)
         def _():
             swap.back(kind, unit - owner * per, owner, me, m, rx, bss, brs).wait_recv()
+
+    def y_copy(start, size, n):
+        at = pl.ds(pl.multiple_of(start, 16), size)
+        return pltpu.make_async_copy(y.at[at], y_hbm.at[at], y_sem.at[n])
+
+    def y_l(n):
+        return y_copy(small_rows + n * patches_l, patches_l, n)
+
+    def y_s(n):
+        return y_copy(n * patches_s, patches_s, count_l + n)
 
     def home_l(n, carry):
         arrived("l", 2 * n, m_l, rx_l, bk_ss_l, bk_rs_l)
@@ -812,18 +826,18 @@
         at = pl.ds(pl.multiple_of(small_rows + n * patches_l, 16), patches_l)
         y[at, :half] = xl[n, :, :half].astype(F32) + rx_l[2 * n].astype(F32) + b2_l
         y[at, half:] = xl[n, :, half:].astype(F32) + rx_l[2 * n + 1].astype(F32) + b2_l
+        y_l(n).start()
         return carry
 
     def home_s(n, carry):
         arrived("s", n, m_s, rx_s, bk_ss_s, bk_rs_s)
         at = pl.ds(pl.multiple_of(n * patches_s, 16), real_s)
         y[at, :] = xs[n].astype(F32) + rx_s[n, :real_s].astype(F32) + b2_s
+        y_s(n).start()
         return carry
 
     lax.fori_loop(0, count_l, home_l, 0)
     lax.fori_loop(0, count_s, home_s, 0)
-    y_out = pltpu.make_async_copy(y, y_hbm, y_sem.at[0])
-    y_out.start()
     for copy in to_x + to_core + relay:
         copy.wait_send()
     if shared:
@@ -837,7 +851,12 @@
         for j in range(per_s):
             swap.out("s", j, there, me, tx_s, u_s, out_ss_s, out_rs_s).wait_send()
             swap.back("s", j, me, there, m_s, rx_s, bk_ss_s, bk_rs_s).wait_send()
-    y_out.wait()
+    for n in range(count_l):
+        y_l(n).wait()
+    for n in range(count_s):
+        y_s(n).wait()
+    if rows > used:
+        spare.wait()
 
 
 def token_forward(xl, xs, w1_l, w1_s, w2_l, w2_s, b1_l, b1_s, b2_l, b2_s, gain, bias, rows):
@@ -872,7 +891,7 @@
             V((per_l, size * patches_l, half), BF), V((per_s, size * patches_s, width), BF),
             V((count_l * 2, patches_l, half), BF), V((count_s, patches_s, width), BF),
             V((rows, width), F32),
-            DMA((1,)), DMA((1,)), DMA((2,)), DMA((3, 2)), DMA((3, 2)),
+            DMA((count_l + count_s + 1,)), DMA((1,)), DMA((2,)), DMA((3, 2)), DMA((3, 2)),
             DMA((count_l * 2,)), DMA((count_s,)), DMA((per_l, size)), DMA((per_s, size)),
             DMA((per_l, size)), DMA((per_s, size)), DMA((count_l * 2,)), DMA((count_s,)),
             DMA((2,)), DMA((far - 1,)), DMA((far - 1,)), DMA((1,)), DMA((1,)), DMA((2,)),
@@ -883,7 +902,7 @@
     )(xl, xs, w1_l, w1_s, w2_l, w2_s, b1_l, b1_s, b2_l, b2_s, gain, bias)
 
 
-DEPTH = 3
+DEPTH = 2
 SLAB = 512
 
 

time: 227 us -> 223 us (0.982)
  Pallas kernels: 226 us -> 222 us
    pallas_call x1, Pallas kernels: 85 us -> 82.3 us  [backward(): pl.pallas_call(functools.partial(backward_kernel, near, far, size, far_in...]
where the time goes in v8:
time: 223 us
  Pallas kernels  222 us (100%)
    pallas_call x1, Pallas kernels, backward(): pl.pallas_call(functools.partial(backward_kernel, near, far, size, far_in...  82.3 us
    pallas_call x1, Pallas kernels, channel(): pl.pallas_call(functools.partial(channel_kernel, near, far, far_inside),...  74.8 us
    pallas_call x1, Pallas kernels, token_forward(): pl.pallas_call(functools.partial(token_kernel, near, far, size), out_shap...  49.7 us
    pallas_call x1, Pallas kernels, widen(): pl.pallas_call(widen_kernel, grid=(hidden // step,), out_shape=tuple((jax...  15.1 us

profile of v8, /device:TPU:0, one launch (start us, length us, event | category | flops | bytes accessed | tf_op | source)
XLA Modules:
  0.0 222.7 jit_solution(4384022557007132388)
XLA Ops:
  0.7 49.7 %shard_map.356 = (f32[1152,768]{1,0:T(8,128)}, bf16[3,576,384]{2,1,0:T(8,128)(2,1)}, bf16[1,256,768]{2,1,0:T(8,128)(2,1)}, bf16[3,384,384]{2,1,0:T(8,128)(2,1)},...) custom-call(bf16[6,144,768]{2,1,0:T(8,128)(2,1)} %xl_in.1, ...), custom_call_target="tpu_custom_call" | custom-call | tf_op jit(solution)/shard_map/pallas_call | solution.py:875
  50.3 74.8 %shard_map.357 = (bf16[6,144,768]{2,1,0:T(8,128)(2,1)}, f32[1152,768]{1,0:T(8,128)}, bf16[12,48,256]{2,1,0:T(8,128)(2,1)}, f32[8,768]{1,0:T(8,128)}, bf16[49,4,7...) custom-call(f32[1152,768]{1,0:T(8,128)} %get-tuple-element.60.y_hbm, s32[1,2]{1,0:T(1,128)} %live.1, ...), custom_call_target="tpu_custom_call" | custom-call | tf_op jit(solution)/shard_map/pallas_call | solution.py:532
  125.1 82.3 %shard_map.358 = (bf16[2,12,2,4,2,48,256]{6,5,4,3,2,1,0:T(8,128)(2,1)}, f32[6,144,768]{2,1,0:T(8,128)}, bf16[512,384]{1,0:T(8,128)(2,1)}, f32[24,768]{1,0:T(8,128)}, f32[49,4,768]{2,1,0:T(4,128)}) custom-call(bf16[12,48,256]{2,1,0:T(8,128)(2,1)} %get-tuple-element.61.chunk_hbm, ...), custom_call_target="tpu_custom_call", output_to_operand_aliasing={{0}: (1, {})} | custom-call | tf_op jit(solution)/shard_map/pallas_call | solution.py:1233
  207.4 15.1 %shard_map.359 = (bf16[6,144,768]{2,1,0:T(8,128)(2,1)}, f32[6,144,768]{2,1,0:T(8,128)}, bf16[49,4,768]{2,1,0:T(4,128)(2,1)}, f32[49,4,768]{2,1,0:T(4,128)}, f32[...) custom-call(bf16[2,12,768,256]{3,2,1,0:T(8,128)(2,1)} %bitcast.9, ...), custom_call_target="tpu_custom_call" | custom-call | tf_op jit(solution)/shard_map/pallas_call | solution.py:1325
